TPU v7x, 32 devices: a whole 2x2x4 slice. The times are simulated.
32 devices in a mesh: dp: 2 (over y), seq: 4 (over z), tensor: 4 (over x, core).
Axes of the slice: x: 2, y: 2, z: 4, core: 2. Of those that a mesh axis runs over, the one named last changes fastest.
Arguments:
- stream: float32 [4096, 2048], P(('dp', 'seq')), may hold values from -6 to 6
- cotangent: float32 [4096, 2048], P(('dp', 'seq')), may hold values from -6 to 6
- w_input: float32 [2048, 16, 768], P(('dp', 'seq'), 'tensor'), may hold values from -0.125 to 0.125
- w_rates: float32 [2048, 16, 2], P(('dp', 'seq'), 'tensor'), may hold values from -0.125 to 0.125
- w_conv: float32 [4, 16, 512], replicated, may hold values from -3 to 3
- w_output: float32 [16, 256, 2048], P('tensor', None, ('dp', 'seq')), may hold values from -0.1875 to 0.1875
- w_swiglu: float32 [2048, 2, 5632], P(('dp', 'seq'), None, 'tensor'), may hold values from -0.125 to 0.125
- w_down: float32 [5632, 2048], P('tensor', ('dp', 'seq')), may hold values from -0.078125 to 0.078125
- w_gains: float32 [2, 2048], replicated, may hold values from 0.5 to 1.5
- w_scale: float32 [256], replicated, may hold values from 0.5 to 1.5
- w_heads: float32 [2, 16], replicated, may hold values from -6 to 2.7, as said below
- m_input: float32 [2, 2048, 16, 768], P(None, ('dp', 'seq'), 'tensor'), may hold values from -2 to 2, as said below
- m_rates: float32 [2, 2048, 16, 2], P(None, ('dp', 'seq'), 'tensor'), may hold values from -2 to 2, as said below
- m_conv: float32 [2, 4, 16, 512], replicated, may hold values from -2 to 2, as said below
- m_output: float32 [2, 16, 256, 2048], P(None, 'tensor', None, ('dp', 'seq')), may hold values from -2 to 2, as said below
- m_swiglu: float32 [2, 2048, 2, 5632], P(None, ('dp', 'seq'), None, 'tensor'), may hold values from -2 to 2, as said below
- m_down: float32 [2, 5632, 2048], P(None, 'tensor', ('dp', 'seq')), may hold values from -2 to 2, as said below
- m_gains: float32 [2, 2, 2048], replicated, may hold values from -2 to 2, as said below
- m_scale: float32 [2, 256], replicated, may hold values from -2 to 2, as said below
- m_heads: float32 [2, 2, 16], replicated, may hold values from -2 to 2, as said below
Outputs:
- result: float32 [4096, 2048], P(('dp', 'seq'))
- grad_stream: float32 [4096, 2048], P(('dp', 'seq'))
- g_input: float32 [2048, 16, 768], P(('dp', 'seq'), 'tensor')
- g_rates: float32 [2048, 16, 2], P(('dp', 'seq'), 'tensor')
- g_conv: float32 [4, 16, 512], replicated
- g_output: float32 [16, 256, 2048], P('tensor', None, ('dp', 'seq'))
- g_swiglu: float32 [2048, 2, 5632], P(('dp', 'seq'), None, 'tensor')
- g_down: float32 [5632, 2048], P('tensor', ('dp', 'seq'))
- g_gains: float32 [2, 2048], replicated
- g_scale: float32 [256], replicated
- g_heads: float32 [2, 16], replicated
- new_input: float32 [2048, 16, 768], P(('dp', 'seq'), 'tensor')
- new_rates: float32 [2048, 16, 2], P(('dp', 'seq'), 'tensor')
- new_conv: float32 [4, 16, 512], replicated
- new_output: float32 [16, 256, 2048], P('tensor', None, ('dp', 'seq'))
- new_swiglu: float32 [2048, 2, 5632], P(('dp', 'seq'), None, 'tensor')
- new_down: float32 [5632, 2048], P('tensor', ('dp', 'seq'))
- new_gains: float32 [2, 2048], replicated
- new_scale: float32 [256], replicated
- new_heads: float32 [2, 16], replicated
- moment_input: float32 [2, 2048, 16, 768], P(None, ('dp', 'seq'), 'tensor')
- moment_rates: float32 [2, 2048, 16, 2], P(None, ('dp', 'seq'), 'tensor')
- moment_conv: float32 [2, 4, 16, 512], replicated
- moment_output: float32 [2, 16, 256, 2048], P(None, 'tensor', None, ('dp', 'seq'))
- moment_swiglu: float32 [2, 2048, 2, 5632], P(None, ('dp', 'seq'), None, 'tensor')
- moment_down: float32 [2, 5632, 2048], P(None, 'tensor', ('dp', 'seq'))
- moment_gains: float32 [2, 2, 2048], replicated
- moment_scale: float32 [2, 256], replicated
- moment_heads: float32 [2, 2, 16], replicated
Inputs may be any that keep to these rules, and one draw needn't show every extreme that they name: `w_heads`: row 0 holds logarithms of decay rates, row 1 decay biases. `m_input`: slice 0 holds first moments, slice 1 second moments, which are positive. `m_rates`: slice 0 holds first moments, slice 1 second moments, which are positive. `m_conv`: slice 0 holds first moments, slice 1 second moments, which are positive. `m_output`: slice 0 holds first moments, slice 1 second moments, which are positive. `m_swiglu`: slice 0 holds first moments, slice 1 second moments, which are positive. `m_down`: slice 0 holds first moments, slice 1 second moments, which are positive. `m_gains`: slice 0 holds first moments, slice 1 second moments, which are positive. `m_scale`: slice 0 holds first moments, slice 1 second moments, which are positive. `m_heads`: slice 0 holds first moments, slice 1 second moments, which are positive.
All inputs are finite; a program needn't handle non-finite values.
Results may differ from a plain program's by a relative error of at most 0.012.
The roundings to bfloat16 on the way count: a program that leaves them out, or rounds other values in their place, can miss the bound.
Values may be sent and summed in bfloat16 or wider, within the bound.
No kernel may reach another device: no remote copies, remote signals or barrier semaphores. Data moves between devices by JAX's collectives and lax.ppermute only.
A program may use at most 320 MiB of HBM per device.

v0:
```python
import jax
import jax.numpy as jnp
from jax import lax
from jax.sharding import PartitionSpec as P

DK = 128
DV = 256
KCONV = 4
BLOCK = 64
ADAM_STEP = 5


HIGHEST = lax.Precision.HIGHEST


def passed_along(block, axis, distance):
    devices = range(lax.axis_size(axis))
    route = [(i - distance, i) for i in devices if i - distance in devices]
    return lax.ppermute(block, axis, route)


def rms_norm(rows, gain):
    return rows * lax.rsqrt(jnp.mean(rows * rows, axis=-1, keepdims=True) + 1e-06) * gain


def finish(mixer_out, gate_raw, scale_gain):
    factor = lax.rsqrt(jnp.mean(mixer_out * mixer_out, axis=-1, keepdims=True) + 1e-05)
    return mixer_out * factor * scale_gain * jax.nn.silu(gate_raw)


def prepare(mixed_rows, before, conv_weight, decay_raw, update_raw, head_rates):
    length = mixed_rows.shape[1]
    padded = jnp.concatenate([before, mixed_rows], axis=1)
    filtered = conv_weight[0] * padded[:, 0:length]
    for tap_index in range(1, conv_weight.shape[0]):
        filtered = filtered + conv_weight[tap_index] * padded[:, tap_index : tap_index + length]
    filtered = jax.nn.silu(filtered)
    query_raw = filtered[..., :DK]
    key_raw = filtered[..., DK : 2 * DK]
    query = (
        query_raw
        * lax.rsqrt(jnp.sum(query_raw * query_raw, axis=-1, keepdims=True) + 1e-06)
        * DK ** (-0.5)
    )
    key_rows = key_raw * lax.rsqrt(jnp.sum(key_raw * key_raw, axis=-1, keepdims=True) + 1e-06)
    value_rows = filtered[..., 2 * DK :]
    update_gate = jax.nn.sigmoid(update_raw)
    log_decay = -jnp.exp(head_rates[0]) * jax.nn.softplus(decay_raw + head_rates[1])
    return (query, key_rows, value_rows, update_gate, log_decay)


def block_parts(query, key_rows, value_rows, update_gate, log_decay):
    length = query.shape[1]
    cumulative = jnp.cumsum(log_decay, axis=1)
    row_index = lax.broadcasted_iota(jnp.int32, (length, length), 0)
    column_index = lax.broadcasted_iota(jnp.int32, (length, length), 1)
    within = (row_index >= column_index)[None, :, :, None]
    strict = (row_index > column_index)[None, :, :, None]
    distance = cumulative[:, :, None, :] - cumulative[:, None, :, :]
    fade_within = jnp.where(within, jnp.exp(jnp.where(within, distance, 0.0)), 0.0)
    fade_strict = jnp.where(strict, fade_within, 0.0)
    key_products = jnp.einsum("bihk,bjhk->bijh", key_rows, key_rows, precision=HIGHEST)
    lower_part = update_gate[:, :, None, :] * key_products * fade_strict
    identity = jnp.eye(length, dtype=jnp.float32)
    system = identity + jnp.transpose(lower_part, (0, 3, 1, 2))
    growth = jnp.exp(cumulative)
    right_keys = jnp.transpose((update_gate * growth)[..., None] * key_rows, (0, 2, 1, 3))
    right_values = jnp.transpose(update_gate[..., None] * value_rows, (0, 2, 1, 3))
    solved_keys = jax.scipy.linalg.solve_triangular(
        system, right_keys, lower=True, unit_diagonal=True
    )
    solved_values = jax.scipy.linalg.solve_triangular(
        system, right_values, lower=True, unit_diagonal=True
    )
    head_query = jnp.transpose(query, (0, 2, 1, 3))
    scores = jnp.einsum("bhik,bjhk->bhij", head_query, key_rows, precision=HIGHEST) * jnp.transpose(
        fade_within, (0, 3, 1, 2)
    )
    carried_scale = jnp.transpose(growth, (0, 2, 1))[..., None]
    trailing = jnp.exp(cumulative[:, -1:, :] - cumulative)
    faded_keys = jnp.transpose(trailing[..., None] * key_rows, (0, 2, 1, 3))
    final_decay = jnp.exp(cumulative[:, -1, :])[:, :, None, None]
    return (solved_keys, solved_values, head_query, scores, carried_scale, faded_keys, final_decay)


def state_step(states, parts):
    solved_keys, solved_values, head_query, scores, carried_scale, faded_keys, final_decay = parts
    fresh_values = solved_values - jnp.einsum(
        "bhck,bhkw->bhcw", solved_keys, states, precision=HIGHEST
    )
    carried = carried_scale * jnp.einsum("bhck,bhkw->bhcw", head_query, states, precision=HIGHEST)
    output = carried + jnp.einsum("bhij,bhjw->bhiw", scores, fresh_values, precision=HIGHEST)
    next_states = final_decay * states + jnp.einsum(
        "bhck,bhcw->bhkw", faded_keys, fresh_values, precision=HIGHEST
    )
    return (next_states, jnp.transpose(output, (0, 2, 1, 3)))


def split_blocks(array):
    batches = array.shape[0]
    block_count = array.shape[1] // BLOCK
    return jnp.moveaxis(array.reshape((batches, block_count, BLOCK) + array.shape[2:]), 1, 0)


def all_parts(query, key_rows, value_rows, update_gate, log_decay):
    blocked = [
        split_blocks(array) for array in (query, key_rows, value_rows, update_gate, log_decay)
    ]
    block_count = blocked[0].shape[0]
    merged = [array.reshape((-1,) + array.shape[2:]) for array in blocked]
    parts = block_parts(merged[0], merged[1], merged[2], merged[3], merged[4])
    return tuple((array.reshape((block_count, -1) + array.shape[1:]) for array in parts))


def run_blocks(states, query, key_rows, value_rows, update_gate, log_decay):
    batches = query.shape[0]
    length = query.shape[1]
    parts = all_parts(query, key_rows, value_rows, update_gate, log_decay)
    final_states, outputs = lax.scan(jax.checkpoint(state_step), states, parts)
    outputs = jnp.moveaxis(outputs, 0, 1)
    return (outputs.reshape((batches, length) + outputs.shape[3:]), final_states)


def state_back(carried_grad, inputs):
    parts, output_grad = inputs

    def only_states(states):
        return state_step(states, parts)

    unused, pull = jax.vjp(only_states, jnp.zeros_like(carried_grad))
    return (pull((carried_grad, output_grad))[0], None)


def states_gradient(zero_states, grad_out, query, key_rows, value_rows, update_gate, log_decay):
    parts = all_parts(query, key_rows, value_rows, update_gate, log_decay)
    result_grad, unused = lax.scan(
        state_back, zero_states, (parts, split_blocks(grad_out)), reverse=True
    )
    return result_grad


def apply_map(matrix, states):
    return jnp.einsum("bhkj,bhjw->bhkw", matrix, states, precision=HIGHEST)


def contract_rows(left, right):
    return lax.dot_general(
        left, right, (((0,), (0,)), ((), ())), preferred_element_type=jnp.float32
    )


def contract_cols(left, right):
    return lax.dot_general(
        left, right, (((1,), (1,)), ((), ())), preferred_element_type=jnp.float32
    )


def adam_update(weight, gradient, moments, token_count):
    mean_grad = gradient / token_count
    first = 0.5 * moments[0] + 0.5 * mean_grad
    second = 0.5 * moments[1] + 0.5 * mean_grad * mean_grad
    correction = 1.0 - 0.5**ADAM_STEP
    change = first / correction / (jnp.sqrt(second / correction) + 1e-08) + 0.1 * weight
    return (weight - 0.1 * change, jnp.stack([first, second]))


def body(
    stream,
    cotangent,
    w_input,
    w_rates,
    w_conv,
    w_output,
    w_swiglu,
    w_down,
    w_gains,
    w_scale,
    w_heads,
    m_input,
    m_rates,
    m_conv,
    m_output,
    m_swiglu,
    m_down,
    m_gains,
    m_scale,
    m_heads,
):
    rounded_weights = (
        w_input.astype(jnp.bfloat16),
        w_rates.astype(jnp.bfloat16),
        w_output.astype(jnp.bfloat16),
        w_swiglu.astype(jnp.bfloat16),
        w_down.astype(jnp.bfloat16),
    )
    full_input, full_rates, full_output, full_swiglu, full_down = (
        lax.all_gather(rounded_weights[0], ("dp", "seq"), axis=0, tiled=True),
        lax.all_gather(rounded_weights[1], ("dp", "seq"), axis=0, tiled=True),
        lax.all_gather(rounded_weights[2], ("dp", "seq"), axis=2, tiled=True),
        lax.all_gather(rounded_weights[3], ("dp", "seq"), axis=0, tiled=True),
        lax.all_gather(rounded_weights[4], ("dp", "seq"), axis=1, tiled=True),
    )
    tokens_dev = stream.shape[0]
    width = stream.shape[1]
    heads_local = full_input.shape[1]
    input_cols = full_input.shape[2]
    units_local = full_swiglu.shape[2]
    conv_cols = 2 * DK + DV
    first_head = lax.axis_index("tensor") * heads_local
    conv_local = lax.dynamic_slice_in_dim(w_conv, first_head, heads_local, 1)
    rates_local = lax.dynamic_slice_in_dim(w_heads, first_head, heads_local, 1)
    normed_in, norm_in_pull = jax.vjp(rms_norm, stream, w_gains[0])
    normed_in_low = normed_in.astype(jnp.bfloat16)
    projected = jnp.dot(
        normed_in_low, full_input.reshape(width, -1), preferred_element_type=jnp.float32
    ).reshape(tokens_dev, heads_local, input_cols)
    rates = jnp.dot(
        normed_in_low, full_rates.reshape(width, -1), preferred_element_type=jnp.float32
    ).reshape(tokens_dev, heads_local, 2)
    conv_input = projected[:, :, :conv_cols]
    before = passed_along(conv_input[tokens_dev - (KCONV - 1) :], "seq", 1)
    prepared, prepare_pull = jax.vjp(
        prepare,
        conv_input[None],
        before[None],
        conv_local,
        rates[None, :, :, 0],
        rates[None, :, :, 1],
        rates_local,
    )
    query, key_rows, value_rows, update_gate, log_decay = prepared
    zero_states = jnp.zeros((1, heads_local, DK, DV), jnp.float32)
    identity_maps = jnp.broadcast_to(jnp.eye(DK, dtype=jnp.float32), (1, heads_local, DK, DK))
    widened = jnp.concatenate(
        [value_rows, jnp.zeros(value_rows.shape[:-1] + (DK,), jnp.float32)], axis=-1
    )
    widened_start = jnp.concatenate([zero_states, identity_maps], axis=-1)
    ignored, transfer_state = run_blocks(
        widened_start, query, key_rows, widened, update_gate, log_decay
    )
    offset_map = transfer_state[..., :DV]
    linear_map = transfer_state[..., DV:]
    incoming = zero_states
    for hop_index in range(lax.axis_size("seq") - 1):
        incoming = passed_along(apply_map(linear_map, incoming) + offset_map, "seq", 1)
    delta_result, delta_pull = jax.vjp(
        run_blocks, incoming, query, key_rows, value_rows, update_gate, log_decay
    )
    mixer_out = delta_result[0]
    mixed, finish_pull = jax.vjp(finish, mixer_out, projected[None, :, :, conv_cols:], w_scale)
    mixed_low = mixed.astype(jnp.bfloat16).reshape(tokens_dev, heads_local * DV)
    attention = lax.psum(
        jnp.dot(
            mixed_low,
            full_output.reshape(heads_local * DV, width),
            preferred_element_type=jnp.float32,
        ),
        "tensor",
    )
    residual = stream + attention
    normed_mid, norm_mid_pull = jax.vjp(rms_norm, residual, w_gains[1])
    normed_mid_low = normed_mid.astype(jnp.bfloat16)
    gate_up = jnp.dot(
        normed_mid_low, full_swiglu.reshape(width, -1), preferred_element_type=jnp.float32
    ).reshape(tokens_dev, 2, units_local)
    gate_part = gate_up[:, 0]
    up_part = gate_up[:, 1]
    sigmoid_gate = jax.nn.sigmoid(gate_part)
    silu_gate = gate_part * sigmoid_gate
    activated_low = (silu_gate * up_part).astype(jnp.bfloat16)
    feedforward = lax.psum(
        jnp.dot(activated_low, full_down, preferred_element_type=jnp.float32).astype(jnp.bfloat16),
        "tensor",
    ).astype(jnp.float32)
    result = residual + feedforward
    grad_ffn = cotangent.astype(jnp.bfloat16)
    grad_down_full = contract_rows(activated_low, grad_ffn)
    grad_activated = contract_cols(grad_ffn, full_down)
    grad_gate = grad_activated * up_part * sigmoid_gate * (1.0 + gate_part * (1.0 - sigmoid_gate))
    grad_up = grad_activated * silu_gate
    grad_gate_up = (
        jnp.stack([grad_gate, grad_up], axis=1)
        .astype(jnp.bfloat16)
        .reshape(tokens_dev, 2 * units_local)
    )
    grad_swiglu_full = contract_rows(normed_mid_low, grad_gate_up).reshape(width, 2, units_local)
    grad_normed_mid = lax.psum(
        contract_cols(grad_gate_up, full_swiglu.reshape(width, 2 * units_local)), "tensor"
    )
    grad_from_mid, grad_gain_mid = norm_mid_pull(grad_normed_mid)
    grad_residual = cotangent + grad_from_mid
    grad_attention = grad_residual.astype(jnp.bfloat16)
    grad_output_full = contract_rows(mixed_low, grad_attention).reshape(heads_local, DV, width)
    grad_mixed = contract_cols(
        grad_attention, full_output.reshape(heads_local * DV, width)
    ).reshape(1, tokens_dev, heads_local, DV)
    grad_mixer_out, grad_gate_raw, grad_scale = finish_pull(grad_mixed)
    correction = states_gradient(
        zero_states, grad_mixer_out, query, key_rows, value_rows, update_gate, log_decay
    )
    linear_turned = jnp.swapaxes(linear_map, -1, -2)
    outgoing = zero_states
    for hop_index in range(lax.axis_size("seq") - 1):
        outgoing = passed_along(apply_map(linear_turned, outgoing) + correction, "seq", -1)
    delta_grads = delta_pull((grad_mixer_out, outgoing))
    (
        grad_conv_rows,
        grad_before,
        grad_conv_local,
        grad_decay_raw,
        grad_update_raw,
        grad_rates_local,
    ) = prepare_pull(delta_grads[1:])
    returned = passed_along(grad_before[0], "seq", -1)
    grad_rows = grad_conv_rows[0].at[tokens_dev - (KCONV - 1) :].add(returned)
    grad_projected = (
        jnp.concatenate([grad_rows, grad_gate_raw[0]], axis=-1)
        .astype(jnp.bfloat16)
        .reshape(tokens_dev, heads_local * input_cols)
    )
    grad_rate_rows = (
        jnp.stack([grad_decay_raw[0], grad_update_raw[0]], axis=-1)
        .astype(jnp.bfloat16)
        .reshape(tokens_dev, heads_local * 2)
    )
    grad_input_full = contract_rows(normed_in_low, grad_projected).reshape(
        width, heads_local, input_cols
    )
    grad_rates_full = contract_rows(normed_in_low, grad_rate_rows).reshape(width, heads_local, 2)
    normed_in_term = contract_cols(
        grad_projected, full_input.reshape(width, heads_local * input_cols)
    ) + contract_cols(grad_rate_rows, full_rates.reshape(width, heads_local * 2))
    grad_normed_in = lax.psum(normed_in_term, "tensor")
    grad_from_in, grad_gain_in = norm_in_pull(grad_normed_in)
    grad_stream = grad_residual + grad_from_in
    reduced = (
        lax.psum_scatter(grad_input_full, ("dp", "seq"), scatter_dimension=0, tiled=True),
        lax.psum_scatter(grad_rates_full, ("dp", "seq"), scatter_dimension=0, tiled=True),
        lax.psum_scatter(grad_output_full, ("dp", "seq"), scatter_dimension=2, tiled=True),
        lax.psum_scatter(grad_swiglu_full, ("dp", "seq"), scatter_dimension=0, tiled=True),
        lax.psum_scatter(grad_down_full, ("dp", "seq"), scatter_dimension=1, tiled=True),
    )
    g_input, g_rates, g_output, g_swiglu, g_down = reduced
    conv_term = lax.dynamic_update_slice_in_dim(
        jnp.zeros_like(w_conv), grad_conv_local, first_head, 1
    )
    heads_term = lax.dynamic_update_slice_in_dim(
        jnp.zeros_like(w_heads), grad_rates_local, first_head, 1
    )
    slice_width = width // lax.axis_size("tensor")
    owned = lax.broadcasted_iota(jnp.int32, (1, width), 1) // slice_width == lax.axis_index(
        "tensor"
    )
    gains_term = jnp.where(owned, jnp.stack([grad_gain_in, grad_gain_mid]), 0.0)
    g_conv, g_heads, g_gains, g_scale = lax.psum(
        (conv_term, heads_term, gains_term, grad_scale), ("dp", "seq", "tensor")
    )
    count = float(tokens_dev * lax.axis_size("dp") * lax.axis_size("seq"))
    new_input, moment_input = adam_update(w_input, g_input, m_input, count)
    new_rates, moment_rates = adam_update(w_rates, g_rates, m_rates, count)
    new_conv, moment_conv = adam_update(w_conv, g_conv, m_conv, count)
    new_output, moment_output = adam_update(w_output, g_output, m_output, count)
    new_swiglu, moment_swiglu = adam_update(w_swiglu, g_swiglu, m_swiglu, count)
    new_down, moment_down = adam_update(w_down, g_down, m_down, count)
    new_gains, moment_gains = adam_update(w_gains, g_gains, m_gains, count)
    new_scale, moment_scale = adam_update(w_scale, g_scale, m_scale, count)
    new_heads, moment_heads = adam_update(w_heads, g_heads, m_heads, count)
    return (
        result,
        grad_stream,
        g_input,
        g_rates,
        g_conv,
        g_output,
        g_swiglu,
        g_down,
        g_gains,
        g_scale,
        g_heads,
        new_input,
        new_rates,
        new_conv,
        new_output,
        new_swiglu,
        new_down,
        new_gains,
        new_scale,
        new_heads,
        moment_input,
        moment_rates,
        moment_conv,
        moment_output,
        moment_swiglu,
        moment_down,
        moment_gains,
        moment_scale,
        moment_heads,
    )


def solution(mesh):
    in_specs = (
        P(("dp", "seq"), None),
        P(("dp", "seq"), None),
        P(("dp", "seq"), "tensor", None),
        P(("dp", "seq"), "tensor", None),
        P(),
        P("tensor", None, ("dp", "seq")),
        P(("dp", "seq"), None, "tensor"),
        P("tensor", ("dp", "seq")),
        P(),
        P(),
        P(),
        P(None, ("dp", "seq"), "tensor", None),
        P(None, ("dp", "seq"), "tensor", None),
        P(),
        P(None, "tensor", None, ("dp", "seq")),
        P(None, ("dp", "seq"), None, "tensor"),
        P(None, "tensor", ("dp", "seq")),
        P(),
        P(),
        P(),
    )
    out_specs = (
        P(("dp", "seq"), None),
        P(("dp", "seq"), None),
        P(("dp", "seq"), "tensor", None),
        P(("dp", "seq"), "tensor", None),
        P(),
        P("tensor", None, ("dp", "seq")),
        P(("dp", "seq"), None, "tensor"),
        P("tensor", ("dp", "seq")),
        P(),
        P(),
        P(),
        P(("dp", "seq"), "tensor", None),
        P(("dp", "seq"), "tensor", None),
        P(),
        P("tensor", None, ("dp", "seq")),
        P(("dp", "seq"), None, "tensor"),
        P("tensor", ("dp", "seq")),
        P(),
        P(),
        P(),
        P(None, ("dp", "seq"), "tensor", None),
        P(None, ("dp", "seq"), "tensor", None),
        P(),
        P(None, "tensor", None, ("dp", "seq")),
        P(None, ("dp", "seq"), None, "tensor"),
        P(None, "tensor", ("dp", "seq")),
        P(),
        P(),
        P(),
    )
    return jax.shard_map(body, mesh=mesh, in_specs=in_specs, out_specs=out_specs, check_vma=False)
```

profile of v0, /device:TPU:0, one launch (start us, length us, event | category | flops | bytes accessed | tf_op | source)
XLA Modules:
  0.0 2840.1 jit_solution(1622207763118015627)
XLA Ops:
  17.1 29.2 %all_gather.15 = bf16[2048,4,2]{0,1,2:T(4,128)(2,1)S(1)} all-gather(bf16[256,4,2]{0,1,2:T(4,128)(2,1)S(1)} %copy.945), channel_id=1, replica_groups=mesh['dp'=2,'seq'=4,'tensor'=4] {'dp','seq'}, dimensions={0}, use_global_device_ids=true | all-gather | bytes 36864 | tf_op jit(solution)/shard_map/all_gather | solution.py:198
  60.3 130.3 %all-gather.5.cloned.1.call-done = bf16[2048,4,768]{2,0,1:T(8,128)(2,1)} async-done(((bf16[256,4,768]{2,0,1:T(8,128)(2,1)}), bf16[2048,4,768]{2,0,1:T(8,128)(2,1)}) %all-gather.5.cloned.1.call-update) | async-done | bytes 12582928 | tf_op jit(solution)/shard_map/all_gather | solution.py:197
  190.6 16.6 copy.621
  238.1 158.0 %custom-call.19 = f32[8,4,1,64,64]{3,4,2,1,0:T(8,128)S(1)} custom-call(f32[8,4,1,64,64]{4,3,2,1,0:T(8,128)} %get-tuple-element.1241), custom_call_target="InvertDiagBlocksLowerTriangular" | custom-call | tf_op jit(solution)/shard_map/jit(_solve_triangular)/vmap(vmap())/triangular_solve | solution.py:72
  396.1 159.2 %custom-call.22 = f32[8,4,1,64,64]{3,4,2,1,0:T(8,128)} custom-call(f32[8,4,1,64,64]{4,3,2,1,0:T(8,128)} %get-tuple-element.1240), custom_call_target="InvertDiagBlocksLowerTriangular" | custom-call | tf_op jit(solution)/shard_map/jit(_solve_triangular)/vmap(vmap())/triangular_solve/custom-call.1 | solution.py:69
  564.1 28.7 %while.68 = (s32[]{:T(128)}, f32[1,4,128,384]{3,2,1,0:T(8,128)S(1)}, f32[8,1,4,1,1]{2,4,3,1,0:T(1,128)S(1)}, f32[8,1,4,64,128]{4,3,2,1,0:T(8,128)}, f32[8,1,4,64...) while((s32[]{:T(128)}, f32[1,4,128,384]{3,2,1,0:T(8,128)S(1)}, ...), condition=%wide.region_4.6_spmd, body=%wide.region_3.5_spmd.sunk | while | flops 302481408 | bytes 3802253 | solution.py:119
  640.9 58.9 %while.69 = (s32[]{:T(128)}, f32[1,4,128,256]{3,2,1,0:T(8,128)S(1)}, f32[8,1,64,4,256]{4,2,3,1,0:T(8,128)}, f32[8,1,4,128,256]{4,3,2,1,0:T(8,128)}, f32[8,1,4,1,...) while((s32[]{:T(128)}, ...), condition=%wide.region_7.9_spmd, body=%wide.region_6.8_spmd.sunk | while | flops 352780288 | bytes 5510337 | solution.py:119
  712.7 15.4 copy.661
  728.1 73.1 %all-reduce.24.cloned.1.call-done = f32[512,2048]{1,0:T(8,128)} async-done(((f32[512,2048]{1,0:T(8,128)}), f32[512,2048]{1,0:T(8,128)}) %all-reduce.24.cloned.1.call-update) | async-done | bytes 4194320 | tf_op jit(solution)/shard_map/psum | solution.py:252
  829.0 193.1 %reduce-scatter.14.cloned.1.call-done = f32[1408,256]{1,0:T(8,128)} async-done(((f32[1408,2048]{1,0:T(8,128)}), f32[1408,256]{1,0:T(8,128)}) %reduce-scatter.14.cloned.1.call-update) | async-done | bytes 1441808 | tf_op jit(solution)/shard_map/reduce_scatter | solution.py:341
  1028.4 92.8 %all-gather.11.cloned.1.call-done = bf16[1408,2048]{1,0:T(8,128)(2,1)} async-done(((bf16[1408,256]{1,0:T(8,128)(2,1)}), bf16[1408,2048]{1,0:T(8,128)(2,1)}) %all-gather.11.cloned.1.call-update) | async-done | bytes 5767184 | tf_op jit(solution)/shard_map/all_gather | solution.py:201
  1151.2 75.5 %all-reduce.28.cloned.1.call-done = f32[512,2048]{1,0:T(8,128)} async-done(((f32[512,2048]{1,0:T(8,128)}), f32[512,2048]{1,0:T(8,128)}) %all-reduce.28.cloned.1.call-update) | async-done | bytes 4194320 | tf_op jit(solution)/shard_map/psum | solution.py:287
  1231.7 49.4 %all-reduce.26.cloned.1.call-done = bf16[512,2048]{1,0:T(8,128)(2,1)} async-done(((bf16[512,2048]{1,0:T(8,128)(2,1)}), bf16[512,2048]{1,0:T(8,128)(2,1)}) %all-reduce.26.cloned.1.call-update) | async-done | bytes 2097168 | tf_op jit(solution)/shard_map/psum | solution.py:271
  1299.5 56.6 %while.71 = (s32[]{:T(128)}, f32[1,4,128,256]{2,3,1,0:T(8,128)S(1)}, f32[8,1,4,1,1]{2,4,3,1,0:T(1,128)S(1)}, f32[8,1,4,64,1]{3,2,4,1,0:T(4,128)S(1)}, f32[8,1,64...) while((s32[]{:T(128)}, ...), condition=%wide.region_16.18_spmd.clone, body=%wide.region_15.17_spmd.clone.sunk | while | flops 353173504 | bytes 4724435 | solution.py:136
  1360.2 14.2 collective-permute-done.4
  1414.6 122.1 %while.70 = (s32[]{:T(128)}, f32[1,4,128,256]{2,3,1,0:T(8,128)S(1)}, f32[8,1,4,64,128]{4,3,2,1,0:T(8,128)}, f32[8,1,4,64,256]{4,3,2,1,0:T(8,128)}, f32[8,1,4,64,...) while((s32[]{:T(128)}, ...), condition=%wide.region_20.22_spmd, body=%wide.region_17.21_spmd.sunk | while | flops 907149056 | bytes 15542597 | solution.py:119
  1648.7 13.9 fusion.105
  1679.4 40.6 %all-reduce.32.cloned.1.call-done = f32[4,16,512]{2,1,0:T(8,128)} async-done(((f32[4,16,512]{2,1,0:T(8,128)}), f32[4,16,512]{2,1,0:T(8,128)}) %all-reduce.32.cloned.1.call-update) | async-done | bytes 131088 | tf_op jit(solution)/shard_map/psum | solution.py:355
  1722.4 64.3 %reduce-scatter.16.cloned.1.call-done = f32[256,8]{1,0:T(8,128)} async-done(((f32[2048,8]{1,0:T(8,128)}), f32[256,8]{1,0:T(8,128)}) %reduce-scatter.16.cloned.1.call-update) | async-done | bytes 8208
  1790.0 84.2 %all-reduce.30.cloned.1.call-done = f32[512,2048]{1,0:T(8,128)} async-done(((f32[512,2048]{1,0:T(8,128)}), f32[512,2048]{1,0:T(8,128)}) %all-reduce.30.cloned.1.call-update) | async-done | bytes 4194320 | tf_op jit(solution)/shard_map/psum | solution.py:333
  1878.7 42.5 %all-reduce.17 = (f32[2,2048]{1,0:T(2,128)S(1)}, f32[256]{0:T(256)S(1)}, f32[2,16]{1,0:T(2,128)S(1)}) all-reduce(f32[2,2048]{1,0:T(2,128)S(1)} %maximum_select_fusion, f32[256]{0:T(256)S(1)} %copy-done.125, f32[2,16]{1,0:T(2,128)S(1)} %dynamic_update_slice.83), channel_id=1, replica_groups=mesh['dp'=2,'seq'=4,'tensor'=4] {'dp','seq','tensor'}, use_global_device_ids=true, to_apply=%region_45.48 | all-reduce | flops 4384 | bytes 35072 | tf_op jit(solution)/shard_map/psum | solution.py:355
  1932.9 96.3 %reduce-scatter.10.cloned.1.call-done = f32[4,256,256]{2,1,0:T(8,128)} async-done(((f32[4,256,2048]{2,1,0:T(8,128)}), f32[4,256,256]{2,1,0:T(8,128)}) %reduce-scatter.10.cloned.1.call-update) | async-done | bytes 1048592 | tf_op jit(solution)/shard_map/reduce_scatter | solution.py:339
  2033.7 372.0 %reduce-scatter.12.cloned.1.call-done = f32[256,2,1408]{2,0,1:T(8,128)} async-done(((f32[2048,2,1408]{2,0,1:T(8,128)}), f32[256,2,1408]{2,0,1:T(8,128)}) %reduce-scatter.12.cloned.1.call-update) | async-done | bytes 2883600 | tf_op jit(solution)/shard_map/reduce_scatter | solution.py:340
  2427.4 384.9 %reduce-scatter.8.cloned.1.call-done = f32[256,4,768]{2,0,1:T(8,128)} async-done(((f32[2048,4,768]{2,0,1:T(8,128)}), f32[256,4,768]{2,0,1:T(8,128)}) %reduce-scatter.8.cloned.1.call-update) | async-done | bytes 3145744 | tf_op jit(solution)/shard_map/reduce_scatter | solution.py:337
  (821 shorter events, 716.3 us)
Async XLA Ops:
  7.2 183.4 %all-gather.5.cloned.1.call-start = ((), (), s32[]{:S(2)}) async-start(), calls=%async_computation.5 | async-start | bytes 14155776 | tf_op jit(solution)/shard_map/all_gather | solution.py:197
  10.9 694.8 %all-gather.7.cloned.1.call-start = ((), (), s32[]{:S(2)}) async-start(), calls=%async_computation.6 | async-start | bytes 4718592 | tf_op jit(solution)/shard_map/all_gather | solution.py:199
  13.1 699.6 %all-gather.9.cloned.1.call-start = ((), (), s32[]{:S(2)}) async-start(), calls=%async_computation.8 | async-start | bytes 12976128 | tf_op jit(solution)/shard_map/all_gather | solution.py:200
  14.4 786.8 %all-reduce.24.cloned.1.call-start = ((), (), s32[]{:S(2)}) async-start(), calls=%async_computation.7 | async-start | bytes 8388608 | tf_op jit(solution)/shard_map/psum | solution.py:252
  59.4 502.6 %copy-start.71 = (f32[8,64,4]{1,2,0:T(4,128)}, f32[8,64,4]{1,2,0:T(4,128)S(1)}, u32[]{:S(2)}) copy-start(f32[8,64,4]{1,2,0:T(4,128)S(1)} %copy.639) | copy-start | bytes 24580
  216.7 3.0 collective-permute-start
  594.3 14.8 collective-permute-start.1
  609.6 14.4 collective-permute-start.2
  626.4 14.5 collective-permute-start.3
  712.6 309.5 %reduce-scatter.14.cloned.1.call-start = ((), (), s32[]{:S(2)}) async-start(), calls=%async_computation.17 | async-start | bytes 12976128 | tf_op jit(solution)/shard_map/reduce_scatter | solution.py:341
  828.7 292.5 %all-gather.11.cloned.1.call-start = ((), (), s32[]{:S(2)}) async-start(), calls=%async_computation.9 | async-start | bytes 6488064 | tf_op jit(solution)/shard_map/all_gather | solution.py:201
  1028.3 198.3 %all-reduce.28.cloned.1.call-start = ((), (), s32[]{:S(2)}) async-start(), calls=%async_computation.11 | async-start | bytes 8388608 | tf_op jit(solution)/shard_map/psum | solution.py:287
  1142.8 138.3 %all-reduce.26.cloned.1.call-start = ((), (), s32[]{:S(2)}) async-start(), calls=%async_computation.10 | async-start | bytes 4194304 | tf_op jit(solution)/shard_map/psum | solution.py:271
  1150.7 569.3 %all-reduce.32.cloned.1.call-start = ((), (), s32[]{:S(2)}) async-start(), calls=%async_computation.14 | async-start | bytes 262144 | tf_op jit(solution)/shard_map/psum | solution.py:355
  1358.9 15.5 collective-permute-start.4
  1376.8 14.9 collective-permute-start.5
  1393.5 13.8 collective-permute-start.6
  1593.7 7.4 collective-permute-start.7
  1595.7 190.9 %reduce-scatter.16.cloned.1.call-start = ((), (), s32[]{:S(2)}) async-start(), calls=%async_computation.18 | async-start | bytes 1179648
  1601.0 273.2 %all-reduce.30.cloned.1.call-start = ((), (), s32[]{:S(2)}) async-start(), calls=%async_computation.12 | async-start | bytes 8388608 | tf_op jit(solution)/shard_map/psum | solution.py:333
  1615.4 413.9 %reduce-scatter.10.cloned.1.call-start = ((), (), s32[]{:S(2)}) async-start(), calls=%async_computation.15 | async-start | bytes 9437184 | tf_op jit(solution)/shard_map/reduce_scatter | solution.py:339
  1625.3 780.4 %reduce-scatter.12.cloned.1.call-start = ((), (), s32[]{:S(2)}) async-start(), calls=%async_computation.16 | async-start | bytes 25952256 | tf_op jit(solution)/shard_map/reduce_scatter | solution.py:340
  1643.7 1168.6 %reduce-scatter.8.cloned.1.call-start = ((), (), s32[]{:S(2)}) async-start(), calls=%async_computation.13 | async-start | bytes 28311552 | tf_op jit(solution)/shard_map/reduce_scatter | solution.py:337
  2421.7 390.6 %copy-start.26 = (f32[256,4,768]{2,1,0:T(4,128)S(1)}, f32[256,4,768]{2,1,0:T(4,128)}, u32[]{:S(2)}) copy-start(f32[256,4,768]{2,1,0:T(4,128)} %param.36) | copy-start | bytes 9437188
  (129 other events, 4825.8 us)
Sparse Core Ops, SparseCore 0:
  11.0 179.4 all-gather.4
  193.2 73.3 all-gather.6
  269.3 162.8 all-gather.8
  712.7 88.3 all-reduce.23
  828.8 193.2 reduce-scatter.13
  1028.4 92.7 all-gather.10
  1142.9 83.6 all-reduce.27
  1229.6 51.5 all-reduce.25
  1595.9 124.0 all-reduce.31
  1724.2 62.4 reduce-scatter.15
  1789.6 84.5 all-reduce.29
  1878.7 150.4 reduce-scatter.9
  2033.1 372.5 reduce-scatter.11
  2409.4 402.8 reduce-scatter.7
where the time goes:
time: 2850 us; the launch traced here: 2840 us
  waiting for transfers between devices  1710 us (60%)
  other arithmetic  446 us (16%)
  matrix products  379 us (13%)
  local copies, waits for them, and re-layouts  192 us (7%)
  blocking collectives  71.7 us (3%)
    reduce_scatter x1, waiting for transfers between devices, body(): lax.psum_scatter(grad_input_full, ('dp', 'seq'), scatter_dimension=0, til...  385 us
    reduce_scatter x1, waiting for transfers between devices, body(): lax.psum_scatter(grad_swiglu_full, ('dp', 'seq'), scatter_dimension=0, ti...  372 us
    reduce_scatter x1, waiting for transfers between devices, body(): lax.psum_scatter(grad_down_full, ('dp', 'seq'), scatter_dimension=1, tile...  193 us
    another operation x3, other arithmetic, block_parts(): jax.scipy.linalg.solve_triangular(system, right_keys, lower=True, unit_di...  161 us
    another operation x4, other arithmetic, block_parts(): jax.scipy.linalg.solve_triangular(system, right_values, lower=True, unit_...  158 us
    all_gather x1, waiting for transfers between devices, body(): lax.all_gather(rounded_weights[0], ('dp', 'seq'), axis=0, tiled=True)  130 us
    reduce_scatter x1, waiting for transfers between devices, body(): lax.psum_scatter(grad_output_full, ('dp', 'seq'), scatter_dimension=2, ti...  96.3 us
    all_gather x1, waiting for transfers between devices, body(): lax.all_gather(rounded_weights[4], ('dp', 'seq'), axis=1, tiled=True)  92.8 us
  transfers between devices with their start and end apart: 22, of which 18 were waited for; matrix products, arithmetic and copies ran while one was open for 23% of the time, Pallas kernels for 0%

commit v1 on v0

--- a/solution.py
+++ b/solution.py
@@ -254,9 +254,9 @@
             mixed_low,
             full_output.reshape(heads_local * DV, width),
             preferred_element_type=jnp.float32,
-        ),
+        ).astype(jnp.bfloat16),
         "tensor",
-    )
+    ).astype(jnp.float32)
     residual = stream + attention
     normed_mid, norm_mid_pull = jax.vjp(rms_norm, residual, w_gains[1])
     normed_mid_low = normed_mid.astype(jnp.bfloat16)
@@ -285,8 +285,11 @@
     )
     grad_swiglu_full = contract_rows(normed_mid_low, grad_gate_up).reshape(width, 2, units_local)
     grad_normed_mid = lax.psum(
-        contract_cols(grad_gate_up, full_swiglu.reshape(width, 2 * units_local)), "tensor"
-    )
+        contract_cols(grad_gate_up, full_swiglu.reshape(width, 2 * units_local)).astype(
+            jnp.bfloat16
+        ),
+        "tensor",
+    ).astype(jnp.float32)
     grad_from_mid, grad_gain_mid = norm_mid_pull(grad_normed_mid)
     grad_residual = cotangent + grad_from_mid
     grad_attention = grad_residual.astype(jnp.bfloat16)
@@ -330,17 +333,17 @@
     normed_in_term = contract_cols(
         grad_projected, full_input.reshape(width, heads_local * input_cols)
     ) + contract_cols(grad_rate_rows, full_rates.reshape(width, heads_local * 2))
-    grad_normed_in = lax.psum(normed_in_term, "tensor")
+    grad_normed_in = lax.psum(normed_in_term.astype(jnp.bfloat16), "tensor").astype(jnp.float32)
     grad_from_in, grad_gain_in = norm_in_pull(grad_normed_in)
     grad_stream = grad_residual + grad_from_in
     reduced = (
-        lax.psum_scatter(grad_input_full, ("dp", "seq"), scatter_dimension=0, tiled=True),
-        lax.psum_scatter(grad_rates_full, ("dp", "seq"), scatter_dimension=0, tiled=True),
-        lax.psum_scatter(grad_output_full, ("dp", "seq"), scatter_dimension=2, tiled=True),
-        lax.psum_scatter(grad_swiglu_full, ("dp", "seq"), scatter_dimension=0, tiled=True),
-        lax.psum_scatter(grad_down_full, ("dp", "seq"), scatter_dimension=1, tiled=True),
-    )
-    g_input, g_rates, g_output, g_swiglu, g_down = reduced
+        lax.psum_scatter(grad_input_full.astype(jnp.bfloat16), ("dp", "seq"), scatter_dimension=0, tiled=True),
+        lax.psum_scatter(grad_rates_full.astype(jnp.bfloat16), ("dp", "seq"), scatter_dimension=0, tiled=True),
+        lax.psum_scatter(grad_output_full.astype(jnp.bfloat16), ("dp", "seq"), scatter_dimension=2, tiled=True),
+        lax.psum_scatter(grad_swiglu_full.astype(jnp.bfloat16), ("dp", "seq"), scatter_dimension=0, tiled=True),
+        lax.psum_scatter(grad_down_full.astype(jnp.bfloat16), ("dp", "seq"), scatter_dimension=1, tiled=True),
+    )
+    g_input, g_rates, g_output, g_swiglu, g_down = [g.astype(jnp.float32) for g in reduced]
     conv_term = lax.dynamic_update_slice_in_dim(
         jnp.zeros_like(w_conv), grad_conv_local, first_head, 1
     )

time: 2850 us -> 2200 us (0.77)
  waiting for transfers between devices: 1710 us -> 1080 us
    reduce_scatter x4, waiting for transfers between devices: 1050 us -> 527 us  [the longest x1 192 us: body(): lax.psum_scatter(grad_swiglu_full.astype(jnp.bfloat16), ('dp', 'seq'), sc...]
    psum x1 -> x0, waiting for transfers between devices: 84.2 us -> none  [body(): grad_normed_in = lax.psum(normed_in_term, 'tensor')]
    psum x1, waiting for transfers between devices: 49.4 us -> 84.7 us  [body(): lax.psum(jnp.dot(activated_low, full_down, preferred_element_type=jnp.flo...]
    psum x1, waiting for transfers between devices: 73.1 us -> 38.6 us  [body(): lax.psum(jnp.dot(mixed_low, full_output.reshape(heads_local * DV, width),...]
    unnamed x15 -> x14, waiting for transfers between devices: 64.5 us -> 62.8 us
    unnamed x281 -> x311, local copies, waits for them, and re-layouts: 60.5 us -> 62.3 us
  transfers between devices with their start and end apart: 22 -> 21, of which waited for: 18 -> 17; matrix products, arithmetic and copies ran while one was open for 23% -> 30% of each run, Pallas kernels for 0% -> 0%
where the time goes in v1:
time: 2200 us; the launch traced here: 2190 us
  waiting for transfers between devices  1080 us (49%)
  other arithmetic  434 us (20%)
  matrix products  374 us (17%)
  local copies, waits for them, and re-layouts  190 us (9%)
  blocking collectives  71.2 us (3%)
  starting transfers between devices  22.6 us (1%)
    reduce_scatter x1, waiting for transfers between devices, body(): lax.psum_scatter(grad_swiglu_full.astype(jnp.bfloat16), ('dp', 'seq'), sc...  192 us
    reduce_scatter x1, waiting for transfers between devices, body(): lax.psum_scatter(grad_input_full.astype(jnp.bfloat16), ('dp', 'seq'), sca...  191 us
    another operation x3, other arithmetic, block_parts(): jax.scipy.linalg.solve_triangular(system, right_keys, lower=True, unit_di...  161 us
    another operation x4, other arithmetic, block_parts(): jax.scipy.linalg.solve_triangular(system, right_values, lower=True, unit_...  159 us
    all_gather x1, waiting for transfers between devices, body(): lax.all_gather(rounded_weights[0], ('dp', 'seq'), axis=0, tiled=True)  130 us
    reduce_scatter x1, waiting for transfers between devices, body(): lax.psum_scatter(grad_down_full.astype(jnp.bfloat16), ('dp', 'seq'), scat...  110 us
    all_gather x1, waiting for transfers between devices, body(): lax.all_gather(rounded_weights[4], ('dp', 'seq'), axis=1, tiled=True)  93.5 us
    psum x1, waiting for transfers between devices, body(): lax.psum(jnp.dot(activated_low, full_down, preferred_element_type=jnp.flo...  84.7 us
  transfers between devices with their start and end apart: 21, of which 17 were waited for; matrix products, arithmetic and copies ran while one was open for 30% of the time, Pallas kernels for 0%

profile of v1, /device:TPU:0, one launch (start us, length us, event | category | flops | bytes accessed | tf_op | source)
XLA Modules:
  0.0 2188.6 jit_solution(4615630992131319105)
XLA Ops:
  17.3 29.1 %all_gather.15 = bf16[2048,4,2]{0,1,2:T(4,128)(2,1)S(1)} all-gather(bf16[256,4,2]{0,1,2:T(4,128)(2,1)S(1)} %copy.944), channel_id=1, replica_groups=mesh['dp'=2,'seq'=4,'tensor'=4] {'dp','seq'}, dimensions={0}, use_global_device_ids=true | all-gather | bytes 36864 | tf_op jit(solution)/shard_map/all_gather | solution.py:198
  60.7 129.9 %all-gather.5.cloned.1.call-done = bf16[2048,4,768]{2,0,1:T(8,128)(2,1)} async-done(((bf16[256,4,768]{2,0,1:T(8,128)(2,1)}), bf16[2048,4,768]{2,0,1:T(8,128)(2,1)}) %all-gather.5.cloned.1.call-update) | async-done | bytes 12582928 | tf_op jit(solution)/shard_map/all_gather | solution.py:197
  190.7 16.8 copy.621
  237.3 158.7 %custom-call.19 = f32[8,4,1,64,64]{3,4,2,1,0:T(8,128)} custom-call(f32[8,4,1,64,64]{4,3,2,1,0:T(8,128)} %get-tuple-element.1243), custom_call_target="InvertDiagBlocksLowerTriangular" | custom-call | tf_op jit(solution)/shard_map/jit(_solve_triangular)/vmap(vmap())/triangular_solve | solution.py:72
  396.0 159.2 %custom-call.22 = f32[8,4,1,64,64]{3,4,2,1,0:T(8,128)} custom-call(f32[8,4,1,64,64]{4,3,2,1,0:T(8,128)} %get-tuple-element.1242), custom_call_target="InvertDiagBlocksLowerTriangular" | custom-call | tf_op jit(solution)/shard_map/jit(_solve_triangular)/vmap(vmap())/triangular_solve/custom-call.1 | solution.py:69
  565.9 28.7 %while.68 = (s32[]{:T(128)}, f32[1,4,128,384]{3,2,1,0:T(8,128)S(1)}, f32[8,1,4,1,1]{2,4,3,1,0:T(1,128)S(1)}, f32[8,1,4,64,128]{4,3,2,1,0:T(8,128)}, f32[8,1,4,64...) while((s32[]{:T(128)}, f32[1,4,128,384]{3,2,1,0:T(8,128)S(1)}, ...), condition=%wide.region_4.6_spmd, body=%wide.region_3.5_spmd.sunk | while | flops 302481408 | bytes 3802753 | solution.py:119
  642.4 58.9 %while.69 = (s32[]{:T(128)}, f32[1,4,128,256]{3,2,1,0:T(8,128)S(1)}, f32[8,1,64,4,256]{4,2,3,1,0:T(8,128)}, f32[8,1,4,128,256]{4,3,2,1,0:T(8,128)}, f32[8,1,4,1,...) while((s32[]{:T(128)}, ...), condition=%wide.region_7.9_spmd, body=%wide.region_6.8_spmd.sunk | while | flops 352780288 | bytes 5511853 | solution.py:119
  713.5 15.3 copy.661
  728.8 38.6 %all-reduce.24.cloned.1.call-done = bf16[512,2048]{1,0:T(8,128)(2,1)} async-done(((bf16[512,2048]{1,0:T(8,128)(2,1)}), bf16[512,2048]{1,0:T(8,128)(2,1)}) %all-reduce.24.cloned.1.call-update) | async-done | bytes 2097168 | tf_op jit(solution)/shard_map/psum | solution.py:252
  792.2 110.3 %reduce-scatter.14.cloned.1.call-done = bf16[1408,256]{1,0:T(8,128)(2,1)} async-done(((bf16[1408,2048]{1,0:T(8,128)(2,1)}), bf16[1408,256]{1,0:T(8,128)(2,1)}) %reduce-scatter.14.cloned.1.call-update) | async-done | bytes 720912 | tf_op jit(solution)/shard_map/reduce_scatter | solution.py:344
  908.6 93.5 %all-gather.11.cloned.1.call-done = bf16[1408,2048]{1,0:T(8,128)(2,1)} async-done(((bf16[1408,256]{1,0:T(8,128)(2,1)}), bf16[1408,2048]{1,0:T(8,128)(2,1)}) %all-gather.11.cloned.1.call-update) | async-done | bytes 5767184 | tf_op jit(solution)/shard_map/all_gather | solution.py:201
  1023.9 49.2 %all-reduce.26.cloned.1.call-done = bf16[512,2048]{1,0:T(8,128)(2,1)} async-done(((bf16[512,2048]{1,0:T(8,128)(2,1)}), bf16[512,2048]{1,0:T(8,128)(2,1)}) %all-reduce.26.cloned.1.call-update) | async-done | bytes 2097168 | tf_op jit(solution)/shard_map/psum | solution.py:287
  1089.1 56.6 %while.71 = (s32[]{:T(128)}, f32[1,4,128,256]{2,3,1,0:T(8,128)S(1)}, f32[8,1,4,1,1]{2,4,3,1,0:T(1,128)S(1)}, f32[8,1,4,64,1]{3,2,4,1,0:T(4,128)S(1)}, f32[8,1,64...) while((s32[]{:T(128)}, ...), condition=%wide.region_16.18_spmd.clone, body=%wide.region_15.17_spmd.clone.sunk | while | flops 353173504 | bytes 4724427 | solution.py:136
  1202.0 122.0 %while.70 = (s32[]{:T(128)}, f32[1,4,128,256]{2,3,1,0:T(8,128)S(1)}, f32[8,1,4,64,128]{4,3,2,1,0:T(8,128)}, f32[8,1,4,64,256]{4,3,2,1,0:T(8,128)}, f32[8,1,4,64,...) while((s32[]{:T(128)}, ...), condition=%wide.region_20.22_spmd, body=%wide.region_17.21_spmd.sunk | while | flops 907149056 | bytes 15542589 | solution.py:119
  1390.4 13.9 fusion.108
  1417.7 11.7 convolution_convert_fusion
  1434.8 11.8 convolution_convert_fusion.2
  1460.6 47.8 %all-reduce.28.cloned.1.call-done = f32[4,16,512]{2,1,0:T(8,128)} async-done(((f32[4,16,512]{2,1,0:T(8,128)}), f32[4,16,512]{2,1,0:T(8,128)}) %all-reduce.28.cloned.1.call-update) | async-done | bytes 131088 | tf_op jit(solution)/shard_map/psum | solution.py:358
  1510.8 62.5 %reduce-scatter.16.cloned.1.call-done = bf16[256,8]{1,0:T(8,128)(2,1)} async-done(((bf16[2048,8]{1,0:T(8,128)(2,1)}), bf16[256,8]{1,0:T(8,128)(2,1)}) %reduce-scatter.16.cloned.1.call-update) | async-done | bytes 4112
  1576.3 84.7 %all-reduce.30.cloned.1.call-done = (bf16[512,2048]{1,0:T(8,128)(2,1)}, bf16[512,2048]{1,0:T(8,128)(2,1)}) async-done(((bf16[512,2048]{1,0:T(8,128)(2,1)}, bf16[512,2048]{1,0:T(8,128)(2,1)}), (bf16[512,2048]{1,0:T(8,128)(2,1)}, bf16[512,2048]{1,0:T(8,128)(2,1)})) %all-reduce.30.cloned.1.call-update) | async-done | bytes 4194320 | tf_op jit(solution)/shard_map/psum | solution.py:271
  1665.4 42.2 %all-reduce.17 = (f32[2,2048]{1,0:T(2,128)S(1)}, f32[256]{0:T(256)S(1)}, f32[2,16]{1,0:T(2,128)S(1)}) all-reduce(f32[2,2048]{1,0:T(2,128)S(1)} %maximum_select_fusion, f32[256]{0:T(256)S(1)} %copy-done.136, f32[2,16]{1,0:T(2,128)S(1)} %dynamic_update_slice.83), channel_id=1, replica_groups=mesh['dp'=2,'seq'=4,'tensor'=4] {'dp','seq','tensor'}, use_global_device_ids=true, to_apply=%region_45.48 | all-reduce | flops 4384 | bytes 35072 | tf_op jit(solution)/shard_map/psum | solution.py:358
  1721.2 33.7 %reduce-scatter.10.cloned.1.call-done = bf16[4,256,256]{2,1,0:T(8,128)(2,1)} async-done(((bf16[4,256,2048]{2,1,0:T(8,128)(2,1)}), bf16[4,256,256]{2,1,0:T(8,128)(2,1)}) %reduce-scatter.10.cloned.1.call-update) | async-done | bytes 524304 | tf_op jit(solution)/shard_map/reduce_scatter | solution.py:342
  1759.5 191.7 %reduce-scatter.12.cloned.1.call-done = bf16[256,2,1408]{2,0,1:T(8,128)(2,1)} async-done(((bf16[2048,2,1408]{2,0,1:T(8,128)(2,1)}), bf16[256,2,1408]{2,0,1:T(8,128)(2,1)}) %reduce-scatter.12.cloned.1.call-update) | async-done | bytes 1441808 | tf_op jit(solution)/shard_map/reduce_scatter | solution.py:343
  1971.0 190.8 %reduce-scatter.8.cloned.1.call-done = bf16[256,4,768]{2,0,1:T(8,128)(2,1)} async-done(((bf16[2048,4,768]{2,0,1:T(8,128)(2,1)}), bf16[256,4,768]{2,0,1:T(8,128)(2,1)}) %reduce-scatter.8.cloned.1.call-update) | async-done | bytes 1572880 | tf_op jit(solution)/shard_map/reduce_scatter | solution.py:340
  (853 shorter events, 678.9 us)
Async XLA Ops:
  7.2 183.4 %all-gather.5.cloned.1.call-start = ((), (), s32[]{:S(2)}) async-start(), calls=%async_computation.5 | async-start | bytes 14155776 | tf_op jit(solution)/shard_map/all_gather | solution.py:197
  10.9 696.3 %all-gather.7.cloned.1.call-start = ((), (), s32[]{:S(2)}) async-start(), calls=%async_computation.6 | async-start | bytes 4718592 | tf_op jit(solution)/shard_map/all_gather | solution.py:199
  13.1 700.4 %all-gather.9.cloned.1.call-start = ((), (), s32[]{:S(2)}) async-start(), calls=%async_computation.8 | async-start | bytes 12976128 | tf_op jit(solution)/shard_map/all_gather | solution.py:200
  14.4 753.0 %all-reduce.24.cloned.1.call-start = ((), (), s32[]{:S(2)}) async-start(), calls=%async_computation.7 | async-start | bytes 4194304 | tf_op jit(solution)/shard_map/psum | solution.py:252
  59.5 497.0 %copy-start.81 = (f32[8,64,4]{1,2,0:T(4,128)}, f32[8,64,4]{1,2,0:T(4,128)S(1)}, u32[]{:S(2)}) copy-start(f32[8,64,4]{1,2,0:T(4,128)S(1)} %copy.639) | copy-start | bytes 24580
  59.6 495.5 %copy-start.83 = (f32[8,64,4]{1,2,0:T(4,128)}, f32[8,64,4]{1,2,0:T(4,128)S(1)}, u32[]{:S(2)}) copy-start(f32[8,64,4]{1,2,0:T(4,128)S(1)} %copy.619) | copy-start | bytes 24580
  217.0 3.4 collective-permute-start
  227.8 328.7 %copy-start.1 = (f32[1,512,4,128]{3,1,2,0:T(8,128)}, f32[1,512,4,128]{3,1,2,0:T(8,128)S(1)}, u32[]{:S(2)}) copy-start(f32[1,512,4,128]{3,1,2,0:T(8,128)S(1)} %get-tuple-element.1234) | copy-start | bytes 3145732
  596.0 14.6 collective-permute-start.1
  611.2 14.3 collective-permute-start.2
  627.9 14.5 collective-permute-start.3
  713.4 189.1 %reduce-scatter.14.cloned.1.call-start = ((), (), s32[]{:S(2)}) async-start(), calls=%async_computation.15 | async-start | bytes 6488064 | tf_op jit(solution)/shard_map/reduce_scatter | solution.py:344
  792.0 210.1 %all-gather.11.cloned.1.call-start = ((), (), s32[]{:S(2)}) async-start(), calls=%async_computation.9 | async-start | bytes 6488064 | tf_op jit(solution)/shard_map/all_gather | solution.py:201
  908.5 164.6 %all-reduce.26.cloned.1.call-start = ((), (), s32[]{:S(2)}) async-start(), calls=%async_computation.10 | async-start | bytes 4194304 | tf_op jit(solution)/shard_map/psum | solution.py:287
  1023.4 485.0 %all-reduce.28.cloned.1.call-start = ((), (), s32[]{:S(2)}) async-start(), calls=%async_computation.12 | async-start | bytes 262144 | tf_op jit(solution)/shard_map/psum | solution.py:358
  1149.3 15.8 collective-permute-start.4
  1166.7 14.6 collective-permute-start.5
  1182.0 13.7 collective-permute-start.6
  1380.3 8.2 collective-permute-start.7
  1384.1 189.2 %reduce-scatter.16.cloned.1.call-start = ((), (), s32[]{:S(2)}) async-start(), calls=%async_computation.16 | async-start | bytes 589824
  1388.4 272.6 %all-reduce.30.cloned.1.call-start = ((), (), s32[]{:S(2)}) async-start(), calls=%async_computation.17 | async-start | bytes 8388608 | tf_op jit(solution)/shard_map/psum | solution.py:271
  1404.3 350.6 %reduce-scatter.10.cloned.1.call-start = ((), (), s32[]{:S(2)}) async-start(), calls=%async_computation.13 | async-start | bytes 4718592 | tf_op jit(solution)/shard_map/reduce_scatter | solution.py:342
  1412.8 538.5 %reduce-scatter.12.cloned.1.call-start = ((), (), s32[]{:S(2)}) async-start(), calls=%async_computation.14 | async-start | bytes 12976128 | tf_op jit(solution)/shard_map/reduce_scatter | solution.py:343
  1429.4 732.3 %reduce-scatter.8.cloned.1.call-start = ((), (), s32[]{:S(2)}) async-start(), calls=%async_computation.11 | async-start | bytes 14155776 | tf_op jit(solution)/shard_map/reduce_scatter | solution.py:340
  (143 other events, 3403.4 us)
Sparse Core Ops, SparseCore 0:
  11.0 179.5 all-gather.4
  193.2 73.7 all-gather.6
  269.7 162.9 all-gather.8
  713.5 53.8 all-reduce.23
  792.1 110.4 reduce-scatter.13
  908.7 93.4 all-gather.10
  1023.5 49.5 all-reduce.25
  1384.2 124.1 all-reduce.27
  1512.3 60.9 reduce-scatter.15
  1576.3 84.6 all-reduce.29
  1665.2 89.6 reduce-scatter.9
  1758.8 192.4 reduce-scatter.11
  1955.3 206.4 reduce-scatter.7

commit v2 on v0

v2 whole, which is shorter than its diff:
```python
import functools

import jax
import jax.numpy as jnp
from jax import lax
from jax.experimental import pallas as pl
from jax.experimental.pallas import tpu as pltpu
from jax.sharding import PartitionSpec as P

DK = 128
DV = 256
QKV = 2 * DK + DV
KCONV = 4
CHUNK = 128
ADAM_STEP = 5
VMEM = 48 * 2**20

F32 = jnp.float32
BF16 = jnp.bfloat16
HIGHEST = lax.Precision.HIGHEST

NN = (((1,), (0,)), ((), ()))
NT = (((1,), (1,)), ((), ()))
TN = (((0,), (0,)), ((), ()))


def dot(left, right, dims):
    return lax.dot_general(left, right, dims, preferred_element_type=F32)


def halves(array):
    high = array.astype(BF16)
    return high, (array - high.astype(F32)).astype(BF16)


def mm(left, right, dims=NN):
    left_high, left_low = halves(left)
    right_high, right_low = halves(right)
    return (
        dot(left_high, right_high, dims)
        + dot(left_high, right_low, dims)
        + dot(left_low, right_high, dims)
    )


def each(function, *lists):
    return [function(*items) for items in zip(*lists)]


def unit_lower_inverses(strict_parts, row_index, column_index):
    size = strict_parts[0].shape[0]
    identity = (row_index == column_index).astype(F32)
    same = (row_index // 8) == (column_index // 8)
    small = [jnp.where(same, part, 0.0) for part in strict_parts]
    squared = each(mm, small, small)
    fourth = each(mm, squared, squared)
    first = each(lambda n, n2: mm(identity - n, identity + n2), small, squared)
    inverse = each(lambda a, n4: a + mm(a, n4), first, fourth)
    width = 8
    while width < size:
        pair = (row_index // (2 * width)) == (column_index // (2 * width))
        below = pair & ((row_index // width) != (column_index // width))
        lower = [jnp.where(below, part, 0.0) for part in strict_parts]
        inner = each(mm, lower, inverse)
        inverse = each(lambda x, y: x - mm(x, y), inverse, inner)
        width *= 2
    return inverse


def silu_parts(values):
    gate = 1.0 / (1.0 + jnp.exp(-values))
    return values * gate, gate


def filtered_parts(padded_ref, rows_ref, halo_ref, taps_ref):
    length = rows_ref.shape[0]
    padded_ref[0:8, :] = halo_ref[0]
    padded_ref[8 : 8 + length, :] = rows_ref[...]
    raw = taps_ref[0:1, :] * padded_ref[5 : 5 + length, :]
    for tap in range(1, KCONV):
        raw = raw + taps_ref[tap : tap + 1, :] * padded_ref[5 + tap : 5 + tap + length, :]
    filtered, gate = silu_parts(raw)
    return raw, gate, filtered


def unit_rows(rows):
    factor = lax.rsqrt(jnp.sum(rows * rows, axis=-1, keepdims=True) + 1e-06)
    return rows * factor, factor


def chunk_slices(array, count):
    return [array[i * CHUNK : (i + 1) * CHUNK] for i in range(count)]


def fades(columns, g_rows, row_index, column_index):
    within = row_index >= column_index
    result = []
    for i, column in enumerate(columns):
        gap = column[:, 1:2] - g_rows[0:1, i * CHUNK : (i + 1) * CHUNK]
        result.append(jnp.where(within, jnp.exp(jnp.where(within, gap, 0.0)), 0.0))
    return result


def forward_kernel(
    rows_ref,
    halo_ref,
    taps_ref,
    columns_ref,
    g_rows_ref,
    reach_ref,
    local_ref,
    end_ref,
    starts_ref,
    inverse_ref,
    solved_values_ref,
    solved_keys_ref,
    step_ref,
    seen_ref,
    padded_ref,
):
    length = rows_ref.shape[0]
    count = length // CHUNK
    raw, gate, filtered = filtered_parts(padded_ref, rows_ref, halo_ref, taps_ref)
    query = unit_rows(filtered[:, :DK])[0] * DK ** (-0.5)
    key = unit_rows(filtered[:, DK : 2 * DK])[0]
    value = filtered[:, 2 * DK :]
    row_index = lax.broadcasted_iota(jnp.int32, (CHUNK, CHUNK), 0)
    column_index = lax.broadcasted_iota(jnp.int32, (CHUNK, CHUNK), 1)
    identity = (row_index == column_index).astype(F32)
    strict = row_index > column_index
    queries, keys, values = (chunk_slices(a, count) for a in (query, key, value))
    columns = chunk_slices(columns_ref[0], count)
    fade = fades(columns, g_rows_ref[0], row_index, column_index)
    key_products = each(lambda k: mm(k, k, NT), keys)
    parts = each(
        lambda kk, f, c: jnp.where(strict, c[:, 0:1] * kk * f, 0.0), key_products, fade, columns
    )
    inverses = unit_lower_inverses(parts, row_index, column_index)
    scores = each(lambda q, k, f: mm(q, k, NT) * f, queries, keys, fade)
    solved_values = each(lambda t, v, c: mm(t, c[:, 0:1] * v), inverses, values, columns)
    solved_keys = each(lambda t, k, c: mm(t, c[:, 0:1] * c[:, 2:3] * k), inverses, keys, columns)
    seen = each(
        lambda q, s, w, c: c[:, 2:3] * q - mm(s, w), queries, scores, solved_keys, columns
    )
    inner = each(mm, scores, solved_values)
    faded = each(lambda k, c: (c[:, 3:4] * k).T, keys, columns)
    steps = each(
        lambda k, w, c: c[CHUNK - 1 : CHUNK, 2:3] * identity - mm(k, w),
        faded,
        solved_keys,
        columns,
    )
    added = each(mm, faded, solved_values)
    state = jnp.concatenate([jnp.zeros((DK, DV), F32), identity], axis=1)
    for i in range(count):
        here = slice(i * CHUNK, (i + 1) * CHUNK)
        starts_ref[0, i] = state
        reached = mm(seen[i], state)
        local_ref[0, here, :] = reached[:, :DV] + inner[i]
        reach_ref[0, here, :] = reached[:, DV:]
        state = mm(steps[i], state)
        state = jnp.concatenate([state[:, :DV] + added[i], state[:, DV:]], axis=1)
        inverse_ref[0, here, :] = inverses[i]
        solved_values_ref[0, here, :] = solved_values[i]
        solved_keys_ref[0, here, :] = solved_keys[i]
        step_ref[0, here, :] = steps[i]
        seen_ref[0, here, :] = seen[i]
    end_ref[0] = state


def finish_kernel(local_ref, reach_ref, state_ref, gate_ref, scale_ref, mixed_ref):
    mixer_out = local_ref[0] + mm(reach_ref[0], state_ref[0])
    factor = lax.rsqrt(jnp.mean(mixer_out * mixer_out, axis=-1, keepdims=True) + 1e-05)
    opened = silu_parts(gate_ref[...])[0]
    mixed_ref[...] = (mixer_out * factor * scale_ref[...] * opened).astype(BF16)


def finish_back_kernel(
    local_ref,
    reach_ref,
    state_ref,
    gate_ref,
    scale_ref,
    grad_ref,
    grad_out_ref,
    grad_gate_ref,
    grad_scale_ref,
    correction_ref,
):
    mixer_out = local_ref[0] + mm(reach_ref[0], state_ref[0])
    factor = lax.rsqrt(jnp.mean(mixer_out * mixer_out, axis=-1, keepdims=True) + 1e-05)
    normal = mixer_out * factor
    gate_raw = gate_ref[...]
    opened, gate = silu_parts(gate_raw)
    grad = grad_ref[...]
    scale = scale_ref[...]
    with_normal = grad * normal
    grad_gate_ref[...] = (
        with_normal * scale * gate * (1.0 + gate_raw * (1.0 - gate))
    ).astype(BF16)
    summed = jnp.sum(with_normal * opened, axis=0, keepdims=True)
    grad_scale_ref[0] = jnp.broadcast_to(summed, (8, DV))
    grad_normal = grad * scale * opened
    shared = jnp.mean(grad_normal * normal, axis=-1, keepdims=True)
    grad_out = factor * (grad_normal - normal * shared)
    grad_out_ref[0] = grad_out
    correction_ref[0] = mm(reach_ref[0].T, grad_out)


def backward_kernel(
    rows_ref,
    halo_ref,
    taps_ref,
    columns_ref,
    g_rows_ref,
    starts_ref,
    inverse_ref,
    solved_values_ref,
    solved_keys_ref,
    step_ref,
    seen_ref,
    state_ref,
    later_ref,
    grad_out_ref,
    grad_rows_ref,
    tail_ref,
    before_ref,
    grad_taps_ref,
    grad_columns_ref,
    padded_ref,
    grad_padded_ref,
):
    length = rows_ref.shape[0]
    count = length // CHUNK
    raw, gate, filtered = filtered_parts(padded_ref, rows_ref, halo_ref, taps_ref)
    query_unit, query_factor = unit_rows(filtered[:, :DK])
    key, key_factor = unit_rows(filtered[:, DK : 2 * DK])
    query = query_unit * DK ** (-0.5)
    value = filtered[:, 2 * DK :]
    row_index = lax.broadcasted_iota(jnp.int32, (CHUNK, CHUNK), 0)
    column_index = lax.broadcasted_iota(jnp.int32, (CHUNK, CHUNK), 1)
    strict = row_index > column_index
    last = lax.broadcasted_iota(jnp.int32, (CHUNK, 1), 0) == CHUNK - 1
    queries, keys, values = (chunk_slices(a, count) for a in (query, key, value))
    columns = chunk_slices(columns_ref[0], count)
    inverses = chunk_slices(inverse_ref[0], count)
    solved_values = chunk_slices(solved_values_ref[0], count)
    solved_keys = chunk_slices(solved_keys_ref[0], count)
    steps = chunk_slices(step_ref[0], count)
    seen = chunk_slices(seen_ref[0], count)
    grad_outs = chunk_slices(grad_out_ref[0], count)
    fade = fades(columns, g_rows_ref[0], row_index, column_index)
    incoming = state_ref[0]
    states = [starts_ref[0, i][:, :DV] + mm(starts_ref[0, i][:, DV:], incoming) for i in range(count)]
    own_grads = each(lambda s, o: mm(s.T, o), seen, grad_outs)
    later = [None] * count
    carried = later_ref[0]
    for i in reversed(range(count)):
        later[i] = carried
        if i > 0:
            carried = mm(steps[i].T, carried) + own_grads[i]
    key_products = each(lambda k: mm(k, k, NT), keys)
    query_products = each(lambda q, k: mm(q, k, NT), queries, keys)
    scores = each(lambda p, f: p * f, query_products, fade)
    fresh = each(lambda u, w, s: u - mm(w, s), solved_values, solved_keys, states)
    faded = each(lambda k, c: c[:, 3:4] * k, keys, columns)
    grad_fresh = each(
        lambda p, o, k, l: mm(p.T, o) + mm(k, l), scores, grad_outs, faded, later
    )
    grad_scaled = each(lambda t, g: mm(t.T, g), inverses, grad_fresh)
    grad_scaled_keys = each(lambda g, s: -mm(g, s, NT), grad_scaled, states)
    grad_lower = each(
        lambda g, f: jnp.where(strict, -mm(g, f, NT), 0.0), grad_scaled, fresh
    )
    grad_scores = each(lambda o, f, d: mm(o, f, NT) * d, grad_outs, fresh, fade)
    lower_fade = each(lambda g, d: g * d, grad_lower, fade)
    pairs = each(lambda h, c: c[:, 0:1] * h, lower_fade, columns)
    from_state = each(lambda o, s: mm(o, s, NT), grad_outs, states)
    from_later = each(lambda f, l: mm(f, l, NT), fresh, later)
    grad_queries = each(
        lambda c, a, g, k: c[:, 2:3] * a + mm(g, k), columns, from_state, grad_scores, keys
    )
    grad_keys = each(
        lambda c, b, p, k, g, q, e: c[:, 0:1] * c[:, 2:3] * b
        + mm(p + p.T, k)
        + mm(g.T, q)
        + c[:, 3:4] * e,
        columns,
        grad_scaled_keys,
        pairs,
        keys,
        grad_scores,
        queries,
        from_later,
    )
    grad_values = each(lambda c, g: c[:, 0:1] * g, columns, grad_scaled)

    def across(array):
        return jnp.sum(array, axis=-1, keepdims=True)

    for i in range(count):
        column = columns[i]
        key_term = column[:, 2:3] * across(grad_scaled_keys[i] * keys[i])
        grad_update = (
            across(grad_scaled[i] * values[i])
            + key_term
            + across(lower_fade[i] * key_products[i])
        )
        both = grad_scores[i] * query_products[i] + pairs[i] * key_products[i]
        trailing = column[:, 3:4] * across(keys[i] * from_later[i])
        whole = column[CHUNK - 1 : CHUNK, 2:3] * jnp.sum(
            across(later[i] * states[i]), axis=0, keepdims=True
        ) + jnp.sum(trailing, axis=0, keepdims=True)
        grad_g = (
            across(both - both.T)
            + column[:, 2:3] * across(queries[i] * from_state[i])
            + column[:, 0:1] * key_term
            - trailing
            + jnp.where(last, whole, 0.0)
        )
        lane = lax.broadcasted_iota(jnp.int32, (CHUNK, 8), 1)
        grad_columns_ref[0, i * CHUNK : (i + 1) * CHUNK, :] = jnp.where(
            lane == 0, grad_update, grad_g
        )
    grad_query = jnp.concatenate(grad_queries, axis=0) * DK ** (-0.5)
    grad_key = jnp.concatenate(grad_keys, axis=0)
    grad_value = jnp.concatenate(grad_values, axis=0)
    grad_query = query_factor * (grad_query - query_unit * across(query_unit * grad_query))
    grad_key = key_factor * (grad_key - key * across(key * grad_key))
    grad_filtered = jnp.concatenate([grad_query, grad_key, grad_value], axis=1)
    grad_raw = grad_filtered * gate * (1.0 + raw * (1.0 - gate))
    zeros = jnp.zeros((8, QKV), F32)
    grad_padded_ref[0:8, :] = zeros
    grad_padded_ref[8 : 8 + length, :] = grad_raw
    grad_padded_ref[8 + length : 16 + length, :] = zeros
    grad_rows = taps_ref[0:1, :] * grad_padded_ref[11 : 11 + length, :]
    before = taps_ref[0:1, :] * grad_padded_ref[3:11, :]
    for tap in range(1, KCONV):
        tap_row = taps_ref[tap : tap + 1, :]
        grad_rows = grad_rows + tap_row * grad_padded_ref[11 - tap : 11 - tap + length, :]
        before = before + tap_row * grad_padded_ref[3 - tap : 11 - tap, :]
    grad_rows_ref[...] = grad_rows.astype(BF16)
    tail_ref[0] = grad_rows[length - 8 :]
    before_ref[0] = before
    sums = [
        jnp.sum(grad_raw * padded_ref[5 + tap : 5 + tap + length, :], axis=0, keepdims=True)
        for tap in range(KCONV)
    ]
    grad_taps_ref[0] = jnp.concatenate(sums, axis=0)


def chains_call(kernel, chains, heads, length, operands, outputs, scratch, flops):
    def spec(tag, shape):
        if tag == "rows":
            return pl.BlockSpec((length, shape[1] // heads), lambda i: (i // heads, i % heads))
        if tag == "edge":
            return pl.BlockSpec((1, 8, shape[2] // heads), lambda i: (i // heads, 0, i % heads))
        if tag == "taps":
            return pl.BlockSpec((shape[0], shape[1] // heads), lambda i: (0, i % heads))
        if tag == "all":
            return pl.BlockSpec(shape, lambda i: (0,) * len(shape))
        return pl.BlockSpec((1,) + tuple(shape[1:]), lambda i: (i,) + (0,) * (len(shape) - 1))

    moved = sum(a.size * a.dtype.itemsize for _, a in operands)
    return pl.pallas_call(
        kernel,
        grid=(chains,),
        in_specs=[spec(tag, a.shape) for tag, a in operands],
        out_specs=[spec(tag, shape) for tag, shape, _ in outputs],
        out_shape=[jax.ShapeDtypeStruct(shape, dtype) for _, shape, dtype in outputs],
        scratch_shapes=scratch,
        compiler_params=pltpu.CompilerParams(vmem_limit_bytes=VMEM),
        cost_estimate=pl.CostEstimate(
            flops=chains * flops, bytes_accessed=2 * moved, transcendentals=0
        ),
    )(*[a for _, a in operands])


def shifted(block, axis, distance):
    devices = range(lax.axis_size(axis))
    route = [(i, i + distance) for i in devices if i + distance in devices]
    return lax.ppermute(block, axis, route)


def swapped(block, axis, bits):
    return lax.ppermute(block, axis, [(i, i ^ bits) for i in range(lax.axis_size(axis))])


def group_swapped(block, dp_bits, tensor_bits):
    dp_size, tensor_size = lax.axis_size("dp"), lax.axis_size("tensor")
    route = [
        (d * tensor_size + t, (d ^ dp_bits) * tensor_size + (t ^ tensor_bits))
        for d in range(dp_size)
        for t in range(tensor_size)
    ]
    return lax.ppermute(block, ("dp", "tensor"), route)


def partner_bits():
    chips = lax.axis_size("tensor") // 2
    return [(d, t) for d in range(lax.axis_size("dp")) for t in range(chips) if (d, t) != (0, 0)]


def bits_slot(dp_bits, chip_bits):
    return dp_bits * (lax.axis_size("tensor") // 2) + chip_bits


def scatter_relative(partial):
    half = partial.shape[0] // 2
    summed = partial[:half].astype(F32) + swapped(partial[half:], "tensor", 1).astype(F32)
    rows = half // (lax.axis_size("dp") * lax.axis_size("tensor") // 2)
    total = summed[:rows]
    low = summed.astype(BF16)
    for d, t in partner_bits():
        slot = bits_slot(d, t)
        received = group_swapped(low[slot * rows : (slot + 1) * rows], d, 2 * t)
        total = total + received.astype(F32)
    return total


def gather_relative(own):
    parts = [own] + [group_swapped(own, d, 2 * t) for d, t in partner_bits()]
    here = jnp.concatenate(parts, axis=0)
    return jnp.concatenate([here, swapped(here, "tensor", 1)], axis=0)


def scatter_absolute(partial):
    dp_size, chips = lax.axis_size("dp"), lax.axis_size("tensor") // 2
    core = lax.axis_index("tensor") % 2
    chip = lax.axis_index("tensor") // 2
    device = lax.axis_index("dp")
    rows = partial.shape[0] // (2 * dp_size * chips)
    blocks = partial.reshape(dp_size * chips, 2, rows, -1)
    even, odd = blocks[:, 0], blocks[:, 1]
    mine = jnp.where(core == 0, even, odd)
    theirs = jnp.where(core == 0, odd, even)
    summed = mine.astype(F32) + swapped(theirs, "tensor", 1).astype(F32)
    low = summed.astype(BF16)
    total = lax.dynamic_index_in_dim(summed, device * chips + chip, 0, keepdims=False)
    for d, t in partner_bits():
        target = (device ^ d) * chips + (chip ^ t)
        block = lax.dynamic_index_in_dim(low, target, 0, keepdims=False)
        total = total + group_swapped(block, d, 2 * t).astype(F32)
    return total


def ordered(parts, core, other):
    first = jnp.where(core == 0, parts, other)
    second = jnp.where(core == 0, other, parts)
    stacked = jnp.stack([first, second], axis=1)
    return stacked.reshape((-1,) + parts.shape[2:])


def gather_absolute(own, over_dp=True):
    dp_size = lax.axis_size("dp") if over_dp else 1
    chips = lax.axis_size("tensor") // 2
    core = lax.axis_index("tensor") % 2
    chip = lax.axis_index("tensor") // 2
    device = lax.axis_index("dp") if over_dp else 0
    here = jnp.zeros((dp_size * chips,) + own.shape, own.dtype)
    here = lax.dynamic_update_index_in_dim(here, own, device * chips + chip, 0)
    for d, t in partner_bits():
        if d < dp_size:
            received = group_swapped(own, d, 2 * t)
            source = (device ^ d) * chips + (chip ^ t)
            here = lax.dynamic_update_index_in_dim(here, received, source, 0)
    return ordered(here, core, swapped(here, "tensor", 1))


def butterfly_sum(array):
    for axis in ("tensor", "dp", "seq"):
        distance = 1
        while distance < lax.axis_size(axis):
            array = array + swapped(array, axis, distance)
            distance *= 2
    return array


def contract_cols(left, right):
    return dot(left, right, NT)


def contract_rows(left, right):
    return dot(left, right, TN)


def adam_update(weight, gradient, moments, token_count):
    mean_grad = gradient / token_count
    first = 0.5 * moments[0] + 0.5 * mean_grad
    second = 0.5 * moments[1] + 0.5 * mean_grad * mean_grad
    correction = 1.0 - 0.5**ADAM_STEP
    change = first / correction / (jnp.sqrt(second / correction) + 1e-08) + 0.1 * weight
    return (weight - 0.1 * change, jnp.stack([first, second]))


def norm_parts(rows):
    factor = lax.rsqrt(jnp.mean(rows * rows, axis=-1, keepdims=True) + 1e-06)
    return factor, rows * factor


def norm_back(factor, normal, gain, grad):
    scaled = grad * gain
    shared = jnp.mean(scaled * normal, axis=-1, keepdims=True)
    return factor * (scaled - normal * shared), jnp.sum(grad * normal, axis=0)


def body(
    stream,
    cotangent,
    w_input,
    w_rates,
    w_conv,
    w_output,
    w_swiglu,
    w_down,
    w_gains,
    w_scale,
    w_heads,
    m_input,
    m_rates,
    m_conv,
    m_output,
    m_swiglu,
    m_down,
    m_gains,
    m_scale,
    m_heads,
):
    dp_size, seq_size, tensor_size = (lax.axis_size(a) for a in ("dp", "seq", "tensor"))
    length, width = stream.shape
    depth = w_input.shape[0]
    heads_stored = w_input.shape[1]
    heads = heads_stored // dp_size
    units_stored = w_swiglu.shape[2]
    units = units_stored // dp_size
    rows = length // tensor_size
    chains = dp_size * heads
    first_part = lax.axis_index("dp") == 0
    first_head = lax.axis_index("tensor") * heads_stored + lax.axis_index("dp") * heads

    def turned(array):
        cut = array.reshape(array.shape[:-1] + (dp_size, seq_size, depth))
        return jnp.swapaxes(cut, -3, -2).reshape(array.shape)

    def turned_back(array):
        cut = array.reshape(array.shape[:-1] + (seq_size, dp_size, depth))
        return jnp.swapaxes(cut, -3, -2).reshape(array.shape)

    def mine_and_theirs(low, high):
        return jnp.where(first_part, low, high), jnp.where(first_part, high, low)

    def by_device(own, received):
        return jnp.where(first_part, own, received), jnp.where(first_part, received, own)

    low_input = w_input.astype(BF16)
    low_output = jnp.transpose(w_output.astype(BF16), (2, 0, 1))
    low_swiglu = w_swiglu.astype(BF16)
    low_down = w_down.astype(BF16).T

    def half_columns(index):
        chosen = slice(index * heads, (index + 1) * heads)
        some = slice(index * units, (index + 1) * units)
        return (
            low_input[:, chosen, :QKV].reshape(depth, -1),
            jnp.concatenate(
                [
                    low_input[:, chosen, QKV:].reshape(depth, -1),
                    low_output[:, chosen].reshape(depth, -1),
                ],
                axis=1,
            ),
            jnp.concatenate(
                [low_swiglu[:, 0, some], low_swiglu[:, 1, some], low_down[:, some]], axis=1
            ),
        )

    gathered = []
    for low, high in zip(half_columns(0), half_columns(1)):
        mine, theirs = mine_and_theirs(low, high)
        received = swapped(theirs, "dp", 1)
        shard = jnp.concatenate(by_device(mine, received), axis=0)
        gathered.append(lax.all_gather(shard, "seq", axis=0, tiled=True))
    full_qkv, full_mixer, full_ffn = gathered
    full_gate, full_output = full_mixer[:, : heads * DV], full_mixer[:, heads * DV :]
    full_swiglu, full_down = full_ffn[:, : 2 * units], full_ffn[:, 2 * units :]

    copies = dp_size * seq_size
    rates_low = jnp.broadcast_to(w_rates.astype(BF16).reshape(1, -1), (copies, depth * heads_stored * 2))
    rates_all = lax.all_to_all(rates_low, ("dp", "seq"), 0, 0, tiled=True)
    rates_all = rates_all.reshape(dp_size, seq_size, depth, dp_size, heads * 2)
    rates_all = jnp.swapaxes(rates_all, 0, 1).reshape(width, dp_size, heads * 2)
    full_rates = jnp.where(first_part, rates_all[:, 0], rates_all[:, dp_size - 1])

    quarter = lax.axis_index("tensor") * rows
    stream_rows = turned(lax.dynamic_slice_in_dim(stream, quarter, rows, 0))
    cotangent_rows = turned(lax.dynamic_slice_in_dim(cotangent, quarter, rows, 0))
    gains = turned(w_gains)
    factor_in, normal_in = norm_parts(stream_rows)
    normed_in = gather_absolute((normal_in * gains[0]).astype(BF16)).reshape(-1, width)
    grad_ffn = gather_relative(cotangent_rows.astype(BF16))

    projected = dot(normed_in, full_qkv, NN)
    rates = dot(normed_in, full_rates, NN)
    last_rows = projected.reshape(dp_size, length, heads * QKV)[:, length - 8 :]
    halo = shifted(last_rows, "seq", 1)
    taps = lax.dynamic_slice_in_dim(w_conv, first_head, heads, 1).reshape(KCONV, heads * QKV)
    head_rates = lax.dynamic_slice_in_dim(w_heads, first_head, heads, 1)
    by_chain = jnp.transpose(rates.reshape(dp_size, length, heads, 2), (3, 0, 2, 1))
    decay_raw = by_chain[0] + head_rates[1][None, :, None]
    update = jax.nn.sigmoid(by_chain[1]).reshape(chains, length)
    log_decay = -jnp.exp(head_rates[0])[None, :, None] * jax.nn.softplus(decay_raw)
    count = length // CHUNK
    upper = jnp.triu(jnp.ones((CHUNK, CHUNK), F32))
    cumulative = jnp.dot(
        log_decay.reshape(-1, CHUNK), upper, precision=HIGHEST
    ).reshape(chains, count, CHUNK)
    trailing = jnp.exp(cumulative[:, :, -1:] - cumulative).reshape(chains, length)
    cumulative = cumulative.reshape(chains, length)
    zero = jnp.zeros_like(update)
    columns = jnp.stack(
        [update, cumulative, jnp.exp(cumulative), trailing, zero, zero, zero, zero], axis=-1
    )
    g_rows = jnp.broadcast_to(cumulative[:, None, :], (chains, 8, length))
    call = functools.partial(chains_call, chains=chains, heads=heads, length=length)
    unit = 2 * CHUNK * DK * DK * count
    padded = pltpu.VMEM((length + 8, QKV), F32)
    reach, local, end, starts, inverse, solved_values, solved_keys, steps, seen = call(
        forward_kernel,
        operands=[
            ("rows", projected),
            ("edge", halo),
            ("taps", taps),
            ("chain", columns),
            ("chain", g_rows),
        ],
        outputs=[
            ("chain", (chains, length, DK), F32),
            ("chain", (chains, length, DV), F32),
            ("chain", (chains, DK, DV + DK), F32),
            ("chain", (chains, count, DK, DV + DK), F32),
            ("chain", (chains, length, CHUNK), F32),
            ("chain", (chains, length, DV), F32),
            ("chain", (chains, length, DK), F32),
            ("chain", (chains, length, DK), F32),
            ("chain", (chains, length, DK), F32),
        ],
        scratch=[padded],
        flops=90 * unit,
    )
    offset_map, linear_map = end[..., :DV], end[..., DV:]
    incoming = jnp.zeros((chains, DK, DV), F32)
    for hop in range(seq_size - 1):
        moved = offset_map
        if hop > 0:
            moved = moved + jnp.einsum("bkj,bjw->bkw", linear_map, incoming, precision=HIGHEST)
        incoming = shifted(moved, "seq", 1)
    gate_raw = dot(normed_in, full_gate, NN)
    scale_row = w_scale.reshape(1, DV)
    (mixed,) = call(
        finish_kernel,
        operands=[
            ("chain", local),
            ("chain", reach),
            ("chain", incoming),
            ("rows", gate_raw),
            ("all", scale_row),
        ],
        outputs=[("rows", (dp_size * length, heads * DV), BF16)],
        scratch=[],
        flops=6 * unit,
    )
    attention = scatter_absolute(contract_cols(mixed, full_output).astype(BF16))

    residual = stream_rows + attention
    factor_mid, normal_mid = norm_parts(residual)
    normed_mid = gather_relative((normal_mid * gains[1]).astype(BF16))
    gate_up = dot(normed_mid, full_swiglu, NN)
    gate_part, up_part = gate_up[:, :units], gate_up[:, units:]
    sigmoid_gate = jax.nn.sigmoid(gate_part)
    silu_gate = gate_part * sigmoid_gate
    activated = (silu_gate * up_part).astype(BF16)
    grad_activated = dot(grad_ffn, full_down, NN)
    grad_gate = grad_activated * up_part * sigmoid_gate * (1.0 + gate_part * (1.0 - sigmoid_gate))
    grad_up = grad_activated * silu_gate
    grad_gate_up = jnp.concatenate([grad_gate.astype(BF16), grad_up.astype(BF16)], axis=1)
    grad_normed_mid = scatter_relative(contract_cols(grad_gate_up, full_swiglu).astype(BF16))
    from_mid, grad_gain_mid = norm_back(factor_mid, normal_mid, gains[1], grad_normed_mid)
    grad_attention = gather_absolute((cotangent_rows + from_mid).astype(BF16)).reshape(-1, width)
    feedforward = scatter_relative(contract_cols(activated, full_down).astype(BF16))
    grad_ffn_weights = jnp.concatenate(
        [
            contract_rows(normed_mid, grad_gate_up).astype(BF16),
            contract_rows(grad_ffn, activated).astype(BF16),
        ],
        axis=1,
    )
    added = gather_absolute((attention + feedforward).astype(BF16), False).reshape(length, width)
    result = stream + turned_back(added).astype(F32)

    grad_mixed = dot(grad_attention, full_output, NN)
    grad_mixer_out, grad_gate_raw, grad_scale, correction = call(
        finish_back_kernel,
        operands=[
            ("chain", local),
            ("chain", reach),
            ("chain", incoming),
            ("rows", gate_raw),
            ("all", scale_row),
            ("rows", grad_mixed),
        ],
        outputs=[
            ("chain", (chains, length, DV), F32),
            ("rows", (dp_size * length, heads * DV), BF16),
            ("chain", (chains, 8, DV), F32),
            ("chain", (chains, DK, DV), F32),
        ],
        scratch=[],
        flops=12 * unit,
    )
    later = jnp.zeros((chains, DK, DV), F32)
    for hop in range(seq_size - 1):
        moved = correction
        if hop > 0:
            moved = moved + jnp.einsum("bjk,bjw->bkw", linear_map, later, precision=HIGHEST)
        later = shifted(moved, "seq", -1)
    grad_mixer_weights = jnp.concatenate(
        [
            contract_rows(normed_in, grad_gate_raw).astype(BF16),
            contract_rows(grad_attention, mixed).astype(BF16),
        ],
        axis=1,
    )
    grad_rows, tail, before, grad_taps, grad_columns = call(
        backward_kernel,
        operands=[
            ("rows", projected),
            ("edge", halo),
            ("taps", taps),
            ("chain", columns),
            ("chain", g_rows),
            ("chain", starts),
            ("chain", inverse),
            ("chain", solved_values),
            ("chain", solved_keys),
            ("chain", steps),
            ("chain", seen),
            ("chain", incoming),
            ("chain", later),
            ("chain", grad_mixer_out),
        ],
        outputs=[
            ("rows", (dp_size * length, heads * QKV), BF16),
            ("edge", (dp_size, 8, heads * QKV), F32),
            ("edge", (dp_size, 8, heads * QKV), F32),
            ("chain", (chains, KCONV, QKV), F32),
            ("chain", (chains, length, 8), F32),
        ],
        scratch=[padded, pltpu.VMEM((length + 16, QKV), F32)],
        flops=120 * unit,
    )
    patched = (tail + shifted(before, "seq", -1)).astype(BF16)
    grad_projected = grad_rows.reshape(dp_size, length, heads * QKV)
    grad_projected = lax.dynamic_update_slice_in_dim(grad_projected, patched, length - 8, 1)
    grad_projected = grad_projected.reshape(dp_size * length, heads * QKV)
    grad_update = grad_columns[..., 0]
    grad_log_decay = jnp.dot(
        grad_columns[..., 1].reshape(-1, CHUNK), upper.T, precision=HIGHEST
    ).reshape(dp_size, heads, length)
    grad_decay_raw = (
        -jnp.exp(head_rates[0])[None, :, None] * grad_log_decay * jax.nn.sigmoid(decay_raw)
    )
    grad_update_raw = (grad_update * update * (1.0 - update)).reshape(dp_size, heads, length)
    grad_rates = jnp.stack([grad_decay_raw, grad_update_raw], axis=-1)
    grad_rates = jnp.transpose(grad_rates, (0, 2, 1, 3)).reshape(-1, heads * 2).astype(BF16)
    grad_heads = jnp.stack(
        [
            jnp.sum(grad_log_decay * log_decay, axis=(0, 2)),
            jnp.sum(grad_decay_raw, axis=(0, 2)),
        ]
    )
    grad_qkv_weights = contract_rows(normed_in, grad_projected).astype(BF16)
    grad_rates_weights = contract_rows(normed_in, grad_rates)
    normed_in_term = (
        contract_cols(grad_projected, full_qkv)
        + contract_cols(grad_gate_raw, full_gate)
        + contract_cols(grad_rates, full_rates)
    )
    grad_normed_in = scatter_absolute(normed_in_term.astype(BF16))
    from_in, grad_gain_in = norm_back(factor_in, normal_in, gains[0], grad_normed_in)
    changed = gather_absolute((from_mid + from_in).astype(BF16), False).reshape(length, width)
    grad_stream = cotangent + turned_back(changed).astype(F32)

    scattered = []
    for full in (grad_ffn_weights, grad_mixer_weights, grad_qkv_weights):
        part = lax.psum_scatter(full, "seq", scatter_dimension=0, tiled=True)
        own, theirs = mine_and_theirs(part[:depth], part[depth:])
        received = swapped(theirs, "dp", 1)
        scattered.append(tuple(a.astype(F32) for a in by_device(own, received)))
    ffn_parts, mixer_parts, qkv_parts = scattered
    g_input = jnp.concatenate(
        [
            jnp.concatenate(
                [
                    q.reshape(depth, heads, QKV),
                    m[:, : heads * DV].reshape(depth, heads, DV),
                ],
                axis=2,
            )
            for q, m in zip(qkv_parts, mixer_parts)
        ],
        axis=1,
    )
    g_output = jnp.concatenate(
        [m[:, heads * DV :].T.reshape(heads, DV, depth) for m in mixer_parts], axis=0
    )
    g_swiglu = jnp.stack(
        [
            jnp.concatenate([f[:, :units] for f in ffn_parts], axis=1),
            jnp.concatenate([f[:, units : 2 * units] for f in ffn_parts], axis=1),
        ],
        axis=1,
    )
    g_down = jnp.concatenate([f[:, 2 * units :].T for f in ffn_parts], axis=0)

    conv_term = jnp.zeros_like(w_conv)
    grad_taps = jnp.sum(grad_taps.reshape(dp_size, heads, KCONV, QKV), axis=0)
    conv_term = lax.dynamic_update_slice_in_dim(
        conv_term, jnp.swapaxes(grad_taps, 0, 1), first_head, 1
    )
    heads_term = lax.dynamic_update_slice_in_dim(
        jnp.zeros_like(w_heads), grad_heads, first_head, 1
    )
    gains_term = turned_back(jnp.stack([grad_gain_in, grad_gain_mid]))
    scale_term = jnp.sum(grad_scale[:, 0], axis=0)
    rates_term = lax.dynamic_update_slice_in_dim(
        jnp.zeros((dp_size, width, heads * 2), F32),
        grad_rates_weights[None],
        lax.axis_index("dp"),
        0,
    )
    rates_term = jnp.transpose(rates_term, (1, 0, 2))
    small = [conv_term, heads_term, gains_term, scale_term]
    flat = butterfly_sum(jnp.concatenate([a.reshape(-1) for a in small]))
    sums, at = [], 0
    for a in small:
        sums.append(flat[at : at + a.size].reshape(a.shape))
        at += a.size
    g_conv, g_heads, g_gains, g_scale = sums
    rates_term = rates_term.reshape(seq_size, dp_size, depth, heads_stored * 2)
    rates_term = jnp.swapaxes(rates_term, 0, 1).reshape(dp_size * seq_size, -1)
    g_rates = jnp.sum(
        lax.all_to_all(rates_term, ("dp", "seq"), 0, 0, tiled=True), axis=0
    ).reshape(depth, heads_stored, 2)

    tokens = float(length * dp_size * seq_size)
    new_input, moment_input = adam_update(w_input, g_input, m_input, tokens)
    new_rates, moment_rates = adam_update(w_rates, g_rates, m_rates, tokens)
    new_conv, moment_conv = adam_update(w_conv, g_conv, m_conv, tokens)
    new_output, moment_output = adam_update(w_output, g_output, m_output, tokens)
    new_swiglu, moment_swiglu = adam_update(w_swiglu, g_swiglu, m_swiglu, tokens)
    new_down, moment_down = adam_update(w_down, g_down, m_down, tokens)
    new_gains, moment_gains = adam_update(w_gains, g_gains, m_gains, tokens)
    new_scale, moment_scale = adam_update(w_scale, g_scale, m_scale, tokens)
    new_heads, moment_heads = adam_update(w_heads, g_heads, m_heads, tokens)
    return (
        result,
        grad_stream,
        g_input,
        g_rates,
        g_conv,
        g_output,
        g_swiglu,
        g_down,
        g_gains,
        g_scale,
        g_heads,
        new_input,
        new_rates,
        new_conv,
        new_output,
        new_swiglu,
        new_down,
        new_gains,
        new_scale,
        new_heads,
        moment_input,
        moment_rates,
        moment_conv,
        moment_output,
        moment_swiglu,
        moment_down,
        moment_gains,
        moment_scale,
        moment_heads,
    )


def solution(mesh):
    in_specs = (
        P(("dp", "seq"), None),
        P(("dp", "seq"), None),
        P(("dp", "seq"), "tensor", None),
        P(("dp", "seq"), "tensor", None),
        P(),
        P("tensor", None, ("dp", "seq")),
        P(("dp", "seq"), None, "tensor"),
        P("tensor", ("dp", "seq")),
        P(),
        P(),
        P(),
        P(None, ("dp", "seq"), "tensor", None),
        P(None, ("dp", "seq"), "tensor", None),
        P(),
        P(None, "tensor", None, ("dp", "seq")),
        P(None, ("dp", "seq"), None, "tensor"),
        P(None, "tensor", ("dp", "seq")),
        P(),
        P(),
        P(),
    )
    out_specs = (
        P(("dp", "seq"), None),
        P(("dp", "seq"), None),
        P(("dp", "seq"), "tensor", None),
        P(("dp", "seq"), "tensor", None),
        P(),
        P("tensor", None, ("dp", "seq")),
        P(("dp", "seq"), None, "tensor"),
        P("tensor", ("dp", "seq")),
        P(),
        P(),
        P(),
        P(("dp", "seq"), "tensor", None),
        P(("dp", "seq"), "tensor", None),
        P(),
        P("tensor", None, ("dp", "seq")),
        P(("dp", "seq"), None, "tensor"),
        P("tensor", ("dp", "seq")),
        P(),
        P(),
        P(),
        P(None, ("dp", "seq"), "tensor", None),
        P(None, ("dp", "seq"), "tensor", None),
        P(),
        P(None, "tensor", None, ("dp", "seq")),
        P(None, ("dp", "seq"), None, "tensor"),
        P(None, "tensor", ("dp", "seq")),
        P(),
        P(),
        P(),
    )
    return jax.shard_map(body, mesh=mesh, in_specs=in_specs, out_specs=out_specs, check_vma=False)
```

time: 2850 us -> 1020 us (0.36)
  waiting for transfers between devices: 1710 us -> 432 us
  other arithmetic: 446 us -> 126 us
  matrix products: 379 us -> 106 us
  blocking collectives: 71.7 us -> 0 us
  Pallas kernels: 0 us -> 68.8 us
  starting transfers between devices: 22.5 us -> 85.4 us
    reduce_scatter x4 -> x3, waiting for transfers between devices: 1050 us -> 0.01 us  [body(): part = lax.psum_scatter(full, 'seq', scatter_dimension=0, tiled=True)]
    ppermute x8 -> x55, waiting for transfers between devices: 53.9 us -> 382 us  [the longest x8 161 us: shifted(): return lax.ppermute(block, axis, route)]
    psum x5 -> x0, waiting for transfers between devices: 323 us -> none  [the longest x1 84.2 us: body(): grad_normed_in = lax.psum(normed_in_term, 'tensor')]
    another operation x9 -> x10, other arithmetic: 326 us -> 7.1 us  [the longest x6 4.42 us: ordered(): stacked = jnp.stack([first, second], axis=1)]
    dot_general x189 -> x24, matrix products: 359 us -> 106 us  [the longest x18 103 us: dot(): return lax.dot_general(left, right, dims, preferred_element_type=F32)]
    all_gather x4 -> x3, waiting for transfers between devices: 223 us -> 33.6 us  [body(): gathered.append(lax.all_gather(shard, 'seq', axis=0, tiled=True))]
    pallas_call x0 -> x4, Pallas kernels: none -> 68.8 us  [chains_call(): pl.pallas_call(kernel, grid=(chains,), in_specs=[spec(tag, a.shape) for t...]
    unnamed x15 -> x6, waiting for transfers between devices: 64.5 us -> 0.1 us
  transfers between devices with their start and end apart: 22 -> 63, of which waited for: 18 -> 37; matrix products, arithmetic and copies ran while one was open for 23% -> 30% of each run, Pallas kernels for 0% -> 6%
where the time goes in v2:
time: 1020 us; the launch traced here: 1010 us
  waiting for transfers between devices  432 us (42%)
  local copies, waits for them, and re-layouts  172 us (17%)
  other arithmetic  126 us (12%)
  matrix products  106 us (10%)
  starting transfers between devices  85.4 us (8%)
  Pallas kernels  68.8 us (7%)
  between operations  16.8 us (2%)
    ppermute x8, waiting for transfers between devices, shifted(): return lax.ppermute(block, axis, route)  161 us
    ppermute x26, waiting for transfers between devices, group_swapped(): return lax.ppermute(block, ('dp', 'tensor'), route)  130 us
    dot_general x18, matrix products, dot(): return lax.dot_general(left, right, dims, preferred_element_type=F32)  103 us
    ppermute x21, waiting for transfers between devices, swapped(): lax.ppermute(block, axis, [(i, i ^ bits) for i in range(lax.axis_size(axi...  91.9 us
    unnamed x269, local copies, waits for them, and re-layouts  84.4 us
    pallas_call x4, Pallas kernels, chains_call(): pl.pallas_call(kernel, grid=(chains,), in_specs=[spec(tag, a.shape) for t...  68.8 us
    all_gather x3, waiting for transfers between devices, body(): gathered.append(lax.all_gather(shard, 'seq', axis=0, tiled=True))  33.6 us
    ppermute x26, starting transfers between devices, group_swapped(): return lax.ppermute(block, ('dp', 'tensor'), route)  31.6 us
  transfers between devices with their start and end apart: 63, of which 37 were waited for; matrix products, arithmetic and copies ran while one was open for 30% of the time, Pallas kernels for 6%

profile of v2, /device:TPU:0, one launch (start us, length us, event | category | flops | bytes accessed | tf_op | source)
XLA Modules:
  0.0 1007.1 jit_solution(5356882855022098999)
XLA Ops:
  14.5 11.9 %collective-permute-done.4 = bf16[256,1024]{1,0:T(8,128)(2,1)S(1)} collective-permute-done((bf16[256,1024]{1,0:T(8,128)(2,1)}, bf16[256,1024]{1,0:T(8,128)(2,1)S(1)}, u32[]{:S(2)}, u32[]{:S(2)}) %collective-permute-start.4) | collective-permute-done | bytes 524320 | tf_op jit(solution)/shard_map/ppermute | solution.py:386
  81.5 12.4 %collective-permute-done.18 = bf16[256,2112]{0,1:T(8,128)(2,1)} collective-permute-done((bf16[256,2112]{0,1:T(8,128)(2,1)}, bf16[256,2112]{0,1:T(8,128)(2,1)}, u32[]{:S(2)}, u32[]{:S(2)}) %collective-permute-start.18) | collective-permute-done | bytes 1081376 | tf_op jit(solution)/shard_map/ppermute | solution.py:386
  127.9 25.0 %shard_map.419 = (f32[4,512,128]{2,1,0:T(8,128)S(1)}, f32[4,512,256]{2,1,0:T(8,128)}, f32[4,128,384]{2,1,0:T(8,128)S(1)}, f32[4,4,128,384]{3,2,1,0:T(8,128)}, f3...) custom-call(f32[1024,1024]{1,0:T(8,128)} %copy-done.104, ...), custom_call_target="tpu_custom_call" | custom-call | flops 6039797760 | bytes 8814592 | tf_op jit(solution)/shard_map/pallas_call | solution.py:365
  158.1 23.0 %collective-permute-done.6 = f32[4,128,256]{2,1,0:T(8,128)S(1)} collective-permute-done((f32[4,128,256]{2,1,0:T(8,128)S(1)}, f32[4,128,256]{2,1,0:T(8,128)S(1)}, u32[]{:S(2)}, u32[]{:S(2)}) %collective-permute-start.6) | collective-permute-done | bytes 524320 | tf_op jit(solution)/shard_map/ppermute | solution.py:382
  181.7 11.3 %collective-permute-start.7 = (f32[4,128,256]{2,1,0:T(8,128)S(1)}, f32[4,128,256]{2,1,0:T(8,128)S(1)}, u32[]{:S(2)}, u32[]{:S(2)}) collective-permute-start(f32[4,128,256]{2,1,0:T(8,128)S(1)} %convolution_add_fusion.3), channel_id=1, source_target_pairs={{0,4},{4,8},{8,12},{1,5},{5,9},{9,13},{2,6},{6,10},{10,14},{3,7},{... | collective-permute-start | bytes 1572872 | tf_op jit(solution)/shard_map/ppermute | solution.py:382
  193.0 18.3 %collective-permute-done.7 = f32[4,128,256]{2,1,0:T(8,128)S(1)} collective-permute-done((f32[4,128,256]{2,1,0:T(8,128)S(1)}, f32[4,128,256]{2,1,0:T(8,128)S(1)}, u32[]{:S(2)}, u32[]{:S(2)}) %collective-permute-start.7) | collective-permute-done | bytes 524320 | tf_op jit(solution)/shard_map/ppermute | solution.py:382
  225.2 13.5 %collective-permute-done.8.state_ref = f32[4,128,256]{2,1,0:T(8,128)} collective-permute-done((f32[4,128,256]{2,1,0:T(8,128)}, f32[4,128,256]{2,1,0:T(8,128)}, u32[]{:S(2)}, u32[]{:S(2)}) %collective-permute-start.8) | collective-permute-done | bytes 524320 | tf_op jit(solution)/shard_map/ppermute | solution.py:382
  295.7 11.6 %collective-permute-done.12 = bf16[128,2048]{1,0:T(8,128)(2,1)S(1)} collective-permute-done((bf16[128,2048]{1,0:T(8,128)(2,1)S(1)}, bf16[128,2048]{1,0:T(8,128)(2,1)S(1)}, u32[]{:S(2)}, u32[]{:S(2)}) %collective-permute-start.12) | collective-permute-done | bytes 524320 | tf_op jit(solution)/shard_map/ppermute | solution.py:396
  312.5 11.4 %collective-permute-done.14 = bf16[128,2048]{1,0:T(8,128)(2,1)S(1)} collective-permute-done((bf16[128,2048]{1,0:T(8,128)(2,1)S(1)}, bf16[128,2048]{1,0:T(8,128)(2,1)S(1)}, u32[]{:S(2)}, u32[]{:S(2)}) %collective-permute-start.14) | collective-permute-done | bytes 524320 | tf_op jit(solution)/shard_map/ppermute | solution.py:396
  323.9 11.0 %collective-permute-done.15 = bf16[128,2048]{1,0:T(8,128)(2,1)S(1)} collective-permute-done((bf16[128,2048]{1,0:T(8,128)(2,1)S(1)}, bf16[128,2048]{1,0:T(8,128)(2,1)S(1)}, u32[]{:S(2)}, u32[]{:S(2)}) %collective-permute-start.15) | collective-permute-done | bytes 524320 | tf_op jit(solution)/shard_map/ppermute | solution.py:396
  340.8 27.3 %all-gather.8.cloned.1.call-done = bf16[2048,2112]{0,1:T(8,128)(2,1)} async-done(((bf16[512,2112]{0,1:T(8,128)(2,1)}), bf16[2048,2112]{0,1:T(8,128)(2,1)}) %all-gather.8.cloned.1.call-update) | async-done | bytes 8650768 | tf_op jit(solution)/shard_map/all_gather | solution.py:582
  368.1 10.7 %fusion.2 = f32[1024,1408]{1,0:T(8,128)S(1)} fusion(bf16[1024,2048]{1,0:T(8,128)(2,1)} %constant_dynamic-update-slice_fusion, bf16[2048,2112]{0,1:T(8,128)(2,1)} %all-gather.8.cloned.1.call-done), kind=kOutput, calls=%fused_computation.7 | convolution fusion | flops 5905580032 | bytes 15728640 | tf_op jit(solution)/shard_map/dot_general | solution.py:28
  400.6 11.3 %collective-permute-done.30 = bf16[128,2048]{1,0:T(8,128)(2,1)S(1)} collective-permute-done((bf16[128,2048]{1,0:T(8,128)(2,1)S(1)}, bf16[128,2048]{1,0:T(8,128)(2,1)S(1)}, u32[]{:S(2)}, u32[]{:S(2)}) %collective-permute-start.30) | collective-permute-done | bytes 524320 | tf_op jit(solution)/shard_map/ppermute | solution.py:396
  411.9 11.6 %collective-permute-done.31 = bf16[128,2048]{1,0:T(8,128)(2,1)S(1)} collective-permute-done((bf16[128,2048]{1,0:T(8,128)(2,1)S(1)}, bf16[128,2048]{1,0:T(8,128)(2,1)S(1)}, u32[]{:S(2)}, u32[]{:S(2)}) %collective-permute-start.31) | collective-permute-done | bytes 524320 | tf_op jit(solution)/shard_map/ppermute | solution.py:396
  428.6 11.4 %collective-permute-done.33 = bf16[128,2048]{1,0:T(8,128)(2,1)S(1)} collective-permute-done((bf16[128,2048]{1,0:T(8,128)(2,1)S(1)}, bf16[128,2048]{1,0:T(8,128)(2,1)S(1)}, u32[]{:S(2)}, u32[]{:S(2)}) %collective-permute-start.33) | collective-permute-done | bytes 524320 | tf_op jit(solution)/shard_map/ppermute | solution.py:396
  476.7 35.6 %collective-permute-done.37 = f32[4,128,256]{2,1,0:T(8,128)S(1)} collective-permute-done((f32[4,128,256]{2,1,0:T(8,128)S(1)}, f32[4,128,256]{2,1,0:T(8,128)S(1)}, u32[]{:S(2)}, u32[]{:S(2)}) %collective-permute-start.37) | collective-permute-done | bytes 524320 | tf_op jit(solution)/shard_map/ppermute | solution.py:382
  514.2 38.2 %collective-permute-done.38 = f32[4,128,256]{2,1,0:T(8,128)S(1)} collective-permute-done((f32[4,128,256]{2,1,0:T(8,128)S(1)}, f32[4,128,256]{2,1,0:T(8,128)S(1)}, u32[]{:S(2)}, u32[]{:S(2)}) %collective-permute-start.38) | collective-permute-done | bytes 524320 | tf_op jit(solution)/shard_map/ppermute | solution.py:382
  554.4 27.3 %collective-permute-done.39.later_ref = f32[4,128,256]{2,1,0:T(8,128)S(1)} collective-permute-done((f32[4,128,256]{2,1,0:T(8,128)S(1)}, f32[4,128,256]{2,1,0:T(8,128)S(1)}, u32[]{:S(2)}, u32[]{:S(2)}) %collective-permute-start.39) | collective-permute-done | bytes 524320 | tf_op jit(solution)/shard_map/ppermute | solution.py:382
  581.7 32.5 %shard_map.422 = (bf16[1024,1024]{1,0:T(8,128)(2,1)}, f32[2,8,1024]{2,1,0:T(8,128)S(1)}, f32[2,8,1024]{2,1,0:T(8,128)S(1)}, f32[4,4,512]{2,1,0:T(4,128)S(1)}, f32[4,512,8]{2,1,0:T(8,128)S(1)}) custom-call(f32[1024,1024]{1,0:T(8,128)} %copy-done.104, f32[2,8,1024]{2,1,0:T(8,128)S(1)} %collective-permute-done.5.halo_ref, f32[4,1024]{1,0:T(4,128)S(1)} %bitcast.480, ...), custom_call_target="tpu_custom_call" | custom-call | flops 8053063680 | bytes 33980416 | tf_op jit(solution)/shard_map/pallas_call | solution.py:365
  655.6 10.8 %convolution_convert_fusion = bf16[2048,1408]{0,1:T(8,128)(2,1)S(1)} fusion(bf16[1024,2048]{1,0:T(8,128)(2,1)} %constant_dynamic-update-slice_fusion, bf16[1024,704]{1,0:T(8,128)(2,1)} %copy-done.115, bf16[1024,704]{1,0:T(8,128)(2,1)} %copy-done.114), kind=kOutput, calls=%fused_computation.2 | convolution fusion | flops 5914230784 | bytes 12845056 | tf_op jit(solution)/shard_map/dot_general | solution.py:28
  682.3 11.2 %collective-permute-done.21 = bf16[128,2048]{1,0:T(8,128)(2,1)S(1)} collective-permute-done((bf16[128,2048]{1,0:T(8,128)(2,1)S(1)}, bf16[128,2048]{1,0:T(8,128)(2,1)S(1)}, u32[]{:S(2)}, u32[]{:S(2)}) %collective-permute-start.21) | collective-permute-done | bytes 524320 | tf_op jit(solution)/shard_map/ppermute | solution.py:396
  787.7 16.0 %all-to-all-done.1 = f32[8,1,2048]{2,1,0:T(1,128)S(1)} async-done(((f32[8,1,2048]{2,1,0:T(1,128)}), f32[8,1,2048]{2,1,0:T(1,128)S(1)}, u32[]{:S(2)}, u32[]{:S(2)}) %all-to-all-start.1) | async-done | bytes 65568 | tf_op jit(solution)/shard_map/all_to_all | solution.py:852
  836.0 19.6 %collective-permute-done.53 = f32[37152]{0:T(1024)S(1)} collective-permute-done((f32[37152]{0:T(1024)S(1)}, f32[37152]{0:T(1024)S(1)}, u32[]{:S(2)}, u32[]{:S(2)}) %collective-permute-start.53) | collective-permute-done | bytes 148640 | tf_op jit(solution)/shard_map/ppermute | solution.py:386
  943.3 13.1 %collective-permute-done.54 = bf16[256,2112]{0,1:T(8,128)(2,1)S(1)} collective-permute-done((bf16[256,2112]{0,1:T(8,128)(2,1)S(1)}, bf16[256,2112]{0,1:T(8,128)(2,1)S(1)}, u32[]{:S(2)}, u32[]{:S(2)}) %collective-permute-start.54) | collective-permute-done | bytes 1081376 | tf_op jit(solution)/shard_map/ppermute | solution.py:386
  (629 shorter events, 564.4 us)
Async XLA Ops:
  7.2 103.4 %all-gather.4.cloned.1.call-start = ((), (), s32[]{:S(2)}) async-start(), calls=%async_computation.5 | async-start | bytes 5242880 | tf_op jit(solution)/shard_map/all_gather | solution.py:582
  27.5 190.5 %all-gather.6.cloned.1.call-start = ((), (), s32[]{:S(2)}) async-start(), calls=%async_computation.6 | async-start | bytes 5242880 | tf_op jit(solution)/shard_map/all_gather | solution.py:582
  57.6 310.6 %all-gather.8.cloned.1.call-start = ((), (), s32[]{:S(2)}) async-start(), calls=%async_computation.7 | async-start | bytes 10813440 | tf_op jit(solution)/shard_map/all_gather | solution.py:582
  67.1 26.7 %collective-permute-start.18 = (bf16[256,2112]{0,1:T(8,128)(2,1)}, bf16[256,2112]{0,1:T(8,128)(2,1)}, u32[]{:S(2)}, u32[]{:S(2)}) collective-permute-start(bf16[256,2112]{0,1:T(8,128)(2,1)} %broadcast_select_fusion.4), channel_id=1, source_target_pairs={{0,16},{16,0},{1,17},{17,1},{2,18},{18,2},{3,19},{19,3},{4,20},{20... | collective-permute-start | bytes 3244040 | tf_op jit(solution)/shard_map/ppermute | solution.py:386
  97.6 780.0 %reduce-scatter.6.cloned.1.call-start = ((), (), s32[]{:S(2)}) async-start(), calls=%async_computation.9 | async-start | bytes 5242880 | tf_op jit(solution)/shard_map/reduce_scatter | solution.py:795
  154.9 26.2 %collective-permute-start.6 = (f32[4,128,256]{2,1,0:T(8,128)S(1)}, f32[4,128,256]{2,1,0:T(8,128)S(1)}, u32[]{:S(2)}, u32[]{:S(2)}) collective-permute-start(f32[4,128,256]{2,1,0:T(8,128)S(1)} %slice.287), channel_id=1, source_target_pairs={{0,4},{4,8},{8,12},{1,5},{5,9},{9,13},{2,6},{6,10},{10,14},{3,7},{... | collective-permute-start | bytes 1572872 | tf_op jit(solution)/shard_map/ppermute | solution.py:382
  181.7 29.6 %collective-permute-start.7 = (f32[4,128,256]{2,1,0:T(8,128)S(1)}, f32[4,128,256]{2,1,0:T(8,128)S(1)}, u32[]{:S(2)}, u32[]{:S(2)}) collective-permute-start(f32[4,128,256]{2,1,0:T(8,128)S(1)} %convolution_add_fusion.3), channel_id=1, source_target_pairs={{0,4},{4,8},{8,12},{1,5},{5,9},{9,13},{2,6},{6,10},{10,14},{3,7},{... | collective-permute-start | bytes 1572872 | tf_op jit(solution)/shard_map/ppermute | solution.py:382
  212.7 26.0 %collective-permute-start.8 = (f32[4,128,256]{2,1,0:T(8,128)}, f32[4,128,256]{2,1,0:T(8,128)}, u32[]{:S(2)}, u32[]{:S(2)}) collective-permute-start(f32[4,128,256]{2,1,0:T(8,128)} %convolution_add_fusion.2), channel_id=1, source_target_pairs={{0,4},{4,8},{8,12},{1,5},{5,9},{9,13},{2,6},{6,10},{10,14},{3,7},{... | collective-permute-start | bytes 1572872 | tf_op jit(solution)/shard_map/ppermute | solution.py:382
  259.6 26.0 %collective-permute-start.26 = (bf16[128,2048]{1,0:T(8,128)(2,1)S(1)}, bf16[128,2048]{1,0:T(8,128)(2,1)S(1)}, u32[]{:S(2)}, u32[]{:S(2)}) collective-permute-start(bf16[128,2048]{1,0:T(8,128)(2,1)S(1)} %get-tuple-element.295), channel_id=1, source_target_pairs={{0,16},{1,17},{2,18},{3,19},{16,0},{17,1},{18,2},{19,3},{4,20},{5,... | collective-permute-start | bytes 1572872 | tf_op jit(solution)/shard_map/ppermute | solution.py:396
  266.5 29.2 %collective-permute-start.11 = (bf16[128,2048]{1,0:T(8,128)(2,1)S(1)}, bf16[128,2048]{1,0:T(8,128)(2,1)S(1)}, u32[]{:S(2)}, u32[]{:S(2)}) collective-permute-start(bf16[128,2048]{1,0:T(8,128)(2,1)S(1)} %get-tuple-element.354), channel_id=1, source_target_pairs={{0,2},{1,3},{2,0},{3,1},{16,18},{17,19},{18,16},{19,17},{4,6},{5,7... | collective-permute-start | bytes 1572872 | tf_op jit(solution)/shard_map/ppermute | solution.py:396
  267.7 39.7 %collective-permute-start.12 = (bf16[128,2048]{1,0:T(8,128)(2,1)S(1)}, bf16[128,2048]{1,0:T(8,128)(2,1)S(1)}, u32[]{:S(2)}, u32[]{:S(2)}) collective-permute-start(bf16[128,2048]{1,0:T(8,128)(2,1)S(1)} %get-tuple-element.356), channel_id=1, source_target_pairs={{0,16},{1,17},{2,18},{3,19},{16,0},{17,1},{18,2},{19,3},{4,20},{5,... | collective-permute-start | bytes 1572872 | tf_op jit(solution)/shard_map/ppermute | solution.py:396
  273.2 34.2 %collective-permute-start.13 = (bf16[128,2048]{1,0:T(8,128)(2,1)S(1)}, bf16[128,2048]{1,0:T(8,128)(2,1)S(1)}, u32[]{:S(2)}, u32[]{:S(2)}) collective-permute-start(bf16[128,2048]{1,0:T(8,128)(2,1)S(1)} %get-tuple-element.355), channel_id=1, source_target_pairs={{0,18},{1,19},{2,16},{3,17},{16,2},{17,3},{18,0},{19,1},{4,22},{5,... | collective-permute-start | bytes 1572872 | tf_op jit(solution)/shard_map/ppermute | solution.py:396
  285.7 49.7 %collective-permute-start.28 = (bf16[512,2048]{1,0:T(8,128)(2,1)S(1)}, bf16[512,2048]{1,0:T(8,128)(2,1)S(1)}, u32[]{:S(2)}, u32[]{:S(2)}) collective-permute-start(bf16[512,2048]{1,0:T(8,128)(2,1)S(1)} %pad_maximum_fusion.14), channel_id=1, source_target_pairs={{0,1},{1,0},{2,3},{3,2},{4,5},{5,4},{6,7},{7,6},{8,9},{9,8},{10,11... | collective-permute-start | bytes 6291464 | tf_op jit(solution)/shard_map/ppermute | solution.py:386
  474.6 427.1 %reduce-scatter.4.cloned.1.call-start = ((), (), s32[]{:S(2)}) async-start(), calls=%async_computation.8 | async-start | bytes 5242880 | tf_op jit(solution)/shard_map/reduce_scatter | solution.py:795
  474.7 37.6 %collective-permute-start.37 = (f32[4,128,256]{2,1,0:T(8,128)S(1)}, f32[4,128,256]{2,1,0:T(8,128)S(1)}, u32[]{:S(2)}, u32[]{:S(2)}) collective-permute-start(f32[4,128,256]{2,1,0:T(8,128)S(1)} %get-tuple-element.56), channel_id=1, source_target_pairs={{4,0},{8,4},{12,8},{5,1},{9,5},{13,9},{6,2},{10,6},{14,10},{7,3},{... | collective-permute-start | bytes 1572872 | tf_op jit(solution)/shard_map/ppermute | solution.py:382
  512.9 39.5 %collective-permute-start.38 = (f32[4,128,256]{2,1,0:T(8,128)S(1)}, f32[4,128,256]{2,1,0:T(8,128)S(1)}, u32[]{:S(2)}, u32[]{:S(2)}) collective-permute-start(f32[4,128,256]{2,1,0:T(8,128)S(1)} %convolution_add_fusion.1), channel_id=1, source_target_pairs={{4,0},{8,4},{12,8},{5,1},{9,5},{13,9},{6,2},{10,6},{14,10},{7,3},{... | collective-permute-start | bytes 1572872 | tf_op jit(solution)/shard_map/ppermute | solution.py:382
  553.1 28.6 %collective-permute-start.39 = (f32[4,128,256]{2,1,0:T(8,128)S(1)}, f32[4,128,256]{2,1,0:T(8,128)S(1)}, u32[]{:S(2)}, u32[]{:S(2)}) collective-permute-start(f32[4,128,256]{2,1,0:T(8,128)S(1)} %convolution_add_fusion), channel_id=1, source_target_pairs={{4,0},{8,4},{12,8},{5,1},{9,5},{13,9},{6,2},{10,6},{14,10},{7,3},{... | collective-permute-start | bytes 1572872 | tf_op jit(solution)/shard_map/ppermute | solution.py:382
  628.6 301.6 %reduce-scatter.8.cloned.1.call-start = ((), (), s32[]{:S(2)}) async-start(), calls=%async_computation.10 | async-start | bytes 10813440 | tf_op jit(solution)/shard_map/reduce_scatter | solution.py:795
  639.3 27.1 %collective-permute-start.19 = (bf16[512,2048]{1,0:T(8,128)(2,1)}, bf16[512,2048]{1,0:T(8,128)(2,1)S(1)}, u32[]{:S(2)}, u32[]{:S(2)}) collective-permute-start(bf16[512,2048]{1,0:T(8,128)(2,1)} %slice.393), channel_id=1, source_target_pairs={{0,1},{1,0},{2,3},{3,2},{4,5},{5,4},{6,7},{7,6},{8,9},{9,8},{10,11... | collective-permute-start | bytes 6291464 | tf_op jit(solution)/shard_map/ppermute | solution.py:386
  711.1 26.8 %collective-permute-start.24 = (bf16[2,128,2048]{2,1,0:T(8,128)(2,1)S(1)}, bf16[2,128,2048]{2,1,0:T(8,128)(2,1)}, u32[]{:S(2)}, u32[]{:S(2)}) collective-permute-start(bf16[2,128,2048]{2,1,0:T(8,128)(2,1)S(1)} %bitcast_dynamic-update-slice_fusion.6), channel_id=1, source_target_pairs={{0,1},{1,0},{2,3},{3,2},{4,5},{5,4},{6,7},{7,6},{8,9},{9,8},{10,11... | collective-permute-start | bytes 3145736 | tf_op jit(solution)/shard_map/ppermute | solution.py:386
  737.3 34.1 %collective-permute-start.41 = (bf16[4,128,2048]{2,1,0:T(8,128)(2,1)}, bf16[4,128,2048]{2,1,0:T(8,128)(2,1)}, u32[]{:S(2)}, u32[]{:S(2)}) collective-permute-start(bf16[4,128,2048]{2,1,0:T(8,128)(2,1)} %select_bitcast_fusion), channel_id=1, source_target_pairs={{0,1},{1,0},{2,3},{3,2},{4,5},{5,4},{6,7},{7,6},{8,9},{9,8},{10,11... | collective-permute-start | bytes 6291464 | tf_op jit(solution)/shard_map/ppermute | solution.py:386
  777.5 28.0 %collective-permute-start.42 = (bf16[128,2048]{1,0:T(8,128)(2,1)}, bf16[128,2048]{1,0:T(8,128)(2,1)}, u32[]{:S(2)}, u32[]{:S(2)}) collective-permute-start(bf16[128,2048]{1,0:T(8,128)(2,1)} %get-tuple-element.343), channel_id=1, source_target_pairs={{0,2},{1,3},{2,0},{3,1},{16,18},{17,19},{18,16},{19,17},{4,6},{5,7... | collective-permute-start | bytes 1572872 | tf_op jit(solution)/shard_map/ppermute | solution.py:396
  778.2 27.2 %collective-permute-start.43 = (bf16[128,2048]{1,0:T(8,128)(2,1)S(1)}, bf16[128,2048]{1,0:T(8,128)(2,1)}, u32[]{:S(2)}, u32[]{:S(2)}) collective-permute-start(bf16[128,2048]{1,0:T(8,128)(2,1)S(1)} %get-tuple-element.345), channel_id=1, source_target_pairs={{0,16},{1,17},{2,18},{3,19},{16,0},{17,1},{18,2},{19,3},{4,20},{5,... | collective-permute-start | bytes 1572872 | tf_op jit(solution)/shard_map/ppermute | solution.py:396
  779.2 26.3 %collective-permute-start.44 = (bf16[128,2048]{1,0:T(8,128)(2,1)S(1)}, bf16[128,2048]{1,0:T(8,128)(2,1)}, u32[]{:S(2)}, u32[]{:S(2)}) collective-permute-start(bf16[128,2048]{1,0:T(8,128)(2,1)S(1)} %get-tuple-element.344), channel_id=1, source_target_pairs={{0,18},{1,19},{2,16},{3,17},{16,2},{17,3},{18,0},{19,1},{4,22},{5,... | collective-permute-start | bytes 1572872 | tf_op jit(solution)/shard_map/ppermute | solution.py:396
  (157 other events, 2692.7 us)
Sparse Core Ops, SparseCore 0:
  27.7 82.8 all-gather.3
  112.7 94.2 all-gather.5
  209.2 158.9 all-gather.7
  474.7 106.2 reduce-scatter.5
  628.8 74.7 reduce-scatter.3
  705.8 156.5 reduce-scatter.7

commit v3 on v2

--- a/solution.py
+++ b/solution.py
@@ -4,6 +4,7 @@
 import jax.numpy as jnp
 from jax import lax
 from jax.experimental import pallas as pl
+from jax.experimental.layout import Layout, with_layout_constraint
 from jax.experimental.pallas import tpu as pltpu
 from jax.sharding import PartitionSpec as P
 
@@ -467,6 +468,10 @@
     return ordered(here, core, swapped(here, "tensor", 1))
 
 
+def after(value, tokens):
+    return lax.optimization_barrier((value, tokens))[0]
+
+
 def butterfly_sum(array):
     for axis in ("tensor", "dp", "seq"):
         distance = 1
@@ -486,11 +491,13 @@
 
 def adam_update(weight, gradient, moments, token_count):
     mean_grad = gradient / token_count
+    is_first = lax.broadcasted_iota(jnp.int32, moments.shape, 0) == 0
+    moved = 0.5 * moments + 0.5 * jnp.where(is_first, mean_grad, mean_grad * mean_grad)
     first = 0.5 * moments[0] + 0.5 * mean_grad
     second = 0.5 * moments[1] + 0.5 * mean_grad * mean_grad
     correction = 1.0 - 0.5**ADAM_STEP
     change = first / correction / (jnp.sqrt(second / correction) + 1e-08) + 0.1 * weight
-    return (weight - 0.1 * change, jnp.stack([first, second]))
+    return (weight - 0.1 * change, moved)
 
 
 def norm_parts(rows):
@@ -538,13 +545,14 @@
     first_part = lax.axis_index("dp") == 0
     first_head = lax.axis_index("tensor") * heads_stored + lax.axis_index("dp") * heads
 
+    def blocks_of(array, order):
+        return jnp.concatenate([array[..., i * depth : (i + 1) * depth] for i in order], axis=-1)
+
     def turned(array):
-        cut = array.reshape(array.shape[:-1] + (dp_size, seq_size, depth))
-        return jnp.swapaxes(cut, -3, -2).reshape(array.shape)
+        return blocks_of(array, [d * seq_size + q for q in range(seq_size) for d in range(dp_size)])
 
     def turned_back(array):
-        cut = array.reshape(array.shape[:-1] + (seq_size, dp_size, depth))
-        return jnp.swapaxes(cut, -3, -2).reshape(array.shape)
+        return blocks_of(array, [q * dp_size + d for d in range(dp_size) for q in range(seq_size)])
 
     def mine_and_theirs(low, high):
         return jnp.where(first_part, low, high), jnp.where(first_part, high, low)
@@ -569,9 +577,8 @@
                 ],
                 axis=1,
             ),
-            jnp.concatenate(
-                [low_swiglu[:, 0, some], low_swiglu[:, 1, some], low_down[:, some]], axis=1
-            ),
+            jnp.concatenate([low_swiglu[:, 0, some], low_swiglu[:, 1, some]], axis=1),
+            low_down[:, some],
         )
 
     gathered = []
@@ -580,9 +587,8 @@
         received = swapped(theirs, "dp", 1)
         shard = jnp.concatenate(by_device(mine, received), axis=0)
         gathered.append(lax.all_gather(shard, "seq", axis=0, tiled=True))
-    full_qkv, full_mixer, full_ffn = gathered
+    full_qkv, full_mixer, full_swiglu, full_down = gathered
     full_gate, full_output = full_mixer[:, : heads * DV], full_mixer[:, heads * DV :]
-    full_swiglu, full_down = full_ffn[:, : 2 * units], full_ffn[:, 2 * units :]
 
     copies = dp_size * seq_size
     rates_low = jnp.broadcast_to(w_rates.astype(BF16).reshape(1, -1), (copies, depth * heads_stored * 2))
@@ -597,7 +603,6 @@
     gains = turned(w_gains)
     factor_in, normal_in = norm_parts(stream_rows)
     normed_in = gather_absolute((normal_in * gains[0]).astype(BF16)).reshape(-1, width)
-    grad_ffn = gather_relative(cotangent_rows.astype(BF16))
 
     projected = dot(normed_in, full_qkv, NN)
     rates = dot(normed_in, full_rates, NN)
@@ -653,8 +658,9 @@
         moved = offset_map
         if hop > 0:
             moved = moved + jnp.einsum("bkj,bjw->bkw", linear_map, incoming, precision=HIGHEST)
-        incoming = shifted(moved, "seq", 1)
-    gate_raw = dot(normed_in, full_gate, NN)
+        incoming = shifted(moved.astype(BF16), "seq", 1).astype(F32)
+    grad_ffn = gather_relative(after(cotangent_rows.astype(BF16), end))
+    gate_raw = dot(after(normed_in, grad_ffn), full_gate, NN)
     scale_row = w_scale.reshape(1, DV)
     (mixed,) = call(
         finish_kernel,
@@ -678,25 +684,21 @@
     gate_part, up_part = gate_up[:, :units], gate_up[:, units:]
     sigmoid_gate = jax.nn.sigmoid(gate_part)
     silu_gate = gate_part * sigmoid_gate
-    activated = (silu_gate * up_part).astype(BF16)
-    grad_activated = dot(grad_ffn, full_down, NN)
+    activated = after((silu_gate * up_part).astype(BF16), full_down)
+    grad_down_weights = contract_rows(grad_ffn, activated).astype(BF16)
+    down_sum = lax.psum_scatter(grad_down_weights, "seq", scatter_dimension=0, tiled=True)
+    grad_activated = dot(after(grad_ffn, grad_down_weights), full_down, NN)
     grad_gate = grad_activated * up_part * sigmoid_gate * (1.0 + gate_part * (1.0 - sigmoid_gate))
     grad_up = grad_activated * silu_gate
     grad_gate_up = jnp.concatenate([grad_gate.astype(BF16), grad_up.astype(BF16)], axis=1)
-    grad_normed_mid = scatter_relative(contract_cols(grad_gate_up, full_swiglu).astype(BF16))
+    normed_mid_term = contract_cols(grad_gate_up, full_swiglu).astype(BF16)
+    grad_normed_mid = scatter_relative(normed_mid_term)
+    grad_swiglu_weights = contract_rows(after(normed_mid, normed_mid_term), grad_gate_up)
+    grad_swiglu_weights = after(grad_swiglu_weights.astype(BF16), grad_down_weights)
+    swiglu_sum = lax.psum_scatter(grad_swiglu_weights, "seq", scatter_dimension=0, tiled=True)
     from_mid, grad_gain_mid = norm_back(factor_mid, normal_mid, gains[1], grad_normed_mid)
+    from_mid = after(from_mid, grad_swiglu_weights)
     grad_attention = gather_absolute((cotangent_rows + from_mid).astype(BF16)).reshape(-1, width)
-    feedforward = scatter_relative(contract_cols(activated, full_down).astype(BF16))
-    grad_ffn_weights = jnp.concatenate(
-        [
-            contract_rows(normed_mid, grad_gate_up).astype(BF16),
-            contract_rows(grad_ffn, activated).astype(BF16),
-        ],
-        axis=1,
-    )
-    added = gather_absolute((attention + feedforward).astype(BF16), False).reshape(length, width)
-    result = stream + turned_back(added).astype(F32)
-
     grad_mixed = dot(grad_attention, full_output, NN)
     grad_mixer_out, grad_gate_raw, grad_scale, correction = call(
         finish_back_kernel,
@@ -722,7 +724,13 @@
         moved = correction
         if hop > 0:
             moved = moved + jnp.einsum("bjk,bjw->bkw", linear_map, later, precision=HIGHEST)
-        later = shifted(moved, "seq", -1)
+        later = shifted(moved.astype(BF16), "seq", -1)
+        if hop == 0:
+            feedforward = scatter_relative(
+                contract_cols(after(activated, later), full_down).astype(BF16)
+            )
+        later = later.astype(F32)
+    later = after(later, (swiglu_sum, feedforward))
     grad_mixer_weights = jnp.concatenate(
         [
             contract_rows(normed_in, grad_gate_raw).astype(BF16),
@@ -779,24 +787,93 @@
         ]
     )
     grad_qkv_weights = contract_rows(normed_in, grad_projected).astype(BF16)
-    grad_rates_weights = contract_rows(normed_in, grad_rates)
+    mixer_sum = lax.psum_scatter(
+        after(grad_mixer_weights, (swiglu_sum, down_sum)),
+        "seq",
+        scatter_dimension=0,
+        tiled=True,
+    )
+    qkv_sum = lax.psum_scatter(
+        after(grad_qkv_weights, swiglu_sum), "seq", scatter_dimension=0, tiled=True
+    )
+    grad_rates_weights = contract_rows(after(normed_in, grad_qkv_weights), grad_rates)
     normed_in_term = (
-        contract_cols(grad_projected, full_qkv)
+        contract_cols(after(grad_projected, (grad_qkv_weights, grad_rates_weights)), full_qkv)
         + contract_cols(grad_gate_raw, full_gate)
         + contract_cols(grad_rates, full_rates)
     )
     grad_normed_in = scatter_absolute(normed_in_term.astype(BF16))
     from_in, grad_gain_in = norm_back(factor_in, normal_in, gains[0], grad_normed_in)
-    changed = gather_absolute((from_mid + from_in).astype(BF16), False).reshape(length, width)
-    grad_stream = cotangent + turned_back(changed).astype(F32)
-
-    scattered = []
-    for full in (grad_ffn_weights, grad_mixer_weights, grad_qkv_weights):
-        part = lax.psum_scatter(full, "seq", scatter_dimension=0, tiled=True)
+    added = turned_back(jnp.concatenate([attention + feedforward, from_mid + from_in], axis=0))
+    added = gather_absolute(
+        jnp.concatenate([added[:rows], added[rows:]], axis=1).astype(BF16), False
+    ).reshape(length, 2 * width)
+    result = stream + added[:, :width].astype(F32)
+    grad_stream = cotangent + added[:, width:].astype(F32)
+
+    def exchanged(part):
         own, theirs = mine_and_theirs(part[:depth], part[depth:])
         received = swapped(theirs, "dp", 1)
-        scattered.append(tuple(a.astype(F32) for a in by_device(own, received)))
-    ffn_parts, mixer_parts, qkv_parts = scattered
+        return tuple(a.astype(F32) for a in by_device(own, received))
+
+    swiglu_parts, down_parts, mixer_parts = (
+        exchanged(part) for part in (swiglu_sum, down_sum, mixer_sum)
+    )
+    g_output = jnp.concatenate(
+        [m[:, heads * DV :].T.reshape(heads, DV, depth) for m in mixer_parts], axis=0
+    )
+    g_swiglu = jnp.stack(
+        [
+            jnp.concatenate([f[:, :units] for f in swiglu_parts], axis=1),
+            jnp.concatenate([f[:, units:] for f in swiglu_parts], axis=1),
+        ],
+        axis=1,
+    )
+    g_swiglu = with_layout_constraint(g_swiglu, Layout((0, 1, 2)))
+    g_down = jnp.concatenate([f.T for f in down_parts], axis=0)
+
+    conv_term = jnp.zeros_like(w_conv)
+    grad_taps = jnp.sum(grad_taps.reshape(dp_size, heads, KCONV, QKV), axis=0)
+    conv_term = lax.dynamic_update_slice_in_dim(
+        conv_term, jnp.swapaxes(grad_taps, 0, 1), first_head, 1
+    )
+    heads_term = lax.dynamic_update_slice_in_dim(
+        jnp.zeros_like(w_heads), grad_heads, first_head, 1
+    )
+    gains_term = turned_back(jnp.stack([grad_gain_in, grad_gain_mid]))
+    scale_term = jnp.sum(grad_scale[:, 0], axis=0)
+    rates_term = lax.dynamic_update_slice_in_dim(
+        jnp.zeros((dp_size, width, heads * 2), F32),
+        grad_rates_weights[None],
+        lax.axis_index("dp"),
+        0,
+    )
+    rates_term = jnp.transpose(rates_term, (1, 0, 2))
+    small = [conv_term, heads_term, gains_term, scale_term]
+    flat = jnp.concatenate([a.reshape(-1) for a in small])
+    flat = butterfly_sum(flat)
+    sums, at = [], 0
+    for a in small:
+        sums.append(flat[at : at + a.size].reshape(a.shape))
+        at += a.size
+    g_conv, g_heads, g_gains, g_scale = sums
+    rates_term = rates_term.reshape(seq_size, dp_size, depth, heads_stored * 2)
+    rates_term = jnp.swapaxes(rates_term, 0, 1).reshape(dp_size * seq_size, -1)
+    g_rates = jnp.sum(
+        lax.all_to_all(rates_term, ("dp", "seq"), 0, 0, tiled=True), axis=0
+    ).reshape(depth, heads_stored, 2)
+
+    tokens = float(length * dp_size * seq_size)
+    new_rates, moment_rates = adam_update(w_rates, g_rates, m_rates, tokens)
+    new_conv, moment_conv = adam_update(w_conv, g_conv, m_conv, tokens)
+    new_output, moment_output = adam_update(w_output, g_output, m_output, tokens)
+    new_swiglu, moment_swiglu = adam_update(w_swiglu, g_swiglu, m_swiglu, tokens)
+    new_down, moment_down = adam_update(w_down, g_down, m_down, tokens)
+    new_gains, moment_gains = adam_update(w_gains, g_gains, m_gains, tokens)
+    new_scale, moment_scale = adam_update(w_scale, g_scale, m_scale, tokens)
+    new_heads, moment_heads = adam_update(w_heads, g_heads, m_heads, tokens)
+    others = (result, grad_stream, g_conv, new_output, new_swiglu, new_down, new_rates)
+    qkv_parts = exchanged(after(qkv_sum, others))
     g_input = jnp.concatenate(
         [
             jnp.concatenate(
@@ -810,58 +887,7 @@
         ],
         axis=1,
     )
-    g_output = jnp.concatenate(
-        [m[:, heads * DV :].T.reshape(heads, DV, depth) for m in mixer_parts], axis=0
-    )
-    g_swiglu = jnp.stack(
-        [
-            jnp.concatenate([f[:, :units] for f in ffn_parts], axis=1),
-            jnp.concatenate([f[:, units : 2 * units] for f in ffn_parts], axis=1),
-        ],
-        axis=1,
-    )
-    g_down = jnp.concatenate([f[:, 2 * units :].T for f in ffn_parts], axis=0)
-
-    conv_term = jnp.zeros_like(w_conv)
-    grad_taps = jnp.sum(grad_taps.reshape(dp_size, heads, KCONV, QKV), axis=0)
-    conv_term = lax.dynamic_update_slice_in_dim(
-        conv_term, jnp.swapaxes(grad_taps, 0, 1), first_head, 1
-    )
-    heads_term = lax.dynamic_update_slice_in_dim(
-        jnp.zeros_like(w_heads), grad_heads, first_head, 1
-    )
-    gains_term = turned_back(jnp.stack([grad_gain_in, grad_gain_mid]))
-    scale_term = jnp.sum(grad_scale[:, 0], axis=0)
-    rates_term = lax.dynamic_update_slice_in_dim(
-        jnp.zeros((dp_size, width, heads * 2), F32),
-        grad_rates_weights[None],
-        lax.axis_index("dp"),
-        0,
-    )
-    rates_term = jnp.transpose(rates_term, (1, 0, 2))
-    small = [conv_term, heads_term, gains_term, scale_term]
-    flat = butterfly_sum(jnp.concatenate([a.reshape(-1) for a in small]))
-    sums, at = [], 0
-    for a in small:
-        sums.append(flat[at : at + a.size].reshape(a.shape))
-        at += a.size
-    g_conv, g_heads, g_gains, g_scale = sums
-    rates_term = rates_term.reshape(seq_size, dp_size, depth, heads_stored * 2)
-    rates_term = jnp.swapaxes(rates_term, 0, 1).reshape(dp_size * seq_size, -1)
-    g_rates = jnp.sum(
-        lax.all_to_all(rates_term, ("dp", "seq"), 0, 0, tiled=True), axis=0
-    ).reshape(depth, heads_stored, 2)
-
-    tokens = float(length * dp_size * seq_size)
     new_input, moment_input = adam_update(w_input, g_input, m_input, tokens)
-    new_rates, moment_rates = adam_update(w_rates, g_rates, m_rates, tokens)
-    new_conv, moment_conv = adam_update(w_conv, g_conv, m_conv, tokens)
-    new_output, moment_output = adam_update(w_output, g_output, m_output, tokens)
-    new_swiglu, moment_swiglu = adam_update(w_swiglu, g_swiglu, m_swiglu, tokens)
-    new_down, moment_down = adam_update(w_down, g_down, m_down, tokens)
-    new_gains, moment_gains = adam_update(w_gains, g_gains, m_gains, tokens)
-    new_scale, moment_scale = adam_update(w_scale, g_scale, m_scale, tokens)
-    new_heads, moment_heads = adam_update(w_heads, g_heads, m_heads, tokens)
     return (
         result,
         grad_stream,

time: 1020 us -> 842 us (0.83)
  waiting for transfers between devices: 432 us -> 299 us
  local copies, waits for them, and re-layouts: 172 us -> 116 us
  other arithmetic: 126 us -> 144 us
    ppermute x8, waiting for transfers between devices: 161 us -> 37.7 us  [shifted(): return lax.ppermute(block, axis, route)]
    unnamed x269 -> x303, local copies, waits for them, and re-layouts: 84.4 us -> 51.7 us
    convert_element_type x6 -> x0, local copies, waits for them, and re-layouts: 30.1 us -> none  [the longest x3 16.1 us: body(): result = stream + turned_back(added).astype(F32)]
    all_gather x3 -> x4, waiting for transfers between devices: 33.6 us -> 62 us  [body(): gathered.append(lax.all_gather(shard, 'seq', axis=0, tiled=True))]
    mul x1 -> x8, other arithmetic: 0.57 us -> 25 us  [the longest x5 24.1 us: adam_update(): mean_grad * mean_grad]
    sub x8 -> x0, other arithmetic: 23.4 us -> none  [adam_update(): return (weight - 0.1 * change, jnp.stack([first, second]))]
    ppermute x21 -> x22, waiting for transfers between devices: 91.9 us -> 72.3 us  [swapped(): lax.ppermute(block, axis, [(i, i ^ bits) for i in range(lax.axis_size(axi...]
    another operation x13 -> x1, other arithmetic: 17.6 us -> 0.27 us  [body(): jnp.stack([jnp.concatenate([f[:, :units] for f in swiglu_parts], axis=1),...]
  transfers between devices with their start and end apart: 63 -> 65, of which waited for: 37 -> 35; matrix products, arithmetic and copies ran while one was open for 30% -> 39% of each run, Pallas kernels for 6% -> 8%
where the time goes in v3:
time: 842 us; the launch traced here: 833 us
  waiting for transfers between devices  299 us (36%)
  other arithmetic  144 us (17%)
  local copies, waits for them, and re-layouts  116 us (14%)
  matrix products  115 us (14%)
  starting transfers between devices  75.4 us (9%)
  Pallas kernels  67.9 us (8%)
  between operations  16.6 us (2%)
    ppermute x25, waiting for transfers between devices, group_swapped(): return lax.ppermute(block, ('dp', 'tensor'), route)  126 us
    dot_general x18, matrix products, dot(): return lax.dot_general(left, right, dims, preferred_element_type=F32)  112 us
    ppermute x22, waiting for transfers between devices, swapped(): lax.ppermute(block, axis, [(i, i ^ bits) for i in range(lax.axis_size(axi...  72.3 us
    pallas_call x4, Pallas kernels, chains_call(): pl.pallas_call(kernel, grid=(chains,), in_specs=[spec(tag, a.shape) for t...  67.9 us
    all_gather x4, waiting for transfers between devices, body(): gathered.append(lax.all_gather(shard, 'seq', axis=0, tiled=True))  62 us
    unnamed x303, local copies, waits for them, and re-layouts  51.7 us
    ppermute x8, waiting for transfers between devices, shifted(): return lax.ppermute(block, axis, route)  37.7 us
    ppermute x25, starting transfers between devices, group_swapped(): return lax.ppermute(block, ('dp', 'tensor'), route)  29.2 us
  transfers between devices with their start and end apart: 65, of which 35 were waited for; matrix products, arithmetic and copies ran while one was open for 39% of the time, Pallas kernels for 8%

profile of v3, /device:TPU:0, one launch (start us, length us, event | category | flops | bytes accessed | tf_op | source)
XLA Modules:
  0.0 833.0 jit_solution(5544961056512976450)
XLA Ops:
  93.5 18.4 %all-gather.5.cloned.1.call-done = bf16[2048,1024]{1,0:T(8,128)(2,1)} async-done(((bf16[512,1024]{1,0:T(8,128)(2,1)}), bf16[2048,1024]{1,0:T(8,128)(2,1)}) %all-gather.5.cloned.1.call-update) | async-done | bytes 4194320 | tf_op jit(solution)/shard_map/all_gather | solution.py:589
  130.4 25.0 %shard_map.419 = (f32[4,512,128]{2,1,0:T(8,128)S(1)}, f32[4,512,256]{2,1,0:T(8,128)}, f32[4,128,384]{2,1,0:T(8,128)S(1)}, f32[4,4,128,384]{3,2,1,0:T(8,128)}, f3...) custom-call(f32[1024,1024]{1,0:T(8,128)} %copy-done.115, ...), custom_call_target="tpu_custom_call" | custom-call | flops 6039797760 | bytes 8814592 | tf_op jit(solution)/shard_map/pallas_call | solution.py:366
  164.6 17.1 %collective-permute-done.10 = bf16[128,2048]{1,0:T(8,128)(2,1)S(1)} collective-permute-done((bf16[128,2048]{1,0:T(8,128)(2,1)S(1)}, bf16[128,2048]{1,0:T(8,128)(2,1)S(1)}, u32[]{:S(2)}, u32[]{:S(2)}) %collective-permute-start.10) | collective-permute-done | bytes 524320 | tf_op jit(solution)/shard_map/ppermute | solution.py:397
  183.5 12.5 %collective-permute-done.22 = bf16[256,1408]{1,0:T(8,128)(2,1)S(1)} collective-permute-done((bf16[256,1408]{1,0:T(8,128)(2,1)S(1)}, bf16[256,1408]{1,0:T(8,128)(2,1)S(1)}, u32[]{:S(2)}, u32[]{:S(2)}) %collective-permute-start.22) | collective-permute-done | bytes 720928 | tf_op jit(solution)/shard_map/ppermute | solution.py:387
  244.9 11.3 %collective-permute-done.15 = bf16[128,2048]{1,0:T(8,128)(2,1)S(1)} collective-permute-done((bf16[128,2048]{1,0:T(8,128)(2,1)S(1)}, bf16[128,2048]{1,0:T(8,128)(2,1)S(1)}, u32[]{:S(2)}, u32[]{:S(2)}) %collective-permute-start.15) | collective-permute-done | bytes 524320 | tf_op jit(solution)/shard_map/ppermute | solution.py:397
  256.1 10.8 %collective-permute-done.16 = bf16[128,2048]{1,0:T(8,128)(2,1)S(1)} collective-permute-done((bf16[128,2048]{1,0:T(8,128)(2,1)S(1)}, bf16[128,2048]{1,0:T(8,128)(2,1)S(1)}, u32[]{:S(2)}, u32[]{:S(2)}) %collective-permute-start.16) | collective-permute-done | bytes 524320 | tf_op jit(solution)/shard_map/ppermute | solution.py:397
  272.8 11.3 %collective-permute-done.18 = bf16[128,2048]{1,0:T(8,128)(2,1)S(1)} collective-permute-done((bf16[128,2048]{1,0:T(8,128)(2,1)S(1)}, bf16[128,2048]{1,0:T(8,128)(2,1)S(1)}, u32[]{:S(2)}, u32[]{:S(2)}) %collective-permute-start.18) | collective-permute-done | bytes 524320 | tf_op jit(solution)/shard_map/ppermute | solution.py:397
  284.1 10.8 %collective-permute-done.19 = bf16[128,2048]{1,0:T(8,128)(2,1)S(1)} collective-permute-done((bf16[128,2048]{1,0:T(8,128)(2,1)S(1)}, bf16[128,2048]{1,0:T(8,128)(2,1)S(1)}, u32[]{:S(2)}, u32[]{:S(2)}) %collective-permute-start.19) | collective-permute-done | bytes 524320 | tf_op jit(solution)/shard_map/ppermute | solution.py:397
  296.8 10.5 %collective-permute-done.23 = bf16[256,704]{0,1:T(8,128)(2,1)S(1)} collective-permute-done((bf16[256,704]{0,1:T(8,128)(2,1)S(1)}, bf16[256,704]{0,1:T(8,128)(2,1)S(1)}, u32[]{:S(2)}, u32[]{:S(2)}) %collective-permute-start.23) | collective-permute-done | bytes 360480 | tf_op jit(solution)/shard_map/ppermute | solution.py:387
  315.6 10.5 %fusion.175 = f32[1024,1408]{1,0:T(8,128)S(1)} fusion(bf16[1024,2048]{1,0:T(8,128)(2,1)} %constant_dynamic-update-slice_fusion.13, bf16[2048,1408]{1,0:T(8,128)(2,1)} %all-gather.9.cloned.1.call-done), kind=kOutput, calls=%fused_computation.454 | convolution fusion | flops 5905580032 | bytes 15728640 | tf_op jit(solution)/shard_map/dot_general | solution.py:29
  331.0 43.6 %all-gather.11.cloned.1.call-done = bf16[2048,704]{0,1:T(8,128)(2,1)} async-done(((bf16[512,704]{0,1:T(8,128)(2,1)}), bf16[2048,704]{0,1:T(8,128)(2,1)}) %all-gather.11.cloned.1.call-update) | async-done | bytes 2883600 | tf_op jit(solution)/shard_map/all_gather | solution.py:589
  382.4 9.3 %multiply_convert_fusion.1 = (bf16[1024,704]{1,0:T(8,128)(2,1)S(1)}, bf16[1024,704]{1,0:T(8,128)(2,1)S(1)}) fusion(f32[1024,1408]{1,0:T(8,128)} %copy-done.39, bf16[1024,2048]{1,0:T(8,128)(2,1)} %constant_dynamic-update-slice_fusion.8, bf16[2048,704]{0,1:T(8,128)(2,1)} %all-gather.11.cloned.1.call-done), kind=kOutput, calls=%fused_computation.44 | convolution fusion | flops 2962161664 | bytes 15728640 | tf_op jit(solution)/shard_map/dot_general | solution.py:29
  423.8 10.1 %collective-permute-done.26 = bf16[128,2048]{1,0:T(8,128)(2,1)} collective-permute-done((bf16[128,2048]{1,0:T(8,128)(2,1)S(1)}, bf16[128,2048]{1,0:T(8,128)(2,1)}, u32[]{:S(2)}, u32[]{:S(2)}) %collective-permute-start.26) | collective-permute-done | bytes 524320 | tf_op jit(solution)/shard_map/ppermute | solution.py:397
  444.9 11.4 %collective-permute-done.28 = bf16[128,2048]{1,0:T(8,128)(2,1)S(1)} collective-permute-done((bf16[128,2048]{1,0:T(8,128)(2,1)S(1)}, bf16[128,2048]{1,0:T(8,128)(2,1)S(1)}, u32[]{:S(2)}, u32[]{:S(2)}) %collective-permute-start.28) | collective-permute-done | bytes 524320 | tf_op jit(solution)/shard_map/ppermute | solution.py:397
  457.1 9.8 %collective-permute-done.29 = bf16[128,2048]{1,0:T(8,128)(2,1)S(1)} collective-permute-done((bf16[128,2048]{1,0:T(8,128)(2,1)S(1)}, bf16[128,2048]{1,0:T(8,128)(2,1)S(1)}, u32[]{:S(2)}, u32[]{:S(2)}) %collective-permute-start.29) | collective-permute-done | bytes 524320 | tf_op jit(solution)/shard_map/ppermute | solution.py:397
  536.8 14.6 %collective-permute-done.38 = bf16[4,128,256]{2,1,0:T(8,128)(2,1)S(1)} collective-permute-done((bf16[4,128,256]{2,1,0:T(8,128)(2,1)}, bf16[4,128,256]{2,1,0:T(8,128)(2,1)S(1)}, u32[]{:S(2)}, u32[]{:S(2)}) %collective-permute-start.38) | collective-permute-done | bytes 262176 | tf_op jit(solution)/shard_map/ppermute | solution.py:383
  579.8 10.1 %collective-permute-done.35 = bf16[128,2048]{1,0:T(8,128)(2,1)S(1)} collective-permute-done((bf16[128,2048]{1,0:T(8,128)(2,1)S(1)}, bf16[128,2048]{1,0:T(8,128)(2,1)S(1)}, u32[]{:S(2)}, u32[]{:S(2)}) %collective-permute-start.35) | collective-permute-done | bytes 524320 | tf_op jit(solution)/shard_map/ppermute | solution.py:397
  592.5 32.4 %shard_map.422 = (bf16[1024,1024]{1,0:T(8,128)(2,1)}, f32[2,8,1024]{2,1,0:T(8,128)S(1)}, f32[2,8,1024]{2,1,0:T(8,128)S(1)}, f32[4,4,512]{2,1,0:T(4,128)S(1)}, f32[4,512,8]{2,1,0:T(8,128)S(1)}) custom-call(f32[1024,1024]{1,0:T(8,128)} %copy-done.115, f32[2,8,1024]{2,1,0:T(8,128)S(1)} %copy-done.14, f32[4,1024]{1,0:T(4,128)S(1)} %bitcast.449, ...), custom_call_target="tpu_custom_call" | custom-call | flops 8053063680 | bytes 33980416 | tf_op jit(solution)/shard_map/pallas_call | solution.py:366
  636.5 9.4 %convolution_convert_fusion.4 = bf16[2048,1024]{1,0:T(8,128)(2,1)} fusion(bf16[1024,2048]{1,0:T(8,128)(2,1)} %bitcast.461, bf16[1024,1024]{1,0:T(8,128)(2,1)} %bitcast.526), kind=kOutput, calls=%fused_computation.32 | convolution fusion | flops 4297064448 | bytes 10485760 | tf_op jit(solution)/shard_map/dot_general | solution.py:29
  654.6 12.2 %add_convert_fusion = bf16[1024,2048]{1,0:T(8,128)(2,1)S(1)} fusion(f32[1024,2048]{1,0:T(8,128)} %fusion.97, f32[1024,2048]{1,0:T(8,128)} %fusion.16, bf16[1024,1024]{1,0:T(8,128)(2,1)} %bitcast.527, bf16[2048,1024]{1,0:T(8,128)(2,1)} %all-gather.5.cloned.1.call-done), kind=kOutput, calls=%fused_computation | convolution fusion | flops 4301258752 | bytes 27262976 | tf_op jit(solution)/shard_map/dot_general | solution.py:29
  690.5 11.4 %fusion.83 = (f32[256,2,1408]{2,1,0:T(2,128)}, f32[256,2,1408]{2,1,0:T(2,128)}) fusion(f32[256,2,1408]{2,1,0:T(2,128)S(1)} %get-tuple-element.280, f32[256,2,1408]{2,1,0:T(2,128)S(1)} %copy-done.35, f32[2,256,2,1408]{3,2,1,0:T(2,128)S(1)} %bitcast.455), kind=kLoop, calls=%fused_computation.303 | loop fusion | flops 11534336 | bytes 17301504 | tf_op jit(solution)/shard_map/mul | solution.py:495
  701.9 10.9 %collective-permute-done.42 = bf16[128,2048]{1,0:T(8,128)(2,1)S(1)} collective-permute-done((bf16[128,2048]{1,0:T(8,128)(2,1)S(1)}, bf16[128,2048]{1,0:T(8,128)(2,1)S(1)}, u32[]{:S(2)}, u32[]{:S(2)}) %collective-permute-start.42) | collective-permute-done | bytes 524320 | tf_op jit(solution)/shard_map/ppermute | solution.py:397
  745.5 10.0 %collective-permute-done.50 = f32[37152]{0:T(1024)S(1)} collective-permute-done((f32[37152]{0:T(1024)S(1)}, f32[37152]{0:T(1024)S(1)}, u32[]{:S(2)}, u32[]{:S(2)}) %collective-permute-start.50) | collective-permute-done | bytes 148640 | tf_op jit(solution)/shard_map/ppermute | solution.py:387
  766.7 10.3 %convert_add_fusion.2 = (f32[512,2048]{1,0:T(8,128)}, f32[512,2048]{1,0:T(8,128)}) fusion(f32[512,2048]{1,0:T(8,128)} %param.21, bf16[512,4096]{1,0:T(8,128)(2,1)} %bitcast.464, f32[512,2048]{1,0:T(8,128)} %param.20), kind=kLoop, calls=%fused_computation.24 | loop fusion | flops 4194304 | bytes 20971520 | tf_op jit(solution)/shard_map/add | solution.py:812
  (669 shorter events, 472.8 us)
Async XLA Ops:
  7.2 104.7 %all-gather.5.cloned.1.call-start = ((), (), s32[]{:S(2)}) async-start(), calls=%async_computation.6 | async-start | bytes 5242880 | tf_op jit(solution)/shard_map/all_gather | solution.py:589
  29.8 32.4 %collective-permute-start = (bf16[128,2048]{1,0:T(8,128)(2,1)}, bf16[128,2048]{1,0:T(8,128)(2,1)}, u32[]{:S(2)}, u32[]{:S(2)}) collective-permute-start(bf16[128,2048]{1,0:T(8,128)(2,1)} %multiply_convert_fusion.4), channel_id=1, source_target_pairs={{0,2},{1,3},{2,0},{3,1},{16,18},{17,19},{18,16},{19,17},{4,6},{5,7... | collective-permute-start | bytes 1572872 | tf_op jit(solution)/shard_map/ppermute | solution.py:397
  31.5 32.5 %collective-permute-start.1 = (bf16[128,2048]{1,0:T(8,128)(2,1)}, bf16[128,2048]{1,0:T(8,128)(2,1)}, u32[]{:S(2)}, u32[]{:S(2)}) collective-permute-start(bf16[128,2048]{1,0:T(8,128)(2,1)} %multiply_convert_fusion.4), channel_id=1, source_target_pairs={{0,16},{1,17},{2,18},{3,19},{16,0},{17,1},{18,2},{19,3},{4,20},{5,... | collective-permute-start | bytes 1572872 | tf_op jit(solution)/shard_map/ppermute | solution.py:397
  33.1 32.9 %collective-permute-start.2 = (bf16[128,2048]{1,0:T(8,128)(2,1)}, bf16[128,2048]{1,0:T(8,128)(2,1)}, u32[]{:S(2)}, u32[]{:S(2)}) collective-permute-start(bf16[128,2048]{1,0:T(8,128)(2,1)} %multiply_convert_fusion.4), channel_id=1, source_target_pairs={{0,18},{1,19},{2,16},{3,17},{16,2},{17,3},{18,0},{19,1},{4,22},{5,... | collective-permute-start | bytes 1572872 | tf_op jit(solution)/shard_map/ppermute | solution.py:397
  35.9 46.2 %all-to-all-start = ((bf16[8,2,1024]{2,1,0:T(2,128)(2,1)}), bf16[8,2,1024]{2,1,0:T(2,128)(2,1)}, u32[]{:S(2)}, u32[]{:S(2)}) async-start(bf16[8,2,1024]{2,1,0:T(2,128)(2,1)} %reshape.659), calls=%async_computation | async-start | bytes 65536 | tf_op jit(solution)/shard_map/all_to_all | solution.py:595
  42.0 180.2 %all-gather.7.cloned.1.call-start = ((), (), s32[]{:S(2)}) async-start(), calls=%async_computation.7 | async-start | bytes 5242880 | tf_op jit(solution)/shard_map/all_gather | solution.py:589
  43.7 33.0 %collective-permute-start.13 = (bf16[256,1024]{1,0:T(8,128)(2,1)}, bf16[256,1024]{1,0:T(8,128)(2,1)}, u32[]{:S(2)}, u32[]{:S(2)}) collective-permute-start(bf16[256,1024]{1,0:T(8,128)(2,1)} %broadcast_select_fusion.14), channel_id=1, source_target_pairs={{0,16},{16,0},{1,17},{17,1},{2,18},{18,2},{3,19},{19,3},{4,20},{20... | collective-permute-start | bytes 1572872 | tf_op jit(solution)/shard_map/ppermute | solution.py:387
  79.1 236.4 %all-gather.9.cloned.1.call-start = ((), (), s32[]{:S(2)}) async-start(), calls=%async_computation.8 | async-start | bytes 7208960 | tf_op jit(solution)/shard_map/all_gather | solution.py:589
  155.5 26.1 %collective-permute-start.10 = (bf16[128,2048]{1,0:T(8,128)(2,1)S(1)}, bf16[128,2048]{1,0:T(8,128)(2,1)S(1)}, u32[]{:S(2)}, u32[]{:S(2)}) collective-permute-start(bf16[128,2048]{1,0:T(8,128)(2,1)S(1)} %convert_element_type.230), channel_id=1, source_target_pairs={{0,16},{1,17},{2,18},{3,19},{16,0},{17,1},{18,2},{19,3},{4,20},{5,... | collective-permute-start | bytes 1572872 | tf_op jit(solution)/shard_map/ppermute | solution.py:397
  157.1 24.5 %collective-permute-start.11 = (bf16[128,2048]{1,0:T(8,128)(2,1)S(1)}, bf16[128,2048]{1,0:T(8,128)(2,1)S(1)}, u32[]{:S(2)}, u32[]{:S(2)}) collective-permute-start(bf16[128,2048]{1,0:T(8,128)(2,1)S(1)} %convert_element_type.230), channel_id=1, source_target_pairs={{0,18},{1,19},{2,16},{3,17},{16,2},{17,3},{18,0},{19,1},{4,22},{5,... | collective-permute-start | bytes 1572872 | tf_op jit(solution)/shard_map/ppermute | solution.py:397
  159.6 36.4 %collective-permute-start.22 = (bf16[256,1408]{1,0:T(8,128)(2,1)S(1)}, bf16[256,1408]{1,0:T(8,128)(2,1)S(1)}, u32[]{:S(2)}, u32[]{:S(2)}) collective-permute-start(bf16[256,1408]{1,0:T(8,128)(2,1)S(1)} %broadcast_select_fusion.4), channel_id=1, source_target_pairs={{0,16},{16,0},{1,17},{17,1},{2,18},{18,2},{3,19},{19,3},{4,20},{20... | collective-permute-start | bytes 2162696 | tf_op jit(solution)/shard_map/ppermute | solution.py:387
  161.2 35.5 %collective-permute-start.6 = (bf16[4,128,256]{2,1,0:T(8,128)(2,1)S(1)}, bf16[4,128,256]{2,1,0:T(8,128)(2,1)S(1)}, u32[]{:S(2)}, u32[]{:S(2)}) collective-permute-start(bf16[4,128,256]{2,1,0:T(8,128)(2,1)S(1)} %slice.930), channel_id=1, source_target_pairs={{0,4},{4,8},{8,12},{1,5},{5,9},{9,13},{2,6},{6,10},{10,14},{3,7},{... | collective-permute-start | bytes 786440 | tf_op jit(solution)/shard_map/ppermute | solution.py:383
  183.4 35.6 %collective-permute-start.12 = (bf16[512,2048]{1,0:T(8,128)(2,1)}, bf16[512,2048]{1,0:T(8,128)(2,1)}, u32[]{:S(2)}, u32[]{:S(2)}) collective-permute-start(bf16[512,2048]{1,0:T(8,128)(2,1)} %pad_maximum_fusion.6), channel_id=1, source_target_pairs={{0,1},{1,0},{2,3},{3,2},{4,5},{5,4},{6,7},{7,6},{8,9},{9,8},{10,11... | collective-permute-start | bytes 6291464 | tf_op jit(solution)/shard_map/ppermute | solution.py:387
  201.5 173.2 %all-gather.11.cloned.1.call-start = ((), (), s32[]{:S(2)}) async-start(), calls=%async_computation.9 | async-start | bytes 3604480 | tf_op jit(solution)/shard_map/all_gather | solution.py:589
  242.6 24.3 %collective-permute-start.16 = (bf16[128,2048]{1,0:T(8,128)(2,1)S(1)}, bf16[128,2048]{1,0:T(8,128)(2,1)S(1)}, u32[]{:S(2)}, u32[]{:S(2)}) collective-permute-start(bf16[128,2048]{1,0:T(8,128)(2,1)S(1)} %get-tuple-element.332), channel_id=1, source_target_pairs={{0,16},{1,17},{2,18},{3,19},{16,0},{17,1},{18,2},{19,3},{4,20},{5,... | collective-permute-start | bytes 1572872 | tf_op jit(solution)/shard_map/ppermute | solution.py:397
  308.4 209.7 %reduce-scatter.9.cloned.1.call-start = ((), (), s32[]{:S(2)}) async-start(), calls=%async_computation.12 | async-start | bytes 3604480 | tf_op jit(solution)/shard_map/reduce_scatter | solution.py:689
  382.1 181.0 %reduce-scatter.5.cloned.1.call-start = ((), (), s32[]{:S(2)}) async-start(), calls=%async_computation.10 | async-start | bytes 7208960 | tf_op jit(solution)/shard_map/reduce_scatter | solution.py:698
  421.1 344.1 %reduce-scatter.11.cloned.1.call-start = ((), (), s32[]{:S(2)}) async-start(), calls=%async_computation.13 | async-start | bytes 5242880 | tf_op jit(solution)/shard_map/reduce_scatter | solution.py:790
  518.0 38.7 %collective-permute-start.33 = (bf16[512,2048]{1,0:T(8,128)(2,1)}, bf16[512,2048]{1,0:T(8,128)(2,1)}, u32[]{:S(2)}, u32[]{:S(2)}) collective-permute-start(bf16[512,2048]{1,0:T(8,128)(2,1)} %slice.563), channel_id=1, source_target_pairs={{0,1},{1,0},{2,3},{3,2},{4,5},{5,4},{6,7},{7,6},{8,9},{9,8},{10,11... | collective-permute-start | bytes 6291464 | tf_op jit(solution)/shard_map/ppermute | solution.py:387
  520.1 31.4 %collective-permute-start.53 = (bf16[256,704]{0,1:T(8,128)(2,1)}, bf16[256,704]{0,1:T(8,128)(2,1)}, u32[]{:S(2)}, u32[]{:S(2)}) collective-permute-start(bf16[256,704]{0,1:T(8,128)(2,1)} %broadcast_select_fusion.18), channel_id=1, source_target_pairs={{0,16},{16,0},{1,17},{17,1},{2,18},{18,2},{3,19},{19,3},{4,20},{20... | collective-permute-start | bytes 1081352 | tf_op jit(solution)/shard_map/ppermute | solution.py:387
  633.9 38.8 %collective-permute-start.52 = (bf16[256,1408]{1,0:T(8,128)(2,1)}, bf16[256,1408]{1,0:T(8,128)(2,1)}, u32[]{:S(2)}, u32[]{:S(2)}) collective-permute-start(bf16[256,1408]{1,0:T(8,128)(2,1)} %broadcast_select_fusion), channel_id=1, source_target_pairs={{0,16},{16,0},{1,17},{17,1},{2,18},{18,2},{3,19},{19,3},{4,20},{20... | collective-permute-start | bytes 2162696 | tf_op jit(solution)/shard_map/ppermute | solution.py:387
  654.3 135.6 %reduce-scatter.7.cloned.1.call-start = ((), (), s32[]{:S(2)}) async-start(), calls=%async_computation.11 | async-start | bytes 5242880 | tf_op jit(solution)/shard_map/reduce_scatter | solution.py:796
  688.0 24.8 %collective-permute-start.42 = (bf16[128,2048]{1,0:T(8,128)(2,1)S(1)}, bf16[128,2048]{1,0:T(8,128)(2,1)S(1)}, u32[]{:S(2)}, u32[]{:S(2)}) collective-permute-start(bf16[128,2048]{1,0:T(8,128)(2,1)S(1)} %get-tuple-element.323), channel_id=1, source_target_pairs={{0,16},{1,17},{2,18},{3,19},{16,0},{17,1},{18,2},{19,3},{4,20},{5,... | collective-permute-start | bytes 1572872 | tf_op jit(solution)/shard_map/ppermute | solution.py:397
  725.4 30.1 %collective-permute-start.44 = (bf16[128,4096]{1,0:T(8,128)(2,1)S(1)}, bf16[128,4096]{1,0:T(8,128)(2,1)S(1)}, u32[]{:S(2)}, u32[]{:S(2)}) collective-permute-start(bf16[128,4096]{1,0:T(8,128)(2,1)S(1)} %pad_maximum_fusion.14), channel_id=1, source_target_pairs={{0,2},{1,3},{2,0},{3,1},{16,18},{17,19},{18,16},{19,17},{4,6},{5,7... | collective-permute-start | bytes 3145736 | tf_op jit(solution)/shard_map/ppermute | solution.py:397
  (169 other events, 2214.8 us)
Sparse Core Ops, SparseCore 0:
  29.0 82.8 all-gather.4
  114.0 81.8 all-gather.6
  201.6 105.4 all-gather.8
  309.0 65.5 all-gather.10
  382.3 54.9 reduce-scatter.8
  439.9 118.9 reduce-scatter.4
  563.3 76.4 reduce-scatter.10
  669.7 82.0 reduce-scatter.6

commit v4 on v3

--- a/solution.py
+++ b/solution.py
@@ -425,7 +425,7 @@
     return jnp.concatenate([here, swapped(here, "tensor", 1)], axis=0)
 
 
-def scatter_absolute(partial):
+def scatter_absolute(partial, tokens=(), started=None):
     dp_size, chips = lax.axis_size("dp"), lax.axis_size("tensor") // 2
     core = lax.axis_index("tensor") % 2
     chip = lax.axis_index("tensor") // 2
@@ -436,7 +436,9 @@
     mine = jnp.where(core == 0, even, odd)
     theirs = jnp.where(core == 0, odd, even)
     summed = mine.astype(F32) + swapped(theirs, "tensor", 1).astype(F32)
-    low = summed.astype(BF16)
+    low = after(summed.astype(BF16), tokens)
+    if started is not None:
+        started.append(low)
     total = lax.dynamic_index_in_dim(summed, device * chips + chip, 0, keepdims=False)
     for d, t in partner_bits():
         target = (device ^ d) * chips + (chip ^ t)
@@ -472,12 +474,16 @@
     return lax.optimization_barrier((value, tokens))[0]
 
 
-def butterfly_sum(array):
-    for axis in ("tensor", "dp", "seq"):
-        distance = 1
-        while distance < lax.axis_size(axis):
-            array = array + swapped(array, axis, distance)
-            distance *= 2
+def butterfly_sum(array, axes):
+    for axis in axes:
+        distance, size = 1, lax.axis_size(axis)
+        while distance < size:
+            near = array + swapped(array, axis, distance)
+            if 2 * distance < size:
+                far = swapped(array, axis, 2 * distance) + swapped(array, axis, 3 * distance)
+                array, distance = near + far, 4 * distance
+            else:
+                array, distance = near, 2 * distance
     return array
 
 
@@ -796,29 +802,36 @@
     qkv_sum = lax.psum_scatter(
         after(grad_qkv_weights, swiglu_sum), "seq", scatter_dimension=0, tiled=True
     )
-    grad_rates_weights = contract_rows(after(normed_in, grad_qkv_weights), grad_rates)
+    grad_rates_weights = contract_rows(grad_rates, after(normed_in, grad_qkv_weights))
+    def halves_of(part):
+        return mine_and_theirs(part[:depth], part[depth:])
+
+    def exchanged(halves):
+        own, theirs = halves
+        received = swapped(theirs, "dp", 1)
+        return tuple(a.astype(F32) for a in by_device(own, received))
+
+    mixer_parts = exchanged(halves_of(mixer_sum))
+    started = []
     normed_in_term = (
         contract_cols(after(grad_projected, (grad_qkv_weights, grad_rates_weights)), full_qkv)
         + contract_cols(grad_gate_raw, full_gate)
         + contract_cols(grad_rates, full_rates)
     )
-    grad_normed_in = scatter_absolute(normed_in_term.astype(BF16))
+    grad_normed_in = scatter_absolute(normed_in_term.astype(BF16), mixer_parts, started)
     from_in, grad_gain_in = norm_back(factor_in, normal_in, gains[0], grad_normed_in)
     added = turned_back(jnp.concatenate([attention + feedforward, from_mid + from_in], axis=0))
     added = gather_absolute(
         jnp.concatenate([added[:rows], added[rows:]], axis=1).astype(BF16), False
     ).reshape(length, 2 * width)
+    gathered_rows = added
+    qkv_halves = halves_of(after(qkv_sum, added))
+    added = after(added, qkv_halves)
     result = stream + added[:, :width].astype(F32)
     grad_stream = cotangent + added[:, width:].astype(F32)
 
-    def exchanged(part):
-        own, theirs = mine_and_theirs(part[:depth], part[depth:])
-        received = swapped(theirs, "dp", 1)
-        return tuple(a.astype(F32) for a in by_device(own, received))
-
-    swiglu_parts, down_parts, mixer_parts = (
-        exchanged(part) for part in (swiglu_sum, down_sum, mixer_sum)
-    )
+    swiglu_parts = exchanged(halves_of(after(swiglu_sum, started)))
+    down_parts = exchanged(halves_of(after(down_sum, started)))
     g_output = jnp.concatenate(
         [m[:, heads * DV :].T.reshape(heads, DV, depth) for m in mixer_parts], axis=0
     )
@@ -842,26 +855,24 @@
     )
     gains_term = turned_back(jnp.stack([grad_gain_in, grad_gain_mid]))
     scale_term = jnp.sum(grad_scale[:, 0], axis=0)
-    rates_term = lax.dynamic_update_slice_in_dim(
-        jnp.zeros((dp_size, width, heads * 2), F32),
-        grad_rates_weights[None],
-        lax.axis_index("dp"),
-        0,
-    )
-    rates_term = jnp.transpose(rates_term, (1, 0, 2))
+    first = lax.axis_index("dp") == 0
+    rates_term = jnp.concatenate(
+        [jnp.where(first, grad_rates_weights, 0.0), jnp.where(first, 0.0, grad_rates_weights)], axis=0
+    )
     small = [conv_term, heads_term, gains_term, scale_term]
     flat = jnp.concatenate([a.reshape(-1) for a in small])
-    flat = butterfly_sum(flat)
+    flat = butterfly_sum(after(flat, gathered_rows), ("tensor",))
+    flat = jnp.concatenate([flat, rates_term.reshape(-1)])
+    flat = butterfly_sum(flat, ("dp", "seq"))
     sums, at = [], 0
     for a in small:
         sums.append(flat[at : at + a.size].reshape(a.shape))
         at += a.size
     g_conv, g_heads, g_gains, g_scale = sums
-    rates_term = rates_term.reshape(seq_size, dp_size, depth, heads_stored * 2)
-    rates_term = jnp.swapaxes(rates_term, 0, 1).reshape(dp_size * seq_size, -1)
-    g_rates = jnp.sum(
-        lax.all_to_all(rates_term, ("dp", "seq"), 0, 0, tiled=True), axis=0
-    ).reshape(depth, heads_stored, 2)
+    block = lax.axis_index("seq") * dp_size + lax.axis_index("dp")
+    g_rates = lax.dynamic_slice_in_dim(
+        flat[at:].reshape(heads_stored * 2, width), block * depth, depth, 1
+    ).T.reshape(depth, heads_stored, 2)
 
     tokens = float(length * dp_size * seq_size)
     new_rates, moment_rates = adam_update(w_rates, g_rates, m_rates, tokens)
@@ -872,8 +883,7 @@
     new_gains, moment_gains = adam_update(w_gains, g_gains, m_gains, tokens)
     new_scale, moment_scale = adam_update(w_scale, g_scale, m_scale, tokens)
     new_heads, moment_heads = adam_update(w_heads, g_heads, m_heads, tokens)
-    others = (result, grad_stream, g_conv, new_output, new_swiglu, new_down, new_rates)
-    qkv_parts = exchanged(after(qkv_sum, others))
+    qkv_parts = exchanged(qkv_halves)
     g_input = jnp.concatenate(
         [
             jnp.concatenate(

time: 842 us -> 820 us (0.974)
  other arithmetic: 144 us -> 128 us
    ppermute x25, waiting for transfers between devices: 126 us -> 107 us  [group_swapped(): return lax.ppermute(block, ('dp', 'tensor'), route)]
    ppermute x22 -> x24, starting transfers between devices: 15.8 us -> 19.6 us  [swapped(): lax.ppermute(block, axis, [(i, i ^ bits) for i in range(lax.axis_size(axi...]
    ppermute x22 -> x24, waiting for transfers between devices: 72.3 us -> 74.6 us  [swapped(): lax.ppermute(block, axis, [(i, i ^ bits) for i in range(lax.axis_size(axi...]
    unnamed x303 -> x306, local copies, waits for them, and re-layouts: 51.7 us -> 49.9 us
  transfers between devices with their start and end apart: 65 -> 66, of which waited for: 35 -> 33; matrix products, arithmetic and copies ran while one was open for 39% -> 39% of each run, Pallas kernels for 8% -> 8%
where the time goes in v4:
time: 820 us; the launch traced here: 810 us
  waiting for transfers between devices  300 us (37%)
  other arithmetic  128 us (16%)
  local copies, waits for them, and re-layouts  111 us (14%)
  matrix products  111 us (14%)
  starting transfers between devices  74.6 us (9%)
  Pallas kernels  68.7 us (8%)
  between operations  17 us (2%)
    dot_general x18, matrix products, dot(): return lax.dot_general(left, right, dims, preferred_element_type=F32)  108 us
    ppermute x25, waiting for transfers between devices, group_swapped(): return lax.ppermute(block, ('dp', 'tensor'), route)  107 us
    ppermute x24, waiting for transfers between devices, swapped(): lax.ppermute(block, axis, [(i, i ^ bits) for i in range(lax.axis_size(axi...  74.6 us
    pallas_call x4, Pallas kernels, chains_call(): pl.pallas_call(kernel, grid=(chains,), in_specs=[spec(tag, a.shape) for t...  68.7 us
    all_gather x4, waiting for transfers between devices, body(): gathered.append(lax.all_gather(shard, 'seq', axis=0, tiled=True))  62 us
    unnamed x306, local copies, waits for them, and re-layouts  49.9 us
    ppermute x8, waiting for transfers between devices, shifted(): return lax.ppermute(block, axis, route)  44.7 us
    ppermute x25, starting transfers between devices, group_swapped(): return lax.ppermute(block, ('dp', 'tensor'), route)  28.6 us
  transfers between devices with their start and end apart: 66, of which 33 were waited for; matrix products, arithmetic and copies ran while one was open for 39% of the time, Pallas kernels for 8%

profile of v4, /device:TPU:0, one launch (start us, length us, event | category | flops | bytes accessed | tf_op | source)
XLA Modules:
  0.0 810.0 jit_solution(1034429019490310332)
XLA Ops:
  91.3 20.6 %all-gather.5.cloned.1.call-done = bf16[2048,1024]{1,0:T(8,128)(2,1)} async-done(((bf16[512,1024]{1,0:T(8,128)(2,1)}), bf16[2048,1024]{1,0:T(8,128)(2,1)}) %all-gather.5.cloned.1.call-update) | async-done | bytes 4194320 | tf_op jit(solution)/shard_map/all_gather | solution.py:595
  131.6 25.0 %shard_map.419 = (f32[4,512,128]{2,1,0:T(8,128)S(1)}, f32[4,512,256]{2,1,0:T(8,128)}, f32[4,128,384]{2,1,0:T(8,128)S(1)}, f32[4,4,128,384]{3,2,1,0:T(8,128)}, f3...) custom-call(f32[1024,1024]{1,0:T(8,128)} %copy-done.119, ...), custom_call_target="tpu_custom_call" | custom-call | flops 6039797760 | bytes 8814592 | tf_op jit(solution)/shard_map/pallas_call | solution.py:366
  165.6 17.1 %collective-permute-done.10 = bf16[128,2048]{1,0:T(8,128)(2,1)S(1)} collective-permute-done((bf16[128,2048]{1,0:T(8,128)(2,1)S(1)}, bf16[128,2048]{1,0:T(8,128)(2,1)S(1)}, u32[]{:S(2)}, u32[]{:S(2)}) %collective-permute-start.10) | collective-permute-done | bytes 524320 | tf_op jit(solution)/shard_map/ppermute | solution.py:397
  184.7 12.4 %collective-permute-done.22 = bf16[256,1408]{1,0:T(8,128)(2,1)S(1)} collective-permute-done((bf16[256,1408]{1,0:T(8,128)(2,1)S(1)}, bf16[256,1408]{1,0:T(8,128)(2,1)S(1)}, u32[]{:S(2)}, u32[]{:S(2)}) %collective-permute-start.22) | collective-permute-done | bytes 720928 | tf_op jit(solution)/shard_map/ppermute | solution.py:387
  247.7 11.3 %collective-permute-done.15 = bf16[128,2048]{1,0:T(8,128)(2,1)S(1)} collective-permute-done((bf16[128,2048]{1,0:T(8,128)(2,1)S(1)}, bf16[128,2048]{1,0:T(8,128)(2,1)S(1)}, u32[]{:S(2)}, u32[]{:S(2)}) %collective-permute-start.15) | collective-permute-done | bytes 524320 | tf_op jit(solution)/shard_map/ppermute | solution.py:397
  259.0 10.9 %collective-permute-done.16 = bf16[128,2048]{1,0:T(8,128)(2,1)S(1)} collective-permute-done((bf16[128,2048]{1,0:T(8,128)(2,1)S(1)}, bf16[128,2048]{1,0:T(8,128)(2,1)S(1)}, u32[]{:S(2)}, u32[]{:S(2)}) %collective-permute-start.16) | collective-permute-done | bytes 524320 | tf_op jit(solution)/shard_map/ppermute | solution.py:397
  275.7 11.3 %collective-permute-done.18 = bf16[128,2048]{1,0:T(8,128)(2,1)S(1)} collective-permute-done((bf16[128,2048]{1,0:T(8,128)(2,1)S(1)}, bf16[128,2048]{1,0:T(8,128)(2,1)S(1)}, u32[]{:S(2)}, u32[]{:S(2)}) %collective-permute-start.18) | collective-permute-done | bytes 524320 | tf_op jit(solution)/shard_map/ppermute | solution.py:397
  287.0 10.8 %collective-permute-done.19 = bf16[128,2048]{1,0:T(8,128)(2,1)S(1)} collective-permute-done((bf16[128,2048]{1,0:T(8,128)(2,1)S(1)}, bf16[128,2048]{1,0:T(8,128)(2,1)S(1)}, u32[]{:S(2)}, u32[]{:S(2)}) %collective-permute-start.19) | collective-permute-done | bytes 524320 | tf_op jit(solution)/shard_map/ppermute | solution.py:397
  299.9 10.5 %collective-permute-done.23 = bf16[256,704]{0,1:T(8,128)(2,1)S(1)} collective-permute-done((bf16[256,704]{0,1:T(8,128)(2,1)S(1)}, bf16[256,704]{0,1:T(8,128)(2,1)S(1)}, u32[]{:S(2)}, u32[]{:S(2)}) %collective-permute-start.23) | collective-permute-done | bytes 360480 | tf_op jit(solution)/shard_map/ppermute | solution.py:387
  319.8 10.6 %fusion.170 = f32[1024,1408]{1,0:T(8,128)S(1)} fusion(bf16[1024,2048]{1,0:T(8,128)(2,1)} %constant_dynamic-update-slice_fusion.13, bf16[2048,1408]{1,0:T(8,128)(2,1)} %all-gather.9.cloned.1.call-done), kind=kOutput, calls=%fused_computation.455 | convolution fusion | flops 5905580032 | bytes 15728640 | tf_op jit(solution)/shard_map/dot_general | solution.py:29
  335.3 41.4 %all-gather.11.cloned.1.call-done = bf16[2048,704]{0,1:T(8,128)(2,1)} async-done(((bf16[512,704]{0,1:T(8,128)(2,1)}), bf16[2048,704]{0,1:T(8,128)(2,1)}) %all-gather.11.cloned.1.call-update) | async-done | bytes 2883600 | tf_op jit(solution)/shard_map/all_gather | solution.py:595
  384.4 9.3 %multiply_convert_fusion.1 = (bf16[1024,704]{1,0:T(8,128)(2,1)S(1)}, bf16[1024,704]{1,0:T(8,128)(2,1)S(1)}) fusion(f32[1024,1408]{1,0:T(8,128)} %copy-done.36, bf16[1024,2048]{1,0:T(8,128)(2,1)} %constant_dynamic-update-slice_fusion.8, bf16[2048,704]{0,1:T(8,128)(2,1)} %all-gather.11.cloned.1.call-done), kind=kOutput, calls=%fused_computation.44 | convolution fusion | flops 2962161664 | bytes 15728640 | tf_op jit(solution)/shard_map/dot_general | solution.py:29
  414.5 8.8 %convolution_convert_fusion = bf16[2048,1408]{1,0:T(8,128)(2,1)} fusion(bf16[1024,2048]{1,0:T(8,128)(2,1)S(1)} %copy-done.89, bf16[1024,704]{1,0:T(8,128)(2,1)S(1)} %get-tuple-element.138, bf16[1024,704]{1,0:T(8,128)(2,1)S(1)} %get-tuple-element.137), kind=kOutput, calls=%fused_computation.1 | convolution fusion | flops 5914230784 | bytes 12845056 | tf_op jit(solution)/shard_map/dot_general | solution.py:29
  426.0 11.5 %collective-permute-done.26 = bf16[128,2048]{1,0:T(8,128)(2,1)} collective-permute-done((bf16[128,2048]{1,0:T(8,128)(2,1)}, bf16[128,2048]{1,0:T(8,128)(2,1)}, u32[]{:S(2)}, u32[]{:S(2)}) %collective-permute-start.26) | collective-permute-done | bytes 524320 | tf_op jit(solution)/shard_map/ppermute | solution.py:397
  445.4 11.4 %collective-permute-done.28 = bf16[128,2048]{1,0:T(8,128)(2,1)S(1)} collective-permute-done((bf16[128,2048]{1,0:T(8,128)(2,1)S(1)}, bf16[128,2048]{1,0:T(8,128)(2,1)S(1)}, u32[]{:S(2)}, u32[]{:S(2)}) %collective-permute-start.28) | collective-permute-done | bytes 524320 | tf_op jit(solution)/shard_map/ppermute | solution.py:397
  456.8 10.4 %collective-permute-done.29 = bf16[128,2048]{1,0:T(8,128)(2,1)S(1)} collective-permute-done((bf16[128,2048]{1,0:T(8,128)(2,1)S(1)}, bf16[128,2048]{1,0:T(8,128)(2,1)S(1)}, u32[]{:S(2)}, u32[]{:S(2)}) %collective-permute-start.29) | collective-permute-done | bytes 524320 | tf_op jit(solution)/shard_map/ppermute | solution.py:397
  487.6 22.1 %collective-permute-done.32 = bf16[4,128,256]{2,1,0:T(8,128)(2,1)S(1)} collective-permute-done((bf16[4,128,256]{2,1,0:T(8,128)(2,1)S(1)}, bf16[4,128,256]{2,1,0:T(8,128)(2,1)S(1)}, u32[]{:S(2)}, u32[]{:S(2)}) %collective-permute-start.32) | collective-permute-done | bytes 262176 | tf_op jit(solution)/shard_map/ppermute | solution.py:383
  536.9 10.0 %collective-permute-done.37 = bf16[4,128,256]{2,1,0:T(8,128)(2,1)S(1)} collective-permute-done((bf16[4,128,256]{2,1,0:T(8,128)(2,1)S(1)}, bf16[4,128,256]{2,1,0:T(8,128)(2,1)S(1)}, u32[]{:S(2)}, u32[]{:S(2)}) %collective-permute-start.37) | collective-permute-done | bytes 262176 | tf_op jit(solution)/shard_map/ppermute | solution.py:383
  566.9 33.1 %shard_map.422 = (bf16[1024,1024]{1,0:T(8,128)(2,1)}, f32[2,8,1024]{2,1,0:T(8,128)S(1)}, f32[2,8,1024]{2,1,0:T(8,128)S(1)}, f32[4,4,512]{2,1,0:T(4,128)S(1)}, f32[4,512,8]{2,1,0:T(8,128)S(1)}) custom-call(f32[1024,1024]{1,0:T(8,128)} %copy-done.119, f32[2,8,1024]{2,1,0:T(8,128)S(1)} %copy-done.12, f32[4,1024]{1,0:T(4,128)S(1)} %bitcast.444, ...), custom_call_target="tpu_custom_call" | custom-call | flops 8053063680 | bytes 33980416 | tf_op jit(solution)/shard_map/pallas_call | solution.py:366
  620.2 9.6 %add_convert_fusion = bf16[1024,2048]{1,0:T(8,128)(2,1)S(1)} fusion(f32[1024,2048]{1,0:T(8,128)} %fusion.97, f32[1024,2048]{1,0:T(8,128)} %fusion.16, bf16[1024,1024]{1,0:T(8,128)(2,1)S(1)} %bitcast.520, bf16[2048,1024]{1,0:T(8,128)(2,1)} %all-gather.5.cloned.1.call-done), kind=kOutput, calls=%fused_computation | convolution fusion | flops 4301258752 | bytes 27262976 | tf_op jit(solution)/shard_map/dot_general | solution.py:29
  676.8 16.8 %collective-permute-done.56 = bf16[256,704]{0,1:T(8,128)(2,1)} collective-permute-done((bf16[256,704]{0,1:T(8,128)(2,1)}, bf16[256,704]{0,1:T(8,128)(2,1)}, u32[]{:S(2)}, u32[]{:S(2)}) %collective-permute-start.56) | collective-permute-done | bytes 360480 | tf_op jit(solution)/shard_map/ppermute | solution.py:387
  715.5 9.6 %collective-permute-done.45 = bf16[128,4096]{1,0:T(8,128)(2,1)S(1)} collective-permute-done((bf16[128,4096]{1,0:T(8,128)(2,1)}, bf16[128,4096]{1,0:T(8,128)(2,1)S(1)}, u32[]{:S(2)}, u32[]{:S(2)}) %collective-permute-start.45) | collective-permute-done | bytes 1048608 | tf_op jit(solution)/shard_map/ppermute | solution.py:397
  725.3 10.0 %fusion.83 = (f32[256,2,1408]{2,1,0:T(2,128)S(1)}, f32[256,2,1408]{2,1,0:T(2,128)}) fusion(f32[256,2,1408]{2,1,0:T(2,128)S(1)} %get-tuple-element.116, f32[256,2,1408]{2,1,0:T(2,128)S(1)} %copy-done.30, f32[2,256,2,1408]{3,2,1,0:T(2,128)S(1)} %bitcast.450), kind=kLoop, calls=%fused_computation.306 | loop fusion | flops 11534336 | bytes 17301504 | tf_op jit(solution)/shard_map/mul | solution.py:501
  771.4 10.3 %convert_add_fusion.2 = (f32[512,2048]{1,0:T(8,128)}, f32[512,2048]{1,0:T(8,128)}) fusion(f32[512,2048]{1,0:T(8,128)} %param.21, bf16[512,4096]{1,0:T(8,128)(2,1)} %bitcast.451, f32[512,2048]{1,0:T(8,128)} %param.20), kind=kLoop, calls=%fused_computation.24 | loop fusion | flops 4194304 | bytes 20971520 | tf_op jit(solution)/shard_map/add | solution.py:831
  (669 shorter events, 438.3 us)
Async XLA Ops:
  7.2 104.7 %all-gather.5.cloned.1.call-start = ((), (), s32[]{:S(2)}) async-start(), calls=%async_computation.5 | async-start | bytes 5242880 | tf_op jit(solution)/shard_map/all_gather | solution.py:595
  29.8 32.2 %collective-permute-start = (bf16[128,2048]{1,0:T(8,128)(2,1)}, bf16[128,2048]{1,0:T(8,128)(2,1)}, u32[]{:S(2)}, u32[]{:S(2)}) collective-permute-start(bf16[128,2048]{1,0:T(8,128)(2,1)} %multiply_convert_fusion.4), channel_id=1, source_target_pairs={{0,2},{1,3},{2,0},{3,1},{16,18},{17,19},{18,16},{19,17},{4,6},{5,7... | collective-permute-start | bytes 1572872 | tf_op jit(solution)/shard_map/ppermute | solution.py:397
  31.5 32.4 %collective-permute-start.1 = (bf16[128,2048]{1,0:T(8,128)(2,1)}, bf16[128,2048]{1,0:T(8,128)(2,1)}, u32[]{:S(2)}, u32[]{:S(2)}) collective-permute-start(bf16[128,2048]{1,0:T(8,128)(2,1)} %multiply_convert_fusion.4), channel_id=1, source_target_pairs={{0,16},{1,17},{2,18},{3,19},{16,0},{17,1},{18,2},{19,3},{4,20},{5,... | collective-permute-start | bytes 1572872 | tf_op jit(solution)/shard_map/ppermute | solution.py:397
  33.1 32.8 %collective-permute-start.2 = (bf16[128,2048]{1,0:T(8,128)(2,1)}, bf16[128,2048]{1,0:T(8,128)(2,1)}, u32[]{:S(2)}, u32[]{:S(2)}) collective-permute-start(bf16[128,2048]{1,0:T(8,128)(2,1)} %multiply_convert_fusion.4), channel_id=1, source_target_pairs={{0,18},{1,19},{2,16},{3,17},{16,2},{17,3},{18,0},{19,1},{4,22},{5,... | collective-permute-start | bytes 1572872 | tf_op jit(solution)/shard_map/ppermute | solution.py:397
  35.9 44.7 %all-to-all-start = ((bf16[8,2,1024]{2,1,0:T(2,128)(2,1)}), bf16[8,2,1024]{2,1,0:T(2,128)(2,1)S(1)}, u32[]{:S(2)}, u32[]{:S(2)}) async-start(bf16[8,2,1024]{2,1,0:T(2,128)(2,1)} %reshape.659), calls=%async_computation | async-start | bytes 65536 | tf_op jit(solution)/shard_map/all_to_all | solution.py:601
  42.0 183.1 %all-gather.7.cloned.1.call-start = ((), (), s32[]{:S(2)}) async-start(), calls=%async_computation.6 | async-start | bytes 5242880 | tf_op jit(solution)/shard_map/all_gather | solution.py:595
  43.7 31.5 %collective-permute-start.13 = (bf16[256,1024]{1,0:T(8,128)(2,1)}, bf16[256,1024]{1,0:T(8,128)(2,1)}, u32[]{:S(2)}, u32[]{:S(2)}) collective-permute-start(bf16[256,1024]{1,0:T(8,128)(2,1)} %broadcast_select_fusion.14), channel_id=1, source_target_pairs={{0,16},{16,0},{1,17},{17,1},{2,18},{18,2},{3,19},{19,3},{4,20},{20... | collective-permute-start | bytes 1572872 | tf_op jit(solution)/shard_map/ppermute | solution.py:387
  77.7 242.1 %all-gather.9.cloned.1.call-start = ((), (), s32[]{:S(2)}) async-start(), calls=%async_computation.7 | async-start | bytes 7208960 | tf_op jit(solution)/shard_map/all_gather | solution.py:595
  160.7 36.4 %collective-permute-start.22 = (bf16[256,1408]{1,0:T(8,128)(2,1)S(1)}, bf16[256,1408]{1,0:T(8,128)(2,1)S(1)}, u32[]{:S(2)}, u32[]{:S(2)}) collective-permute-start(bf16[256,1408]{1,0:T(8,128)(2,1)S(1)} %broadcast_select_fusion.4), channel_id=1, source_target_pairs={{0,16},{16,0},{1,17},{17,1},{2,18},{18,2},{3,19},{19,3},{4,20},{20... | collective-permute-start | bytes 2162696 | tf_op jit(solution)/shard_map/ppermute | solution.py:387
  162.3 35.5 %collective-permute-start.6 = (bf16[4,128,256]{2,1,0:T(8,128)(2,1)S(1)}, bf16[4,128,256]{2,1,0:T(8,128)(2,1)S(1)}, u32[]{:S(2)}, u32[]{:S(2)}) collective-permute-start(bf16[4,128,256]{2,1,0:T(8,128)(2,1)S(1)} %slice.927), channel_id=1, source_target_pairs={{0,4},{4,8},{8,12},{1,5},{5,9},{9,13},{2,6},{6,10},{10,14},{3,7},{... | collective-permute-start | bytes 786440 | tf_op jit(solution)/shard_map/ppermute | solution.py:383
  184.6 37.3 %collective-permute-start.12 = (bf16[512,2048]{1,0:T(8,128)(2,1)}, bf16[512,2048]{1,0:T(8,128)(2,1)}, u32[]{:S(2)}, u32[]{:S(2)}) collective-permute-start(bf16[512,2048]{1,0:T(8,128)(2,1)} %pad_maximum_fusion.6), channel_id=1, source_target_pairs={{0,1},{1,0},{2,3},{3,2},{4,5},{5,4},{6,7},{7,6},{8,9},{9,8},{10,11... | collective-permute-start | bytes 6291464 | tf_op jit(solution)/shard_map/ppermute | solution.py:387
  203.2 173.4 %all-gather.11.cloned.1.call-start = ((), (), s32[]{:S(2)}) async-start(), calls=%async_computation.8 | async-start | bytes 3604480 | tf_op jit(solution)/shard_map/all_gather | solution.py:595
  311.4 238.0 %reduce-scatter.7.cloned.1.call-start = ((), (), s32[]{:S(2)}) async-start(), calls=%async_computation.10 | async-start | bytes 3604480 | tf_op jit(solution)/shard_map/reduce_scatter | solution.py:695
  384.1 171.9 %reduce-scatter.5.cloned.1.call-start = ((), (), s32[]{:S(2)}) async-start(), calls=%async_computation.9 | async-start | bytes 7208960 | tf_op jit(solution)/shard_map/reduce_scatter | solution.py:704
  423.3 217.0 %reduce-scatter.9.cloned.1.call-start = ((), (), s32[]{:S(2)}) async-start(), calls=%async_computation.11 | async-start | bytes 5242880 | tf_op jit(solution)/shard_map/reduce_scatter | solution.py:796
  556.1 189.9 %reduce-scatter.11.cloned.1.call-start = ((), (), s32[]{:S(2)}) async-start(), calls=%async_computation.12 | async-start | bytes 5242880 | tf_op jit(solution)/shard_map/reduce_scatter | solution.py:802
  657.9 41.2 %collective-permute-start.42 = (bf16[128,2048]{1,0:T(8,128)(2,1)}, bf16[128,2048]{1,0:T(8,128)(2,1)}, u32[]{:S(2)}, u32[]{:S(2)}) collective-permute-start(bf16[128,2048]{1,0:T(8,128)(2,1)} %get-tuple-element.159), channel_id=1, source_target_pairs={{0,2},{1,3},{2,0},{3,1},{16,18},{17,19},{18,16},{19,17},{4,6},{5,7... | collective-permute-start | bytes 1572872 | tf_op jit(solution)/shard_map/ppermute | solution.py:397
  659.4 39.7 %collective-permute-start.43 = (bf16[128,2048]{1,0:T(8,128)(2,1)}, bf16[128,2048]{1,0:T(8,128)(2,1)}, u32[]{:S(2)}, u32[]{:S(2)}) collective-permute-start(bf16[128,2048]{1,0:T(8,128)(2,1)} %get-tuple-element.161), channel_id=1, source_target_pairs={{0,16},{1,17},{2,18},{3,19},{16,0},{17,1},{18,2},{19,3},{4,20},{5,... | collective-permute-start | bytes 1572872 | tf_op jit(solution)/shard_map/ppermute | solution.py:397
  660.9 38.2 %collective-permute-start.44 = (bf16[128,2048]{1,0:T(8,128)(2,1)}, bf16[128,2048]{1,0:T(8,128)(2,1)}, u32[]{:S(2)}, u32[]{:S(2)}) collective-permute-start(bf16[128,2048]{1,0:T(8,128)(2,1)} %get-tuple-element.160), channel_id=1, source_target_pairs={{0,18},{1,19},{2,16},{3,17},{16,2},{17,3},{18,0},{19,1},{4,22},{5,... | collective-permute-start | bytes 1572872 | tf_op jit(solution)/shard_map/ppermute | solution.py:397
  662.2 31.4 %collective-permute-start.56 = (bf16[256,704]{0,1:T(8,128)(2,1)}, bf16[256,704]{0,1:T(8,128)(2,1)}, u32[]{:S(2)}, u32[]{:S(2)}) collective-permute-start(bf16[256,704]{0,1:T(8,128)(2,1)} %broadcast_select_fusion.18), channel_id=1, source_target_pairs={{0,16},{16,0},{1,17},{17,1},{2,18},{18,2},{3,19},{19,3},{4,20},{20... | collective-permute-start | bytes 1081352 | tf_op jit(solution)/shard_map/ppermute | solution.py:387
  664.6 42.2 %collective-permute-start.55 = (bf16[256,1408]{1,0:T(8,128)(2,1)}, bf16[256,1408]{1,0:T(8,128)(2,1)}, u32[]{:S(2)}, u32[]{:S(2)}) collective-permute-start(bf16[256,1408]{1,0:T(8,128)(2,1)} %broadcast_select_fusion), channel_id=1, source_target_pairs={{0,16},{16,0},{1,17},{17,1},{2,18},{18,2},{3,19},{19,3},{4,20},{20... | collective-permute-start | bytes 2162696 | tf_op jit(solution)/shard_map/ppermute | solution.py:387
  755.2 39.0 %collective-permute-start.52 = (f32[53536]{0:T(1024)S(1)}, f32[53536]{0:T(1024)}, u32[]{:S(2)}, u32[]{:S(2)}) collective-permute-start(f32[53536]{0:T(1024)S(1)} %fusion.151), channel_id=1, source_target_pairs={{0,4},{4,0},{8,12},{12,8},{1,5},{5,1},{9,13},{13,9},{2,6},{6,2},{1... | collective-permute-start | bytes 642440 | tf_op jit(solution)/shard_map/ppermute | solution.py:387
  756.7 37.5 %collective-permute-start.53 = (f32[53536]{0:T(1024)S(1)}, f32[53536]{0:T(1024)}, u32[]{:S(2)}, u32[]{:S(2)}) collective-permute-start(f32[53536]{0:T(1024)S(1)} %fusion.151), channel_id=1, source_target_pairs={{0,8},{4,12},{8,0},{12,4},{1,9},{5,13},{9,1},{13,5},{2,10},{6,14},... | collective-permute-start | bytes 642440 | tf_op jit(solution)/shard_map/ppermute | solution.py:387
  758.1 36.1 %collective-permute-start.54 = (f32[53536]{0:T(1024)S(1)}, f32[53536]{0:T(1024)}, u32[]{:S(2)}, u32[]{:S(2)}) collective-permute-start(f32[53536]{0:T(1024)S(1)} %fusion.151), channel_id=1, source_target_pairs={{0,12},{4,8},{8,4},{12,0},{1,13},{5,9},{9,5},{13,1},{2,14},{6,10},... | collective-permute-start | bytes 642440 | tf_op jit(solution)/shard_map/ppermute | solution.py:387
  (172 other events, 2166.0 us)
Sparse Core Ops, SparseCore 0:
  29.0 82.8 all-gather.4
  114.0 81.8 all-gather.6
  203.4 104.9 all-gather.8
  311.5 65.0 all-gather.10
  384.3 54.9 reduce-scatter.6
  441.9 114.0 reduce-scatter.4
  558.3 81.9 reduce-scatter.8
  642.8 77.2 reduce-scatter.10

commit v5 on v4

--- a/solution.py
+++ b/solution.py
@@ -809,7 +809,7 @@
     def exchanged(halves):
         own, theirs = halves
         received = swapped(theirs, "dp", 1)
-        return tuple(a.astype(F32) for a in by_device(own, received))
+        return by_device(own, received)
 
     mixer_parts = exchanged(halves_of(mixer_sum))
     started = []
@@ -834,7 +834,7 @@
     down_parts = exchanged(halves_of(after(down_sum, started)))
     g_output = jnp.concatenate(
         [m[:, heads * DV :].T.reshape(heads, DV, depth) for m in mixer_parts], axis=0
-    )
+    ).astype(F32)
     g_swiglu = jnp.stack(
         [
             jnp.concatenate([f[:, :units] for f in swiglu_parts], axis=1),
@@ -842,8 +842,8 @@
         ],
         axis=1,
     )
-    g_swiglu = with_layout_constraint(g_swiglu, Layout((0, 1, 2)))
-    g_down = jnp.concatenate([f.T for f in down_parts], axis=0)
+    g_swiglu = with_layout_constraint(g_swiglu.astype(F32), Layout((0, 1, 2)))
+    g_down = jnp.concatenate([f.T for f in down_parts], axis=0).astype(F32)
 
     conv_term = jnp.zeros_like(w_conv)
     grad_taps = jnp.sum(grad_taps.reshape(dp_size, heads, KCONV, QKV), axis=0)
@@ -896,7 +896,7 @@
             for q, m in zip(qkv_parts, mixer_parts)
         ],
         axis=1,
-    )
+    ).astype(F32)
     new_input, moment_input = adam_update(w_input, g_input, m_input, tokens)
     return (
         result,

time: 820 us -> 817 us (level)
  transfers between devices with their start and end apart: 66 -> 66, of which waited for: 33 -> 33; matrix products, arithmetic and copies ran while one was open for 39% -> 39% of each run, Pallas kernels for 8% -> 9%
where the time goes in v5:
time: 817 us; the launch traced here: 807 us
  waiting for transfers between devices  299 us (37%)
  other arithmetic  128 us (16%)
  matrix products  111 us (14%)
  local copies, waits for them, and re-layouts  108 us (13%)
  starting transfers between devices  74.6 us (9%)
  Pallas kernels  68.7 us (8%)
  between operations  17 us (2%)
    ppermute x25, waiting for transfers between devices, group_swapped(): return lax.ppermute(block, ('dp', 'tensor'), route)  108 us
    dot_general x18, matrix products, dot(): return lax.dot_general(left, right, dims, preferred_element_type=F32)  108 us
    ppermute x24, waiting for transfers between devices, swapped(): lax.ppermute(block, axis, [(i, i ^ bits) for i in range(lax.axis_size(axi...  74.2 us
    pallas_call x4, Pallas kernels, chains_call(): pl.pallas_call(kernel, grid=(chains,), in_specs=[spec(tag, a.shape) for t...  68.7 us
    all_gather x4, waiting for transfers between devices, body(): gathered.append(lax.all_gather(shard, 'seq', axis=0, tiled=True))  62 us
    unnamed x306, local copies, waits for them, and re-layouts  49.9 us
    ppermute x8, waiting for transfers between devices, shifted(): return lax.ppermute(block, axis, route)  44.7 us
    ppermute x25, starting transfers between devices, group_swapped(): return lax.ppermute(block, ('dp', 'tensor'), route)  28.6 us
  transfers between devices with their start and end apart: 66, of which 33 were waited for; matrix products, arithmetic and copies ran while one was open for 39% of the time, Pallas kernels for 9%

profile of v5, /device:TPU:0, one launch (start us, length us, event | category | flops | bytes accessed | tf_op | source)
XLA Modules:
  0.0 807.1 jit_solution(4001345385077544553)
XLA Ops:
  91.3 20.6 %all-gather.5.cloned.1.call-done = bf16[2048,1024]{1,0:T(8,128)(2,1)} async-done(((bf16[512,1024]{1,0:T(8,128)(2,1)}), bf16[2048,1024]{1,0:T(8,128)(2,1)}) %all-gather.5.cloned.1.call-update) | async-done | bytes 4194320 | tf_op jit(solution)/shard_map/all_gather | solution.py:595
  131.6 25.0 %shard_map.419 = (f32[4,512,128]{2,1,0:T(8,128)S(1)}, f32[4,512,256]{2,1,0:T(8,128)}, f32[4,128,384]{2,1,0:T(8,128)S(1)}, f32[4,4,128,384]{3,2,1,0:T(8,128)}, f3...) custom-call(f32[1024,1024]{1,0:T(8,128)} %copy-done.119, ...), custom_call_target="tpu_custom_call" | custom-call | flops 6039797760 | bytes 8814592 | tf_op jit(solution)/shard_map/pallas_call | solution.py:366
  165.6 17.1 %collective-permute-done.10 = bf16[128,2048]{1,0:T(8,128)(2,1)S(1)} collective-permute-done((bf16[128,2048]{1,0:T(8,128)(2,1)S(1)}, bf16[128,2048]{1,0:T(8,128)(2,1)S(1)}, u32[]{:S(2)}, u32[]{:S(2)}) %collective-permute-start.10) | collective-permute-done | bytes 524320 | tf_op jit(solution)/shard_map/ppermute | solution.py:397
  184.7 12.4 %collective-permute-done.22 = bf16[256,1408]{1,0:T(8,128)(2,1)S(1)} collective-permute-done((bf16[256,1408]{1,0:T(8,128)(2,1)S(1)}, bf16[256,1408]{1,0:T(8,128)(2,1)S(1)}, u32[]{:S(2)}, u32[]{:S(2)}) %collective-permute-start.22) | collective-permute-done | bytes 720928 | tf_op jit(solution)/shard_map/ppermute | solution.py:387
  247.7 11.3 %collective-permute-done.15 = bf16[128,2048]{1,0:T(8,128)(2,1)S(1)} collective-permute-done((bf16[128,2048]{1,0:T(8,128)(2,1)S(1)}, bf16[128,2048]{1,0:T(8,128)(2,1)S(1)}, u32[]{:S(2)}, u32[]{:S(2)}) %collective-permute-start.15) | collective-permute-done | bytes 524320 | tf_op jit(solution)/shard_map/ppermute | solution.py:397
  259.0 10.9 %collective-permute-done.16 = bf16[128,2048]{1,0:T(8,128)(2,1)S(1)} collective-permute-done((bf16[128,2048]{1,0:T(8,128)(2,1)S(1)}, bf16[128,2048]{1,0:T(8,128)(2,1)S(1)}, u32[]{:S(2)}, u32[]{:S(2)}) %collective-permute-start.16) | collective-permute-done | bytes 524320 | tf_op jit(solution)/shard_map/ppermute | solution.py:397
  275.7 11.3 %collective-permute-done.18 = bf16[128,2048]{1,0:T(8,128)(2,1)S(1)} collective-permute-done((bf16[128,2048]{1,0:T(8,128)(2,1)S(1)}, bf16[128,2048]{1,0:T(8,128)(2,1)S(1)}, u32[]{:S(2)}, u32[]{:S(2)}) %collective-permute-start.18) | collective-permute-done | bytes 524320 | tf_op jit(solution)/shard_map/ppermute | solution.py:397
  287.0 10.8 %collective-permute-done.19 = bf16[128,2048]{1,0:T(8,128)(2,1)S(1)} collective-permute-done((bf16[128,2048]{1,0:T(8,128)(2,1)S(1)}, bf16[128,2048]{1,0:T(8,128)(2,1)S(1)}, u32[]{:S(2)}, u32[]{:S(2)}) %collective-permute-start.19) | collective-permute-done | bytes 524320 | tf_op jit(solution)/shard_map/ppermute | solution.py:397
  299.9 10.5 %collective-permute-done.23 = bf16[256,704]{0,1:T(8,128)(2,1)S(1)} collective-permute-done((bf16[256,704]{0,1:T(8,128)(2,1)S(1)}, bf16[256,704]{0,1:T(8,128)(2,1)S(1)}, u32[]{:S(2)}, u32[]{:S(2)}) %collective-permute-start.23) | collective-permute-done | bytes 360480 | tf_op jit(solution)/shard_map/ppermute | solution.py:387
  319.8 10.6 %fusion.170 = f32[1024,1408]{1,0:T(8,128)S(1)} fusion(bf16[1024,2048]{1,0:T(8,128)(2,1)} %constant_dynamic-update-slice_fusion.13, bf16[2048,1408]{1,0:T(8,128)(2,1)} %all-gather.9.cloned.1.call-done), kind=kOutput, calls=%fused_computation.455 | convolution fusion | flops 5905580032 | bytes 15728640 | tf_op jit(solution)/shard_map/dot_general | solution.py:29
  335.3 41.4 %all-gather.11.cloned.1.call-done = bf16[2048,704]{0,1:T(8,128)(2,1)} async-done(((bf16[512,704]{0,1:T(8,128)(2,1)}), bf16[2048,704]{0,1:T(8,128)(2,1)}) %all-gather.11.cloned.1.call-update) | async-done | bytes 2883600 | tf_op jit(solution)/shard_map/all_gather | solution.py:595
  384.4 9.3 %multiply_convert_fusion.1 = (bf16[1024,704]{1,0:T(8,128)(2,1)S(1)}, bf16[1024,704]{1,0:T(8,128)(2,1)S(1)}) fusion(f32[1024,1408]{1,0:T(8,128)} %copy-done.36, bf16[1024,2048]{1,0:T(8,128)(2,1)} %constant_dynamic-update-slice_fusion.8, bf16[2048,704]{0,1:T(8,128)(2,1)} %all-gather.11.cloned.1.call-done), kind=kOutput, calls=%fused_computation.43 | convolution fusion | flops 2962161664 | bytes 15728640 | tf_op jit(solution)/shard_map/dot_general | solution.py:29
  414.5 8.8 %convolution_convert_fusion = bf16[2048,1408]{1,0:T(8,128)(2,1)} fusion(bf16[1024,2048]{1,0:T(8,128)(2,1)S(1)} %copy-done.89, bf16[1024,704]{1,0:T(8,128)(2,1)S(1)} %get-tuple-element.138, bf16[1024,704]{1,0:T(8,128)(2,1)S(1)} %get-tuple-element.137), kind=kOutput, calls=%fused_computation.1 | convolution fusion | flops 5914230784 | bytes 12845056 | tf_op jit(solution)/shard_map/dot_general | solution.py:29
  426.0 11.5 %collective-permute-done.26 = bf16[128,2048]{1,0:T(8,128)(2,1)} collective-permute-done((bf16[128,2048]{1,0:T(8,128)(2,1)}, bf16[128,2048]{1,0:T(8,128)(2,1)}, u32[]{:S(2)}, u32[]{:S(2)}) %collective-permute-start.26) | collective-permute-done | bytes 524320 | tf_op jit(solution)/shard_map/ppermute | solution.py:397
  445.4 11.4 %collective-permute-done.28 = bf16[128,2048]{1,0:T(8,128)(2,1)S(1)} collective-permute-done((bf16[128,2048]{1,0:T(8,128)(2,1)S(1)}, bf16[128,2048]{1,0:T(8,128)(2,1)S(1)}, u32[]{:S(2)}, u32[]{:S(2)}) %collective-permute-start.28) | collective-permute-done | bytes 524320 | tf_op jit(solution)/shard_map/ppermute | solution.py:397
  456.8 10.4 %collective-permute-done.29 = bf16[128,2048]{1,0:T(8,128)(2,1)S(1)} collective-permute-done((bf16[128,2048]{1,0:T(8,128)(2,1)S(1)}, bf16[128,2048]{1,0:T(8,128)(2,1)S(1)}, u32[]{:S(2)}, u32[]{:S(2)}) %collective-permute-start.29) | collective-permute-done | bytes 524320 | tf_op jit(solution)/shard_map/ppermute | solution.py:397
  487.6 22.1 %collective-permute-done.32 = bf16[4,128,256]{2,1,0:T(8,128)(2,1)S(1)} collective-permute-done((bf16[4,128,256]{2,1,0:T(8,128)(2,1)S(1)}, bf16[4,128,256]{2,1,0:T(8,128)(2,1)S(1)}, u32[]{:S(2)}, u32[]{:S(2)}) %collective-permute-start.32) | collective-permute-done | bytes 262176 | tf_op jit(solution)/shard_map/ppermute | solution.py:383
  536.9 10.0 %collective-permute-done.37 = bf16[4,128,256]{2,1,0:T(8,128)(2,1)S(1)} collective-permute-done((bf16[4,128,256]{2,1,0:T(8,128)(2,1)S(1)}, bf16[4,128,256]{2,1,0:T(8,128)(2,1)S(1)}, u32[]{:S(2)}, u32[]{:S(2)}) %collective-permute-start.37) | collective-permute-done | bytes 262176 | tf_op jit(solution)/shard_map/ppermute | solution.py:383
  566.9 33.1 %shard_map.422 = (bf16[1024,1024]{1,0:T(8,128)(2,1)}, f32[2,8,1024]{2,1,0:T(8,128)S(1)}, f32[2,8,1024]{2,1,0:T(8,128)S(1)}, f32[4,4,512]{2,1,0:T(4,128)S(1)}, f32[4,512,8]{2,1,0:T(8,128)S(1)}) custom-call(f32[1024,1024]{1,0:T(8,128)} %copy-done.119, f32[2,8,1024]{2,1,0:T(8,128)S(1)} %copy-done.12, f32[4,1024]{1,0:T(4,128)S(1)} %bitcast.446, ...), custom_call_target="tpu_custom_call" | custom-call | flops 8053063680 | bytes 33980416 | tf_op jit(solution)/shard_map/pallas_call | solution.py:366
  620.2 9.6 %add_convert_fusion = bf16[1024,2048]{1,0:T(8,128)(2,1)S(1)} fusion(f32[1024,2048]{1,0:T(8,128)} %fusion.97, f32[1024,2048]{1,0:T(8,128)} %fusion.16, bf16[1024,1024]{1,0:T(8,128)(2,1)S(1)} %bitcast.522, bf16[2048,1024]{1,0:T(8,128)(2,1)} %all-gather.5.cloned.1.call-done), kind=kOutput, calls=%fused_computation | convolution fusion | flops 4301258752 | bytes 27262976 | tf_op jit(solution)/shard_map/dot_general | solution.py:29
  676.9 16.4 %collective-permute-done.56 = bf16[256,704]{0,1:T(8,128)(2,1)} collective-permute-done((bf16[256,704]{0,1:T(8,128)(2,1)}, bf16[256,704]{0,1:T(8,128)(2,1)}, u32[]{:S(2)}, u32[]{:S(2)}) %collective-permute-start.56) | collective-permute-done | bytes 360480 | tf_op jit(solution)/shard_map/ppermute | solution.py:387
  715.2 9.7 %collective-permute-done.45 = bf16[128,4096]{1,0:T(8,128)(2,1)S(1)} collective-permute-done((bf16[128,4096]{1,0:T(8,128)(2,1)}, bf16[128,4096]{1,0:T(8,128)(2,1)S(1)}, u32[]{:S(2)}, u32[]{:S(2)}) %collective-permute-start.45) | collective-permute-done | bytes 1048608 | tf_op jit(solution)/shard_map/ppermute | solution.py:397
  725.1 11.2 %fusion.83 = (f32[256,2,1408]{2,1,0:T(2,128)S(1)}, f32[256,2,1408]{2,1,0:T(2,128)}) fusion(f32[256,2,1408]{2,1,0:T(2,128)S(1)} %get-tuple-element.116, f32[256,2,1408]{2,1,0:T(2,128)S(1)} %copy-done.30, f32[2,256,2,1408]{3,2,1,0:T(2,128)S(1)} %bitcast.452), kind=kLoop, calls=%fused_computation.306 | loop fusion | flops 11534336 | bytes 17301504 | tf_op jit(solution)/shard_map/mul | solution.py:501
  768.8 10.3 %convert_add_fusion.2 = (f32[512,2048]{1,0:T(8,128)}, f32[512,2048]{1,0:T(8,128)}) fusion(f32[512,2048]{1,0:T(8,128)} %param.21, bf16[512,4096]{1,0:T(8,128)(2,1)} %bitcast.453, f32[512,2048]{1,0:T(8,128)} %param.20), kind=kLoop, calls=%fused_computation.24 | loop fusion | flops 4194304 | bytes 20971520 | tf_op jit(solution)/shard_map/add | solution.py:831
  (669 shorter events, 434.5 us)
Async XLA Ops:
  7.2 104.7 %all-gather.5.cloned.1.call-start = ((), (), s32[]{:S(2)}) async-start(), calls=%async_computation.5 | async-start | bytes 5242880 | tf_op jit(solution)/shard_map/all_gather | solution.py:595
  29.8 32.2 %collective-permute-start = (bf16[128,2048]{1,0:T(8,128)(2,1)}, bf16[128,2048]{1,0:T(8,128)(2,1)}, u32[]{:S(2)}, u32[]{:S(2)}) collective-permute-start(bf16[128,2048]{1,0:T(8,128)(2,1)} %multiply_convert_fusion.4), channel_id=1, source_target_pairs={{0,2},{1,3},{2,0},{3,1},{16,18},{17,19},{18,16},{19,17},{4,6},{5,7... | collective-permute-start | bytes 1572872 | tf_op jit(solution)/shard_map/ppermute | solution.py:397
  31.5 32.4 %collective-permute-start.1 = (bf16[128,2048]{1,0:T(8,128)(2,1)}, bf16[128,2048]{1,0:T(8,128)(2,1)}, u32[]{:S(2)}, u32[]{:S(2)}) collective-permute-start(bf16[128,2048]{1,0:T(8,128)(2,1)} %multiply_convert_fusion.4), channel_id=1, source_target_pairs={{0,16},{1,17},{2,18},{3,19},{16,0},{17,1},{18,2},{19,3},{4,20},{5,... | collective-permute-start | bytes 1572872 | tf_op jit(solution)/shard_map/ppermute | solution.py:397
  33.1 32.8 %collective-permute-start.2 = (bf16[128,2048]{1,0:T(8,128)(2,1)}, bf16[128,2048]{1,0:T(8,128)(2,1)}, u32[]{:S(2)}, u32[]{:S(2)}) collective-permute-start(bf16[128,2048]{1,0:T(8,128)(2,1)} %multiply_convert_fusion.4), channel_id=1, source_target_pairs={{0,18},{1,19},{2,16},{3,17},{16,2},{17,3},{18,0},{19,1},{4,22},{5,... | collective-permute-start | bytes 1572872 | tf_op jit(solution)/shard_map/ppermute | solution.py:397
  35.9 44.7 %all-to-all-start = ((bf16[8,2,1024]{2,1,0:T(2,128)(2,1)}), bf16[8,2,1024]{2,1,0:T(2,128)(2,1)S(1)}, u32[]{:S(2)}, u32[]{:S(2)}) async-start(bf16[8,2,1024]{2,1,0:T(2,128)(2,1)} %reshape.645), calls=%async_computation | async-start | bytes 65536 | tf_op jit(solution)/shard_map/all_to_all | solution.py:601
  42.0 183.1 %all-gather.7.cloned.1.call-start = ((), (), s32[]{:S(2)}) async-start(), calls=%async_computation.6 | async-start | bytes 5242880 | tf_op jit(solution)/shard_map/all_gather | solution.py:595
  43.7 31.5 %collective-permute-start.13 = (bf16[256,1024]{1,0:T(8,128)(2,1)}, bf16[256,1024]{1,0:T(8,128)(2,1)}, u32[]{:S(2)}, u32[]{:S(2)}) collective-permute-start(bf16[256,1024]{1,0:T(8,128)(2,1)} %broadcast_select_fusion.20), channel_id=1, source_target_pairs={{0,16},{16,0},{1,17},{17,1},{2,18},{18,2},{3,19},{19,3},{4,20},{20... | collective-permute-start | bytes 1572872 | tf_op jit(solution)/shard_map/ppermute | solution.py:387
  77.7 242.1 %all-gather.9.cloned.1.call-start = ((), (), s32[]{:S(2)}) async-start(), calls=%async_computation.7 | async-start | bytes 7208960 | tf_op jit(solution)/shard_map/all_gather | solution.py:595
  160.7 36.4 %collective-permute-start.22 = (bf16[256,1408]{1,0:T(8,128)(2,1)S(1)}, bf16[256,1408]{1,0:T(8,128)(2,1)S(1)}, u32[]{:S(2)}, u32[]{:S(2)}) collective-permute-start(bf16[256,1408]{1,0:T(8,128)(2,1)S(1)} %broadcast_select_fusion.6), channel_id=1, source_target_pairs={{0,16},{16,0},{1,17},{17,1},{2,18},{18,2},{3,19},{19,3},{4,20},{20... | collective-permute-start | bytes 2162696 | tf_op jit(solution)/shard_map/ppermute | solution.py:387
  162.3 35.5 %collective-permute-start.6 = (bf16[4,128,256]{2,1,0:T(8,128)(2,1)S(1)}, bf16[4,128,256]{2,1,0:T(8,128)(2,1)S(1)}, u32[]{:S(2)}, u32[]{:S(2)}) collective-permute-start(bf16[4,128,256]{2,1,0:T(8,128)(2,1)S(1)} %slice.927), channel_id=1, source_target_pairs={{0,4},{4,8},{8,12},{1,5},{5,9},{9,13},{2,6},{6,10},{10,14},{3,7},{... | collective-permute-start | bytes 786440 | tf_op jit(solution)/shard_map/ppermute | solution.py:383
  184.6 37.3 %collective-permute-start.12 = (bf16[512,2048]{1,0:T(8,128)(2,1)}, bf16[512,2048]{1,0:T(8,128)(2,1)}, u32[]{:S(2)}, u32[]{:S(2)}) collective-permute-start(bf16[512,2048]{1,0:T(8,128)(2,1)} %pad_maximum_fusion.5), channel_id=1, source_target_pairs={{0,1},{1,0},{2,3},{3,2},{4,5},{5,4},{6,7},{7,6},{8,9},{9,8},{10,11... | collective-permute-start | bytes 6291464 | tf_op jit(solution)/shard_map/ppermute | solution.py:387
  203.2 173.4 %all-gather.11.cloned.1.call-start = ((), (), s32[]{:S(2)}) async-start(), calls=%async_computation.8 | async-start | bytes 3604480 | tf_op jit(solution)/shard_map/all_gather | solution.py:595
  311.4 238.0 %reduce-scatter.7.cloned.1.call-start = ((), (), s32[]{:S(2)}) async-start(), calls=%async_computation.10 | async-start | bytes 3604480 | tf_op jit(solution)/shard_map/reduce_scatter | solution.py:695
  384.1 171.9 %reduce-scatter.5.cloned.1.call-start = ((), (), s32[]{:S(2)}) async-start(), calls=%async_computation.9 | async-start | bytes 7208960 | tf_op jit(solution)/shard_map/reduce_scatter | solution.py:704
  423.3 217.0 %reduce-scatter.9.cloned.1.call-start = ((), (), s32[]{:S(2)}) async-start(), calls=%async_computation.11 | async-start | bytes 5242880 | tf_op jit(solution)/shard_map/reduce_scatter | solution.py:796
  556.1 190.9 %reduce-scatter.11.cloned.1.call-start = ((), (), s32[]{:S(2)}) async-start(), calls=%async_computation.12 | async-start | bytes 5242880 | tf_op jit(solution)/shard_map/reduce_scatter | solution.py:802
  657.7 41.2 %collective-permute-start.42 = (bf16[128,2048]{1,0:T(8,128)(2,1)}, bf16[128,2048]{1,0:T(8,128)(2,1)}, u32[]{:S(2)}, u32[]{:S(2)}) collective-permute-start(bf16[128,2048]{1,0:T(8,128)(2,1)} %get-tuple-element.159), channel_id=1, source_target_pairs={{0,2},{1,3},{2,0},{3,1},{16,18},{17,19},{18,16},{19,17},{4,6},{5,7... | collective-permute-start | bytes 1572872 | tf_op jit(solution)/shard_map/ppermute | solution.py:397
  659.2 39.7 %collective-permute-start.43 = (bf16[128,2048]{1,0:T(8,128)(2,1)}, bf16[128,2048]{1,0:T(8,128)(2,1)}, u32[]{:S(2)}, u32[]{:S(2)}) collective-permute-start(bf16[128,2048]{1,0:T(8,128)(2,1)} %get-tuple-element.161), channel_id=1, source_target_pairs={{0,16},{1,17},{2,18},{3,19},{16,0},{17,1},{18,2},{19,3},{4,20},{5,... | collective-permute-start | bytes 1572872 | tf_op jit(solution)/shard_map/ppermute | solution.py:397
  660.7 38.2 %collective-permute-start.44 = (bf16[128,2048]{1,0:T(8,128)(2,1)}, bf16[128,2048]{1,0:T(8,128)(2,1)}, u32[]{:S(2)}, u32[]{:S(2)}) collective-permute-start(bf16[128,2048]{1,0:T(8,128)(2,1)} %get-tuple-element.160), channel_id=1, source_target_pairs={{0,18},{1,19},{2,16},{3,17},{16,2},{17,3},{18,0},{19,1},{4,22},{5,... | collective-permute-start | bytes 1572872 | tf_op jit(solution)/shard_map/ppermute | solution.py:397
  662.0 31.4 %collective-permute-start.56 = (bf16[256,704]{0,1:T(8,128)(2,1)}, bf16[256,704]{0,1:T(8,128)(2,1)}, u32[]{:S(2)}, u32[]{:S(2)}) collective-permute-start(bf16[256,704]{0,1:T(8,128)(2,1)} %broadcast_select_fusion.24), channel_id=1, source_target_pairs={{0,16},{16,0},{1,17},{17,1},{2,18},{18,2},{3,19},{19,3},{4,20},{20... | collective-permute-start | bytes 1081352 | tf_op jit(solution)/shard_map/ppermute | solution.py:387
  664.4 42.2 %collective-permute-start.55 = (bf16[256,1408]{1,0:T(8,128)(2,1)}, bf16[256,1408]{1,0:T(8,128)(2,1)}, u32[]{:S(2)}, u32[]{:S(2)}) collective-permute-start(bf16[256,1408]{1,0:T(8,128)(2,1)} %broadcast_select_fusion.2), channel_id=1, source_target_pairs={{0,16},{16,0},{1,17},{17,1},{2,18},{18,2},{3,19},{19,3},{4,20},{20... | collective-permute-start | bytes 2162696 | tf_op jit(solution)/shard_map/ppermute | solution.py:387
  756.2 35.1 %collective-permute-start.52 = (f32[53536]{0:T(1024)S(1)}, f32[53536]{0:T(1024)}, u32[]{:S(2)}, u32[]{:S(2)}) collective-permute-start(f32[53536]{0:T(1024)S(1)} %fusion.151), channel_id=1, source_target_pairs={{0,4},{4,0},{8,12},{12,8},{1,5},{5,1},{9,13},{13,9},{2,6},{6,2},{1... | collective-permute-start | bytes 642440 | tf_op jit(solution)/shard_map/ppermute | solution.py:387
  757.6 33.7 %collective-permute-start.53 = (f32[53536]{0:T(1024)S(1)}, f32[53536]{0:T(1024)}, u32[]{:S(2)}, u32[]{:S(2)}) collective-permute-start(f32[53536]{0:T(1024)S(1)} %fusion.151), channel_id=1, source_target_pairs={{0,8},{4,12},{8,0},{12,4},{1,9},{5,13},{9,1},{13,5},{2,10},{6,14},... | collective-permute-start | bytes 642440 | tf_op jit(solution)/shard_map/ppermute | solution.py:387
  759.0 32.3 %collective-permute-start.54 = (f32[53536]{0:T(1024)S(1)}, f32[53536]{0:T(1024)}, u32[]{:S(2)}, u32[]{:S(2)}) collective-permute-start(f32[53536]{0:T(1024)S(1)} %fusion.151), channel_id=1, source_target_pairs={{0,12},{4,8},{8,4},{12,0},{1,13},{5,9},{9,5},{13,1},{2,14},{6,10},... | collective-permute-start | bytes 642440 | tf_op jit(solution)/shard_map/ppermute | solution.py:387
  (172 other events, 2171.8 us)
Sparse Core Ops, SparseCore 0:
  29.0 82.8 all-gather.4
  114.0 81.8 all-gather.6
  203.4 104.9 all-gather.8
  311.5 65.0 all-gather.10
  384.3 54.9 reduce-scatter.6
  441.9 114.0 reduce-scatter.4
  558.3 81.9 reduce-scatter.8
  642.8 77.2 reduce-scatter.10
